TPU v7x, 32 devices: a whole 2x2x4 slice. The times are simulated.
32 devices in a mesh: dp: 16 (over z, y, core), mp: 2 (over x).
Axes of the slice: x: 2, y: 2, z: 4, core: 2. Of those that a mesh axis runs over, the one named last changes fastest.
Arguments:
- hidden_in: bfloat16 [4096, 2048], P(('dp', 'mp')), may hold values from -6 to 6
- cotangent: bfloat16 [4096, 2048], P(('dp', 'mp')), may hold values from -6 to 6
- norm_gains: float32 [2, 2048], replicated, may hold values from 0.5 to 1.5
- qkv_weight: bfloat16 [3, 2048, 2048], P(None, 'dp', 'mp'), may hold values from -0.125 to 0.125
- qkv_bias: bfloat16 [3, 2048], replicated, may hold values from -3 to 3
- out_weight: bfloat16 [2048, 2048], P('mp', 'dp'), may hold values from -2 to 2
- router_weight: bfloat16 [2048, 16], replicated, may hold values from -0.0625 to 0.0625
- shared_gate_vec: bfloat16 [2048], replicated, may hold values from -0.125 to 0.125
- shared_gate_up: bfloat16 [2, 2048, 5632], P(None, 'dp', 'mp'), may hold values from -0.125 to 0.125
- shared_down: bfloat16 [5632, 2048], P('mp', 'dp'), may hold values from -0.109375 to 0.109375
- expert_gate_up: bfloat16 [16, 2, 2048, 1408], P('dp', None, None, 'mp'), may hold values from -0.125 to 0.125
- expert_down: bfloat16 [16, 1408, 2048], P('dp', 'mp'), may hold values from -6 to 6
- segments: int32 [4096], P('dp'), may hold values from 0 to 4095, as said below
- valid_mask: int32 [4096], P('dp'), may hold values 0 or 1
- routes: int32 [4096, 4], P('dp'), may hold values from 0 to 15, as said below
- slots: int32 [4096, 4], P('dp'), may hold values from 0 to 84, as said below
Outputs:
- output: bfloat16 [4096, 2048], P(('dp', 'mp'))
- input_grad: float32 [4096, 2048], P(('dp', 'mp'))
- grad_norm_gains: float32 [2, 2048], replicated
- grad_qkv_weight: float32 [3, 2048, 2048], P(None, 'dp', 'mp')
- grad_qkv_bias: float32 [3, 2048], replicated
- grad_out_weight: float32 [2048, 2048], P('mp', 'dp')
- grad_router_weight: float32 [2048, 16], replicated
- grad_shared_gate_vec: float32 [2048], replicated
- grad_shared_gate_up: float32 [2, 2048, 5632], P(None, 'dp', 'mp')
- grad_shared_down: float32 [5632, 2048], P('mp', 'dp')
- grad_expert_gate_up: float32 [16, 2, 2048, 1408], P('dp', None, None, 'mp')
- grad_expert_down: float32 [16, 1408, 2048], P('dp', 'mp')
- rms_residual: float32 [], replicated
- rms_attention: float32 [], replicated
- rms_moe: float32 [], replicated
Inputs may be any that keep to these rules, and one draw needn't show every extreme that they name: `segments`: each document's number is the position of its first token. Numbers never fall, a new document begins at every multiple of 4096 positions, and the last token begins a document of its own. `routes`: each row names 4 different experts. Among the 256 rows of one index of dp (aligned blocks), no expert is named more than 85 times, and one expert is named exactly 85 times in every block. Within one block of 256 rows, the routes to one expert carry different slots.
All inputs are finite; a program needn't handle non-finite values. No bound on the sum of `valid_mask` on one device may be relied on, other than what follows from the above.
Results may differ from a plain program's by a relative error of at most 0.018.
Values may be sent and summed in bfloat16 or wider, within the bound.
No kernel may reach another device: no remote copies, remote signals or barrier semaphores. Data moves between devices by JAX's collectives and lax.ppermute only.
A program may use at most 448 MiB of HBM per device.

v0:
```python
import jax
import jax.numpy as jnp
from jax import lax
from jax.sharding import PartitionSpec as P

HEAD = 128
TOP = 4
SEQ = 4096
WINDOW = 1024


EPSILON = 1e-06
ROPE_BASE = 1000000.0
MASKED = -1e30


def from_behind(block, axis, distance):
    devices = range(lax.axis_size(axis))
    route = [(i - distance, i) for i in devices if i - distance in devices]
    return lax.ppermute(block, axis, route)


def swish(gate_in):
    return gate_in * jax.nn.sigmoid(gate_in)


def swish_back(gate_in, up_in, grad):
    sigma = jax.nn.sigmoid(gate_in)
    grad_gate = grad * up_in * sigma * (1.0 + gate_in * (1.0 - sigma))
    grad_up = grad * gate_in * sigma
    return (grad_gate, grad_up)


def rope_tables(first_row, row_count, head_size):
    placing = (first_row + jnp.arange(row_count, dtype=jnp.int32)) % SEQ
    frequency = ROPE_BASE ** (-(jnp.arange(head_size // 2, dtype=jnp.float32) * 2.0 / head_size))
    angles = placing.astype(jnp.float32)[:, None] * frequency[None, :]
    return (jnp.cos(angles), jnp.sin(angles))


def rotate(vector, cos_table, sin_table):
    half_size = vector.shape[-1] // 2
    first_half = vector[..., :half_size]
    second_half = vector[..., half_size:]
    cosine = cos_table[:, None, :]
    sine_part = sin_table[:, None, :]
    return jnp.concatenate(
        [
            first_half * cosine - second_half * sine_part,
            second_half * cosine + first_half * sine_part,
        ],
        axis=-1,
    )


def unrotate(vector, cos_table, sin_table):
    half_size = vector.shape[-1] // 2
    first_half = vector[..., :half_size]
    second_half = vector[..., half_size:]
    cosine = cos_table[:, None, :]
    sine_part = sin_table[:, None, :]
    return jnp.concatenate(
        [
            first_half * cosine + second_half * sine_part,
            second_half * cosine - first_half * sine_part,
        ],
        axis=-1,
    )


def norm_scale(rows_in):
    return lax.rsqrt(jnp.mean(rows_in * rows_in, axis=-1, keepdims=True) + EPSILON)


def norm_back(rows_in, scaling, gain, grad):
    unit_rows = rows_in * scaling
    grad_unit = grad * gain
    grad_rows = scaling * (
        grad_unit - unit_rows * jnp.mean(grad_unit * unit_rows, axis=-1, keepdims=True)
    )
    return (grad_rows, jnp.sum(grad * unit_rows, axis=0))


def window_mask(query_ids, key_ids, query_segs, key_segs, key_valid):
    distance = query_ids[:, None] - key_ids[None, :]
    return (
        (distance >= 0)
        & (distance < WINDOW)
        & (key_ids[None, :] >= 0)
        & (query_segs[:, None] == key_segs[None, :])
        & ((key_valid[None, :] == 1) | (distance == 0))
    )


def score_block(queries, key_rows, allowed, score_scale):
    scores = (
        jnp.einsum("qhd,khd->hqk", queries, key_rows, preferred_element_type=jnp.float32)
        * score_scale
    )
    return jnp.where(allowed[None], scores, MASKED)


def collect(rows_in):
    return lax.all_gather(rows_in, "mp", axis=0, tiled=True)


def spread(partial_value):
    return lax.psum_scatter(partial_value, "mp", scatter_dimension=0, tiled=True)


def collect_grad(rows_in):
    return lax.all_gather(rows_in, "mp", axis=0, tiled=True)


def spread_grad(partial_value):
    return lax.psum_scatter(partial_value, "mp", scatter_dimension=0, tiled=True)


def to_experts(arriving, dp_size, expert_here, capacity):
    model_width = arriving.shape[-1]
    return (
        arriving.reshape(dp_size, expert_here, capacity, model_width)
        .transpose(1, 0, 2, 3)
        .reshape(expert_here, dp_size * capacity, model_width)
    )


def to_sources(leaving, dp_size, expert_here, capacity):
    model_width = leaving.shape[-1]
    return (
        leaving.reshape(expert_here, dp_size, capacity, model_width)
        .transpose(1, 0, 2, 3)
        .reshape(dp_size, expert_here * capacity, model_width)
    )


def per_device(
    hidden_in,
    cotangent,
    norm_gains,
    qkv_weight,
    qkv_bias,
    out_weight,
    router_weight,
    shared_gate_vec,
    shared_gate_up,
    shared_down,
    expert_gate_up,
    expert_down,
    segments,
    valid_mask,
    routes,
    slots,
):
    dp_size = lax.axis_size("dp")
    dp_rank = lax.axis_index("dp")
    mp_rank = lax.axis_index("mp")
    blocks = segments.shape[0]
    rows_here = hidden_in.shape[0]
    model_width = hidden_in.shape[1]
    local_cols = qkv_weight.shape[2]
    shared_cols = shared_gate_up.shape[2]
    head_count = local_cols // HEAD
    expert_count = router_weight.shape[1]
    capacity = blocks * TOP * 4 // (3 * expert_count)
    expert_here = expert_down.shape[0]
    reach_blocks = (WINDOW + blocks - 2) // blocks
    score_scale = HEAD ** (-0.5)
    head_shape = (blocks, head_count, HEAD)
    w_qkv, w_out, w_sgu, w_sdown = (
        lax.all_gather(qkv_weight, "dp", axis=1, tiled=True),
        lax.all_gather(out_weight, "dp", axis=1, tiled=True),
        lax.all_gather(shared_gate_up, "dp", axis=1, tiled=True),
        lax.all_gather(shared_down, "dp", axis=1, tiled=True),
    )
    residual = hidden_in.astype(jnp.float32)
    gain_attn = norm_gains[0]
    gain_moe = norm_gains[1]
    scale_attn = norm_scale(residual)
    normed_attn = collect((residual * scale_attn * gain_attn).astype(jnp.bfloat16))
    bias_here = lax.dynamic_slice_in_dim(qkv_bias, mp_rank * local_cols, local_cols, 1).astype(
        jnp.float32
    )
    projected = (
        jnp.einsum("td,jdc->jtc", normed_attn, w_qkv, preferred_element_type=jnp.float32)
        + bias_here[:, None, :]
    )
    cos_table, sin_table = rope_tables(dp_rank * blocks, blocks, HEAD)
    queries = rotate(projected[0].reshape(head_shape), cos_table, sin_table).astype(jnp.bfloat16)
    key_own = rotate(projected[1].reshape(head_shape), cos_table, sin_table).astype(jnp.bfloat16)
    value_own = projected[2].reshape(head_shape).astype(jnp.bfloat16)
    token_ids = dp_rank * blocks + jnp.arange(blocks, dtype=jnp.int32)
    key_parts, value_parts, seg_parts, valid_parts, index_parts = ([], [], [], [], [])
    for steps_back in range(reach_blocks, 0, -1):
        moved = from_behind((key_own, value_own, segments, valid_mask), "dp", steps_back)
        key_parts.append(moved[0])
        value_parts.append(moved[1])
        seg_parts.append(moved[2])
        valid_parts.append(moved[3])
        index_parts.append(token_ids - steps_back * blocks)
    key_parts.append(key_own)
    value_parts.append(value_own)
    seg_parts.append(segments)
    valid_parts.append(valid_mask)
    index_parts.append(token_ids)
    key_rows = jnp.concatenate(key_parts, 0)
    values = jnp.concatenate(value_parts, 0)
    allowed = window_mask(
        token_ids,
        jnp.concatenate(index_parts, 0),
        segments,
        jnp.concatenate(seg_parts, 0),
        jnp.concatenate(valid_parts, 0),
    )
    scores = score_block(queries, key_rows, allowed, score_scale)
    highest = jnp.max(scores, axis=-1, keepdims=True)
    powers = jnp.exp(scores - highest)
    totals = jnp.sum(powers, axis=-1, keepdims=True)
    log_total = highest + jnp.log(totals)
    weights = powers / totals
    attended = jnp.einsum(
        "hqk,khd->qhd", weights.astype(jnp.bfloat16), values, preferred_element_type=jnp.float32
    )
    attn_flat = attended.reshape(blocks, local_cols).astype(jnp.bfloat16)
    attn_rows = spread(jnp.dot(attn_flat, w_out, preferred_element_type=jnp.float32))
    middle = residual + attn_rows
    scale_moe = norm_scale(middle)
    normed_moe = collect((middle * scale_moe * gain_moe).astype(jnp.bfloat16))
    logits = jnp.dot(normed_moe, router_weight, preferred_element_type=jnp.float32)
    router_top = jnp.max(logits, axis=-1, keepdims=True)
    router_pow = jnp.exp(logits - router_top)
    router_probs = router_pow / jnp.sum(router_pow, axis=-1, keepdims=True)
    one_hot = (
        routes[:, :, None] == jnp.arange(expert_count, dtype=jnp.int32)[None, None, :]
    ).astype(jnp.float32)
    gate_probs = jnp.einsum("tke,te->tk", one_hot, router_probs)
    slot_index = (routes * capacity + slots).reshape(-1)
    copies = jnp.broadcast_to(normed_moe[:, None, :], (blocks, TOP, model_width)).reshape(
        blocks * TOP, model_width
    )
    outbound = (
        jnp.zeros((expert_count * capacity, model_width), jnp.bfloat16).at[slot_index].set(copies)
    )
    inbound = lax.all_to_all(
        outbound.reshape(dp_size, expert_here * capacity, model_width),
        "dp",
        split_axis=0,
        concat_axis=0,
        tiled=True,
    )
    expert_rows = to_experts(inbound, dp_size, expert_here, capacity)
    gate_up = jnp.einsum(
        "erd,ejdf->ejrf", expert_rows, expert_gate_up, preferred_element_type=jnp.float32
    )
    expert_hidden = (swish(gate_up[:, 0]) * gate_up[:, 1]).astype(jnp.bfloat16)
    expert_out = jnp.einsum(
        "erf,efd->erd", expert_hidden, expert_down, preferred_element_type=jnp.float32
    ).astype(jnp.bfloat16)
    returning = lax.all_to_all(
        to_sources(expert_out, dp_size, expert_here, capacity),
        "dp",
        split_axis=0,
        concat_axis=0,
        tiled=True,
    )
    picked = (
        returning.reshape(expert_count * capacity, model_width)[slot_index]
        .reshape(blocks, TOP, model_width)
        .astype(jnp.float32)
    )
    shared_in = jnp.einsum("td,jdf->jtf", normed_moe, w_sgu, preferred_element_type=jnp.float32)
    shared_hidden = (swish(shared_in[0]) * shared_in[1]).astype(jnp.bfloat16)
    shared_out = jnp.dot(shared_hidden, w_sdown, preferred_element_type=jnp.float32)
    shared_gate = jax.nn.sigmoid(
        jnp.dot(normed_moe, shared_gate_vec, preferred_element_type=jnp.float32)
    )
    mixed_part = jnp.einsum("tk,tkd->td", gate_probs, picked) + shared_gate[:, None] * shared_out
    moe_rows = spread(mixed_part)
    output = (middle + moe_rows).astype(jnp.bfloat16)
    grad_out = cotangent.astype(jnp.float32)
    grad_moe = collect_grad(cotangent).astype(jnp.float32)
    grad_shared = (shared_gate[:, None] * grad_moe).astype(jnp.bfloat16)
    grad_shared_hidden = jnp.einsum(
        "td,fd->tf", grad_shared, w_sdown, preferred_element_type=jnp.float32
    )
    gate_signal = jnp.sum(grad_moe * shared_out, axis=-1) * shared_gate * (1.0 - shared_gate)
    shared_gate_grad, shared_up_grad = swish_back(shared_in[0], shared_in[1], grad_shared_hidden)
    grad_shared_in = jnp.stack([shared_gate_grad, shared_up_grad]).astype(jnp.bfloat16)
    normed_float = normed_moe.astype(jnp.float32)
    grad_gate_vec = jnp.dot(gate_signal, normed_float)
    grad_normed = jnp.einsum(
        "jtf,jdf->td", grad_shared_in, w_sgu, preferred_element_type=jnp.float32
    )
    grad_normed = grad_normed + gate_signal[:, None] * shared_gate_vec.astype(jnp.float32)[None, :]
    grad_picked = (gate_probs[:, :, None] * grad_moe[:, None, :]).astype(jnp.bfloat16)
    grad_gates = jnp.einsum("tkd,td->tk", picked, grad_moe)
    outbound_grad = (
        jnp.zeros((expert_count * capacity, model_width), jnp.bfloat16)
        .at[slot_index]
        .set(grad_picked.reshape(blocks * TOP, model_width))
    )
    inbound_grad = lax.all_to_all(
        outbound_grad.reshape(dp_size, expert_here * capacity, model_width),
        "dp",
        split_axis=0,
        concat_axis=0,
        tiled=True,
    )
    grad_expert_out = to_experts(inbound_grad, dp_size, expert_here, capacity)
    grad_expert_hidden = jnp.einsum(
        "erd,efd->erf", grad_expert_out, expert_down, preferred_element_type=jnp.float32
    )
    grad_edown = jnp.einsum(
        "erf,erd->efd", expert_hidden, grad_expert_out, preferred_element_type=jnp.float32
    )
    expert_gate_grad, expert_up_grad = swish_back(gate_up[:, 0], gate_up[:, 1], grad_expert_hidden)
    grad_gate_up = jnp.stack([expert_gate_grad, expert_up_grad], axis=1).astype(jnp.bfloat16)
    grad_egu = jnp.einsum(
        "erd,ejrf->ejdf", expert_rows, grad_gate_up, preferred_element_type=jnp.float32
    )
    grad_expert_rows = jnp.einsum(
        "ejrf,ejdf->erd", grad_gate_up, expert_gate_up, preferred_element_type=jnp.float32
    )
    grad_returned = lax.all_to_all(
        to_sources(grad_expert_rows, dp_size, expert_here, capacity).astype(jnp.bfloat16),
        "dp",
        split_axis=0,
        concat_axis=0,
        tiled=True,
    ).astype(jnp.float32)
    grad_copies = grad_returned.reshape(expert_count * capacity, model_width)[slot_index].reshape(
        blocks, TOP, model_width
    )
    grad_normed = grad_normed + jnp.sum(grad_copies, axis=1)
    grad_router_probs = jnp.einsum("tk,tke->te", grad_gates, one_hot)
    grad_logits = router_probs * (
        grad_router_probs - jnp.sum(router_probs * grad_router_probs, axis=-1, keepdims=True)
    )
    grad_router = jnp.einsum("td,te->de", normed_float, grad_logits)
    grad_normed = grad_normed + jnp.einsum(
        "te,de->td", grad_logits, router_weight.astype(jnp.float32)
    )
    grad_middle_norm, grad_gain_moe = norm_back(
        middle, scale_moe, gain_moe, spread_grad(grad_normed)
    )
    grad_middle = grad_out + grad_middle_norm
    grad_attn = collect_grad(grad_middle.astype(jnp.bfloat16))
    grad_attended = (
        jnp.einsum("td,cd->tc", grad_attn, w_out, preferred_element_type=jnp.float32)
        .astype(jnp.bfloat16)
        .reshape(head_shape)
    )
    scores_again = score_block(queries, key_rows, allowed, score_scale)
    probs_again = jnp.where(allowed[None], jnp.exp(scores_again - log_total), 0.0)
    grad_weights = jnp.einsum(
        "qhd,khd->hqk", grad_attended, values, preferred_element_type=jnp.float32
    )
    inner = jnp.sum(probs_again * grad_weights, axis=-1, keepdims=True)
    grad_scores = (probs_again * (grad_weights - inner)).astype(jnp.bfloat16)
    grad_queries = (
        jnp.einsum("hqk,khd->qhd", grad_scores, key_rows, preferred_element_type=jnp.float32)
        * score_scale
    )
    grad_keys = (
        jnp.einsum("hqk,qhd->khd", grad_scores, queries, preferred_element_type=jnp.float32)
        * score_scale
    )
    grad_values = jnp.einsum(
        "hqk,qhd->khd",
        probs_again.astype(jnp.bfloat16),
        grad_attended,
        preferred_element_type=jnp.float32,
    )
    grad_key_own = grad_keys[reach_blocks * blocks :]
    grad_value_own = grad_values[reach_blocks * blocks :]
    for steps_back in range(reach_blocks, 0, -1):
        first_row = (reach_blocks - steps_back) * blocks
        arrived = (
            from_behind(
                grad_keys[first_row : first_row + blocks].astype(jnp.bfloat16), "dp", -steps_back
            ).astype(jnp.float32),
            from_behind(
                grad_values[first_row : first_row + blocks].astype(jnp.bfloat16), "dp", -steps_back
            ).astype(jnp.float32),
        )
        grad_key_own = grad_key_own + arrived[0]
        grad_value_own = grad_value_own + arrived[1]
    grad_projected = jnp.stack(
        [
            unrotate(grad_queries, cos_table, sin_table).reshape(blocks, local_cols),
            unrotate(grad_key_own, cos_table, sin_table).reshape(blocks, local_cols),
            grad_value_own.reshape(blocks, local_cols),
        ]
    ).astype(jnp.bfloat16)
    grad_bias_here = jnp.sum(grad_projected.astype(jnp.float32), axis=1)
    grad_bias = lax.dynamic_update_slice_in_dim(
        jnp.zeros((3, model_width), jnp.float32), grad_bias_here, mp_rank * local_cols, 1
    )
    grad_normed_attn = jnp.einsum(
        "jtc,jdc->td", grad_projected, w_qkv, preferred_element_type=jnp.float32
    )
    grad_residual_norm, grad_gain_attn = norm_back(
        residual, scale_attn, gain_attn, spread_grad(grad_normed_attn)
    )
    input_grad = grad_middle + grad_residual_norm
    term_qkv = jnp.einsum(
        "td,jtc->djc", normed_attn, grad_projected, preferred_element_type=jnp.float32
    ).reshape(model_width, 3 * local_cols)
    term_out = jnp.einsum("tc,td->dc", attn_flat, grad_attn, preferred_element_type=jnp.float32)
    term_sgu = jnp.einsum(
        "td,jtf->djf", normed_moe, grad_shared_in, preferred_element_type=jnp.float32
    ).reshape(model_width, 2 * shared_cols)
    term_sdown = jnp.einsum(
        "tf,td->df", shared_hidden, grad_shared, preferred_element_type=jnp.float32
    )
    dense_total = lax.psum_scatter(
        jnp.concatenate([term_qkv, term_out, term_sgu, term_sdown], 1),
        "dp",
        scatter_dimension=0,
        tiled=True,
    )
    rows_owned = dense_total.shape[0]
    grad_qkv_total = (
        dense_total[:, : 3 * local_cols].reshape(rows_owned, 3, local_cols).transpose(1, 0, 2)
    )
    grad_out_total = dense_total[:, 3 * local_cols : 4 * local_cols].T
    grad_sgu_total = (
        dense_total[:, 4 * local_cols : 4 * local_cols + 2 * shared_cols]
        .reshape(rows_owned, 2, shared_cols)
        .transpose(1, 0, 2)
    )
    grad_sdown_total = dense_total[:, 4 * local_cols + 2 * shared_cols :].T
    valid_rows = lax.dynamic_slice_in_dim(valid_mask, mp_rank * rows_here, rows_here, 0).astype(
        jnp.float32
    )[:, None]
    sums_here = jnp.stack(
        [
            jnp.sum(valid_rows * residual * residual),
            jnp.sum(valid_rows * attn_rows * attn_rows),
            jnp.sum(valid_rows * moe_rows * moe_rows),
            jnp.sum(valid_rows),
        ]
    )
    gain_total, bias_total, router_total, gate_vec_total, sums_total = lax.psum(
        (
            jnp.stack([grad_gain_attn, grad_gain_moe]),
            grad_bias,
            grad_router,
            grad_gate_vec,
            sums_here,
        ),
        ("dp", "mp"),
    )
    valid_count = jnp.maximum(sums_total[3], 1.0)
    root_means = jnp.sqrt(sums_total[:3] / (valid_count * model_width))
    return (
        output,
        input_grad,
        gain_total,
        grad_qkv_total,
        bias_total,
        grad_out_total,
        router_total,
        gate_vec_total,
        grad_sgu_total,
        grad_sdown_total,
        grad_egu,
        grad_edown,
        root_means[0],
        root_means[1],
        root_means[2],
    )


def solution(mesh):
    placed = (
        P(("dp", "mp"), None),
        P(("dp", "mp"), None),
        P(),
        P(None, "dp", "mp"),
        P(),
        P("mp", "dp"),
        P(),
        P(),
        P(None, "dp", "mp"),
        P("mp", "dp"),
        P("dp", None, None, "mp"),
        P("dp", "mp", None),
        P("dp"),
        P("dp"),
        P("dp", None),
        P("dp", None),
    )
    return jax.shard_map(
        per_device,
        mesh=mesh,
        in_specs=placed,
        out_specs=(
            P(("dp", "mp"), None),
            P(("dp", "mp"), None),
            P(),
            P(None, "dp", "mp"),
            P(),
            P("mp", "dp"),
            P(),
            P(),
            P(None, "dp", "mp"),
            P("mp", "dp"),
            P("dp", None, None, "mp"),
            P("dp", "mp", None),
            P(),
            P(),
            P(),
        ),
        check_vma=False,
    )
```

profile of v0, /device:TPU:0, one launch (start us, length us, event | category | flops | bytes accessed | tf_op | source)
XLA Modules:
  0.0 2475.4 jit_solution(6812678828253741262)
XLA Ops:
  42.8 96.5 %all-gather.11.cloned.1.call-done = bf16[3,2048,1024]{2,1,0:T(8,128)(2,1)} async-done(((bf16[3,128,1024]{2,1,0:T(8,128)(2,1)}), bf16[3,2048,1024]{2,1,0:T(8,128)(2,1)}) %all-gather.11.cloned.1.call-update) | async-done | bytes 12582928 | tf_op jit(solution)/shard_map/all_gather | solution.py:171
  186.8 35.4 %collective-permute-start.13 = (bf16[256,8,128]{2,0,1:T(8,128)(2,1)S(1)}, bf16[256,8,128]{2,0,1:T(8,128)(2,1)S(1)}, u32[]{:S(2)}, u32[]{:S(2)}) collective-permute-start(bf16[256,8,128]{2,0,1:T(8,128)(2,1)S(1)} %pad_maximum_fusion.8), channel_id=1, source_target_pairs={{0,6},{2,8},{4,10},{6,12},{8,14},{10,16},{12,18},{14,20},{16,22},{... | collective-permute-start | bytes 1572872 | tf_op jit(solution)/shard_map/ppermute | solution.py:20
  255.2 47.1 %reduce-scatter.6.cloned.1.call-done = f32[128,2048]{1,0:T(8,128)} async-done(((f32[256,2048]{1,0:T(8,128)}), f32[128,2048]{1,0:T(8,128)}) %reduce-scatter.6.cloned.1.call-update) | async-done | bytes 1048592 | tf_op jit(solution)/shard_map/reduce_scatter | solution.py:108
  307.4 19.8 all-gather.15.cloned.1.call-done
  339.6 10.9 scatter_custom_fusion
  381.1 11.8 scatter_custom_fusion.1
  398.0 137.9 %all-to-all-done = bf16[16,85,2048]{2,1,0:T(8,128)(2,1)} async-done(((bf16[16,85,2048]{2,1,0:T(8,128)(2,1)}), bf16[16,85,2048]{2,1,0:T(8,128)(2,1)}, u32[]{:S(2)}, u32[]{:S(2)}) %all-to-all-start) | async-done | bytes 5570592 | tf_op jit(solution)/shard_map/all_to_all | solution.py:244
  535.9 18.6 all-to-all-start.2
  560.5 12.8 fusion.13
  589.7 104.5 %all-to-all-done.2 = bf16[16,85,2048]{2,1,0:T(8,128)(2,1)} async-done(((bf16[16,85,2048]{2,1,0:T(8,128)(2,1)}), bf16[16,85,2048]{2,1,0:T(8,128)(2,1)}, u32[]{:S(2)}, u32[]{:S(2)}) %all-to-all-start.2) | async-done | bytes 5570592 | tf_op jit(solution)/shard_map/all_to_all | solution.py:302
  694.2 49.3 %all-to-all-start.1 = ((bf16[16,85,2048]{2,1,0:T(8,128)(2,1)}), bf16[16,85,2048]{2,1,0:T(8,128)(2,1)}, u32[]{:S(2)}, u32[]{:S(2)}) async-start(bf16[16,85,2048]{2,1,0:T(8,128)(2,1)} %reshape_transpose_reshape.2), calls=%async_computation.2 | async-start | bytes 11534336 | tf_op jit(solution)/shard_map/all_to_all | solution.py:259
  763.5 13.5 reshape.549
  777.0 14.7 bitcast_convert_fusion
  791.7 103.2 %all-to-all-done.1 = bf16[16,85,2048]{2,1,0:T(8,128)(2,1)} async-done(((bf16[16,85,2048]{2,1,0:T(8,128)(2,1)}), bf16[16,85,2048]{2,1,0:T(8,128)(2,1)}, u32[]{:S(2)}, u32[]{:S(2)}) %all-to-all-start.1) | async-done | bytes 5570592 | tf_op jit(solution)/shard_map/all_to_all | solution.py:259
  894.9 25.9 %all-to-all-start.3 = ((bf16[16,85,2048]{2,1,0:T(8,128)(2,1)}), bf16[16,85,2048]{2,1,0:T(8,128)(2,1)}, u32[]{:S(2)}, u32[]{:S(2)}) async-start(bf16[16,85,2048]{2,1,0:T(8,128)(2,1)} %bitcast_convert_fusion), calls=%async_computation.5 | async-start | bytes 11534336 | tf_op jit(solution)/shard_map/all_to_all | solution.py:324
  921.5 10.7 convolution_bitcast_fusion.1
  945.2 14.6 fusion.55
  964.9 12.1 gather_fusion
  992.9 32.9 %all-to-all-done.3 = bf16[16,85,2048]{2,1,0:T(8,128)(2,1)} async-done(((bf16[16,85,2048]{2,1,0:T(8,128)(2,1)}), bf16[16,85,2048]{2,1,0:T(8,128)(2,1)}, u32[]{:S(2)}, u32[]{:S(2)}) %all-to-all-start.3) | async-done | bytes 5570592 | tf_op jit(solution)/shard_map/all_to_all | solution.py:324
  1035.8 13.1 gather_fusion.1
  1068.7 12.8 fusion.41
  1085.2 53.5 %reduce-scatter.10.cloned.1.call-done = f32[128,2048]{1,0:T(8,128)} async-done(((f32[256,2048]{1,0:T(8,128)}), f32[128,2048]{1,0:T(8,128)}) %reduce-scatter.10.cloned.1.call-update) | async-done | bytes 1048592 | tf_op jit(solution)/shard_map/reduce_scatter | solution.py:116
  1143.3 21.4 all-gather.23.cloned.1.call-done
  1218.3 29.1 %collective-permute-done.16 = bf16[256,8,128]{2,0,1:T(8,128)(2,1)S(1)} collective-permute-done((bf16[256,8,128]{2,0,1:T(8,128)(2,1)}, bf16[256,8,128]{2,0,1:T(8,128)(2,1)S(1)}, u32[]{:S(2)}, u32[]{:S(2)}) %collective-permute-start.16) | collective-permute-done | bytes 524320 | tf_op jit(solution)/shard_map/ppermute | solution.py:20
  1267.2 11.1 fusion.92
  1278.3 20.3 fusion.49
  1322.3 70.9 %pad_maximum_fusion = f32[2048,12544]{0,1:T(8,128)} fusion(f32[2048,2816]{0,1:T(8,128)} %fusion.92, f32[2048,5632]{0,1:T(8,128)} %bitcast.256, f32[2048,1024]{0,1:T(8,128)} %fusion.137, f32[2048,3072]{0,1:T(8,128)} %bitcast.257), kind=kLoop, calls=%fused_computation.4 | loop fusion | flops 77070336 | bytes 205520896 | tf_op jit(solution)/shard_map/concatenate | solution.py:417
  1394.5 10.5 convolution_bitcast_fusion.2
  1405.1 14.4 convolution_bitcast_fusion
  1434.0 62.0 %all-reduce = (f32[2,2048]{1,0:T(2,128)}, f32[3,2048]{1,0:T(4,128)}, f32[2048]{0:T(1024)}, f32[4]{0:T(128)S(1)}) all-reduce(f32[2,2048]{1,0:T(2,128)S(1)} %pad_maximum_fusion.13, f32[3,2048]{1,0:T(4,128)S(1)} %constant_dynamic-update-slice_fusion.25, f32[2048]{0:T(1024)S(1)} %bitcast.285, ...), channel_id=1, replica_groups=mesh['dp'=16,'mp'=2] {'dp','mp'}, use_global_device_ids=true, to_apply=%region_20.21 | all-reduce | flops 12292 | bytes 98336 | tf_op jit(solution)/shard_map/psum | solution.py:444
  1497.8 841.7 %reduce-scatter.14.cloned.1.call-done = f32[128,12544]{0,1:T(8,128)} async-done(((f32[2048,12544]{0,1:T(8,128)}), f32[128,12544]{0,1:T(8,128)}) %reduce-scatter.14.cloned.1.call-update) | async-done | bytes 6422544 | tf_op jit(solution)/shard_map/reduce_scatter | solution.py:416
  2356.7 110.4 %all-reduce.3.cloned.1.call-done = f32[2048,16]{0,1:T(8,128)} async-done(((f32[2048,16]{0,1:T(8,128)}), f32[2048,16]{0,1:T(8,128)}) %all-reduce.3.cloned.1.call-update) | async-done | bytes 131088 | tf_op jit(solution)/shard_map/psum | solution.py:444
  (395 shorter events, 415.7 us)
Async XLA Ops:
  7.2 35.6 %all-gather.9.cloned.1.call-start = ((), (), s32[]{:S(2)}) async-start(), calls=%async_computation.9 | async-start | bytes 1572864 | tf_op jit(solution)/shard_map/all_gather | solution.py:104
  12.1 127.2 %all-gather.11.cloned.1.call-start = ((), (), s32[]{:S(2)}) async-start(), calls=%async_computation.10 | async-start | bytes 13369344 | tf_op jit(solution)/shard_map/all_gather | solution.py:171
  12.8 237.3 %all-gather.13.cloned.1.call-start = ((), (), s32[]{:S(2)}) async-start(), calls=%async_computation.11 | async-start | bytes 4456448 | tf_op jit(solution)/shard_map/all_gather | solution.py:172
  12.9 24.2 collective-permute-start.6
  29.4 273.0 %reduce-scatter.6.cloned.1.call-start = ((), (), s32[]{:S(2)}) async-start(), calls=%async_computation.12 | async-start | bytes 3145728 | tf_op jit(solution)/shard_map/reduce_scatter | solution.py:108
  150.6 73.5 %collective-permute-start.3 = (bf16[256,8,128]{0,2,1:T(8,128)(2,1)}, bf16[256,8,128]{0,2,1:T(8,128)(2,1)S(1)}, u32[]{:S(2)}, u32[]{:S(2)}) collective-permute-start(bf16[256,8,128]{0,2,1:T(8,128)(2,1)} %bitcast.267), channel_id=1, source_target_pairs={{0,2},{2,4},{4,6},{6,8},{8,10},{10,12},{12,14},{14,16},{16,18},{18... | collective-permute-start | bytes 1572872 | tf_op jit(solution)/shard_map/ppermute | solution.py:20
  152.7 69.4 %collective-permute-start.2 = (bf16[256,8,128]{0,2,1:T(8,128)(2,1)}, bf16[256,8,128]{0,2,1:T(8,128)(2,1)S(1)}, u32[]{:S(2)}, u32[]{:S(2)}) collective-permute-start(bf16[256,8,128]{0,2,1:T(8,128)(2,1)} %bitcast.268), channel_id=1, source_target_pairs={{0,4},{2,6},{4,8},{6,10},{8,12},{10,14},{12,16},{14,18},{16,20},{1... | collective-permute-start | bytes 1572872 | tf_op jit(solution)/shard_map/ppermute | solution.py:20
  155.2 31.5 %collective-permute-start.1 = (bf16[256,8,128]{0,2,1:T(8,128)(2,1)}, bf16[256,8,128]{0,2,1:T(8,128)(2,1)S(1)}, u32[]{:S(2)}, u32[]{:S(2)}) collective-permute-start(bf16[256,8,128]{0,2,1:T(8,128)(2,1)} %bitcast.269), channel_id=1, source_target_pairs={{0,6},{2,8},{4,10},{6,12},{8,14},{10,16},{12,18},{14,20},{16,22},{... | collective-permute-start | bytes 1572872 | tf_op jit(solution)/shard_map/ppermute | solution.py:20
  165.7 74.4 %collective-permute-start.15 = (bf16[256,8,128]{2,0,1:T(8,128)(2,1)S(1)}, bf16[256,8,128]{2,0,1:T(8,128)(2,1)S(1)}, u32[]{:S(2)}, u32[]{:S(2)}) collective-permute-start(bf16[256,8,128]{2,0,1:T(8,128)(2,1)S(1)} %pad_maximum_fusion.8), channel_id=1, source_target_pairs={{0,2},{2,4},{4,6},{6,8},{8,10},{10,12},{12,14},{14,16},{16,18},{18... | collective-permute-start | bytes 1572872 | tf_op jit(solution)/shard_map/ppermute | solution.py:20
  177.5 46.8 %collective-permute-start.12 = (bf16[256,8,128]{2,0,1:T(8,128)(2,1)S(1)}, bf16[256,8,128]{2,0,1:T(8,128)(2,1)S(1)}, u32[]{:S(2)}, u32[]{:S(2)}) collective-permute-start(bf16[256,8,128]{2,0,1:T(8,128)(2,1)S(1)} %pad_maximum_fusion.8), channel_id=1, source_target_pairs={{0,8},{2,10},{4,12},{6,14},{8,16},{10,18},{12,20},{14,22},{16,24},... | collective-permute-start | bytes 1572872 | tf_op jit(solution)/shard_map/ppermute | solution.py:20
  186.8 46.2 %collective-permute-start.13 = (bf16[256,8,128]{2,0,1:T(8,128)(2,1)S(1)}, bf16[256,8,128]{2,0,1:T(8,128)(2,1)S(1)}, u32[]{:S(2)}, u32[]{:S(2)}) collective-permute-start(bf16[256,8,128]{2,0,1:T(8,128)(2,1)S(1)} %pad_maximum_fusion.8), channel_id=1, source_target_pairs={{0,6},{2,8},{4,10},{6,12},{8,14},{10,16},{12,18},{14,20},{16,22},{... | collective-permute-start | bytes 1572872 | tf_op jit(solution)/shard_map/ppermute | solution.py:20
  255.2 72.0 %all-gather.15.cloned.1.call-start = ((), (), s32[]{:S(2)}) async-start(), calls=%async_computation.13 | async-start | bytes 1572864 | tf_op jit(solution)/shard_map/all_gather | solution.py:104
  305.8 55.9 %all-gather.21.cloned.1.call-start = ((), (), s32[]{:S(2)}) async-start(), calls=%async_computation.17 | async-start | bytes 1572864 | tf_op jit(solution)/shard_map/all_gather | solution.py:112
  306.3 615.1 %all-gather.17.cloned.1.call-start = ((), (), s32[]{:S(2)}) async-start(), calls=%async_computation.14 | async-start | bytes 24510464 | tf_op jit(solution)/shard_map/all_gather | solution.py:173
  355.6 180.3 %all-to-all-start = ((bf16[16,85,2048]{2,1,0:T(8,128)(2,1)}), bf16[16,85,2048]{2,1,0:T(8,128)(2,1)}, u32[]{:S(2)}, u32[]{:S(2)}) async-start(bf16[16,85,2048]{2,1,0:T(8,128)(2,1)} %reshape.478), calls=%async_computation.1 | async-start | bytes 11534336 | tf_op jit(solution)/shard_map/all_to_all | solution.py:244
  535.9 158.2 %all-to-all-start.2 = ((bf16[16,85,2048]{2,1,0:T(8,128)(2,1)}), bf16[16,85,2048]{2,1,0:T(8,128)(2,1)}, u32[]{:S(2)}, u32[]{:S(2)}) async-start(bf16[16,85,2048]{2,1,0:T(8,128)(2,1)} %reshape.484), calls=%async_computation.4 | async-start | bytes 11534336 | tf_op jit(solution)/shard_map/all_to_all | solution.py:302
  554.5 381.2 %all-gather.19.cloned.1.call-start = ((), (), s32[]{:S(2)}) async-start(), calls=%async_computation.15 | async-start | bytes 12255232 | tf_op jit(solution)/shard_map/all_gather | solution.py:174
  694.2 200.7 %all-to-all-start.1 = ((bf16[16,85,2048]{2,1,0:T(8,128)(2,1)}), bf16[16,85,2048]{2,1,0:T(8,128)(2,1)}, u32[]{:S(2)}, u32[]{:S(2)}) async-start(bf16[16,85,2048]{2,1,0:T(8,128)(2,1)} %reshape_transpose_reshape.2), calls=%async_computation.2 | async-start | bytes 11534336 | tf_op jit(solution)/shard_map/all_to_all | solution.py:259
  894.9 130.9 %all-to-all-start.3 = ((bf16[16,85,2048]{2,1,0:T(8,128)(2,1)}), bf16[16,85,2048]{2,1,0:T(8,128)(2,1)}, u32[]{:S(2)}, u32[]{:S(2)}) async-start(bf16[16,85,2048]{2,1,0:T(8,128)(2,1)} %bitcast_convert_fusion), calls=%async_computation.5 | async-start | bytes 11534336 | tf_op jit(solution)/shard_map/all_to_all | solution.py:324
  920.8 217.9 %reduce-scatter.10.cloned.1.call-start = ((), (), s32[]{:S(2)}) async-start(), calls=%async_computation.18 | async-start | bytes 3145728 | tf_op jit(solution)/shard_map/reduce_scatter | solution.py:116
  1085.1 79.5 %all-gather.23.cloned.1.call-start = ((), (), s32[]{:S(2)}) async-start(), calls=%async_computation.19 | async-start | bytes 1572864 | tf_op jit(solution)/shard_map/all_gather | solution.py:112
  1143.2 279.4 %reduce-scatter.12.cloned.1.call-start = ((), (), s32[]{:S(2)}) async-start(), calls=%async_computation.20 | async-start | bytes 3145728 | tf_op jit(solution)/shard_map/reduce_scatter | solution.py:116
  1186.8 19.6 collective-permute-start.23
  1188.1 24.2 collective-permute-start.22
  1189.4 27.1 %collective-permute-start.21 = (bf16[256,8,128]{0,2,1:T(8,128)(2,1)S(1)}, bf16[256,8,128]{0,2,1:T(8,128)(2,1)S(1)}, u32[]{:S(2)}, u32[]{:S(2)}) collective-permute-start(bf16[256,8,128]{0,2,1:T(8,128)(2,1)S(1)} %get-tuple-element.45), channel_id=1, source_target_pairs={{6,0},{8,2},{10,4},{12,6},{14,8},{16,10},{18,12},{20,14},{22,16},{... | collective-permute-start | bytes 1572872 | tf_op jit(solution)/shard_map/ppermute | solution.py:20
  1203.7 43.7 %collective-permute-start.16 = (bf16[256,8,128]{2,0,1:T(8,128)(2,1)}, bf16[256,8,128]{2,0,1:T(8,128)(2,1)S(1)}, u32[]{:S(2)}, u32[]{:S(2)}) collective-permute-start(bf16[256,8,128]{2,0,1:T(8,128)(2,1)} %get-tuple-element.38), channel_id=1, source_target_pairs={{8,0},{10,2},{12,4},{14,6},{16,8},{18,10},{20,12},{22,14},{24,16},... | collective-permute-start | bytes 1572872 | tf_op jit(solution)/shard_map/ppermute | solution.py:20
  1205.1 42.3 %collective-permute-start.19 = (bf16[256,8,128]{2,0,1:T(8,128)(2,1)}, bf16[256,8,128]{2,0,1:T(8,128)(2,1)}, u32[]{:S(2)}, u32[]{:S(2)}) collective-permute-start(bf16[256,8,128]{2,0,1:T(8,128)(2,1)} %get-tuple-element.39), channel_id=1, source_target_pairs={{2,0},{4,2},{6,4},{8,6},{10,8},{12,10},{14,12},{16,14},{18,16},{20... | collective-permute-start | bytes 1572872 | tf_op jit(solution)/shard_map/ppermute | solution.py:20
  1206.4 41.0 %collective-permute-start.18 = (bf16[256,8,128]{2,0,1:T(8,128)(2,1)}, bf16[256,8,128]{2,0,1:T(8,128)(2,1)}, u32[]{:S(2)}, u32[]{:S(2)}) collective-permute-start(bf16[256,8,128]{2,0,1:T(8,128)(2,1)} %get-tuple-element.40), channel_id=1, source_target_pairs={{4,0},{6,2},{8,4},{10,6},{12,8},{14,10},{16,12},{18,14},{20,16},{2... | collective-permute-start | bytes 1572872 | tf_op jit(solution)/shard_map/ppermute | solution.py:20
  1212.3 35.0 %collective-permute-start.17 = (bf16[256,8,128]{2,0,1:T(8,128)(2,1)S(1)}, bf16[256,8,128]{2,0,1:T(8,128)(2,1)}, u32[]{:S(2)}, u32[]{:S(2)}) collective-permute-start(bf16[256,8,128]{2,0,1:T(8,128)(2,1)S(1)} %get-tuple-element.41), channel_id=1, source_target_pairs={{6,0},{8,2},{10,4},{12,6},{14,8},{16,10},{18,12},{20,14},{22,16},{... | collective-permute-start | bytes 1572872 | tf_op jit(solution)/shard_map/ppermute | solution.py:20
  1267.2 158.0 %reduce-scatter.8.cloned.1.call-start = ((), (), s32[]{:S(2)}) async-start(), calls=%async_computation.16 | async-start | bytes 3145728 | tf_op jit(solution)/shard_map/reduce_scatter | solution.py:108
  1305.9 1033.7 %reduce-scatter.14.cloned.1.call-start = ((), (), s32[]{:S(2)}) async-start(), calls=%async_computation.21 | async-start | bytes 109182976 | tf_op jit(solution)/shard_map/reduce_scatter | solution.py:416
  1393.2 1073.9 %all-reduce.3.cloned.1.call-start = ((), (), s32[]{:S(2)}) async-start(), calls=%async_computation.22 | async-start | bytes 262144 | tf_op jit(solution)/shard_map/psum | solution.py:444
  (94 other events, 5529.2 us)
Sparse Core Ops, SparseCore 0:
  12.2 23.9 all-gather.8
  38.4 100.7 all-gather.10
  141.4 64.4 all-gather.12
  255.3 47.0 reduce-scatter.5
  305.9 21.2 all-gather.14
  328.7 21.2 all-gather.20
  351.7 313.6 all-gather.16
  667.8 214.7 all-gather.18
  1085.3 53.3 reduce-scatter.9
  1143.3 21.3 all-gather.22
  1267.3 50.8 reduce-scatter.11
  1320.9 35.7 reduce-scatter.7
  1393.3 946.1 reduce-scatter.13
  2345.5 121.5 all-reduce.2
where the time goes:
time: 2480 us
  waiting for transfers between devices  1640 us (66%)
  matrix products  240 us (10%)
  starting transfers between devices  190 us (8%)
  local copies, waits for them, and re-layouts  189 us (8%)
  other arithmetic  141 us (6%)
  blocking collectives  62 us (2%)
    reduce_scatter x1, waiting for transfers between devices, per_device(): lax.psum_scatter(jnp.concatenate([term_qkv, term_out, term_sgu, term_sdow...  842 us
    all_to_all x1, waiting for transfers between devices, per_device(): lax.all_to_all(outbound.reshape(dp_size, expert_here * capacity, model_wi...  138 us
    psum x1, waiting for transfers between devices, per_device(): lax.psum((jnp.stack([grad_gain_attn, grad_gain_moe]), grad_bias, grad_rou...  110 us
    all_to_all x1, waiting for transfers between devices, per_device(): lax.all_to_all(outbound_grad.reshape(dp_size, expert_here * capacity, mod...  105 us
    all_to_all x1, waiting for transfers between devices, per_device(): lax.all_to_all(to_sources(expert_out, dp_size, expert_here, capacity), 'd...  103 us
    all_gather x1, waiting for transfers between devices, per_device(): lax.all_gather(qkv_weight, 'dp', axis=1, tiled=True)  96.5 us
    ppermute x24, starting transfers between devices, from_behind(): return lax.ppermute(block, axis, route)  89.4 us
    concatenate x1, other arithmetic, per_device(): jnp.concatenate([term_qkv, term_out, term_sgu, term_sdown], 1)  70.9 us
  transfers between devices with their start and end apart: 42, of which 19 were waited for; matrix products, arithmetic and copies ran while one was open for 18% of the time, Pallas kernels for 0%

commit v1 on v0

v1 whole, which is shorter than its diff:
```python
import functools

import jax
import jax.numpy as jnp
from jax import lax
from jax.experimental import pallas as pl
from jax.experimental.pallas import tpu as pltpu
from jax.sharding import Mesh
from jax.sharding import PartitionSpec as P

HEAD = 128
SEQ = 4096
WINDOW = 1024

EPSILON = 1e-06
ROPE_BASE = 1000000.0
MASKED = -1e30

LINE = 4
GROUP = ("z", "y", "c")
EVERY = ("g", "z", "y", "c", "x")
SWAP = [(0, 1), (1, 0)]
ORDERS = (("x", "y", "z"), ("y", "z", "x"), ("z", "x", "y"))
VMEM_LIMIT = 56 * 1024 * 1024

F32 = jnp.float32
BF16 = jnp.bfloat16


def swap(value, axis):
    return lax.ppermute(value, axis, SWAP)


def pair_gather(value, axis):
    index = lax.axis_index(axis)
    other = swap(value, axis)
    return jnp.where(index == 0, jnp.stack([value, other]), jnp.stack([other, value]))


def line_gather(value, axis):
    index = lax.axis_index(axis)
    up = [(k, k + 1) for k in range(LINE - 1)]
    down = [(k + 1, k) for k in range(LINE - 1)]
    below, above = [], []
    rising = falling = value
    for step in range(1, LINE):
        rising = lax.ppermute(rising, axis, up[step - 1 :])
        falling = lax.ppermute(falling, axis, down[: LINE - step])
        below.append(rising)
        above.append(falling)
    placed = []
    for slot in range(LINE):
        block = value
        for here in range(LINE):
            if here != slot:
                source = below[here - slot - 1] if slot < here else above[slot - here - 1]
                block = jnp.where(index == here, source, block)
        placed.append(block)
    return jnp.stack(placed)


def gather_axis(value, axis):
    return line_gather(value, axis) if axis == "z" else pair_gather(value, axis)


def take(value, index, dim):
    return lax.dynamic_index_in_dim(value, index, dim, keepdims=False)


def pair_scatter(value, axis, dim):
    index = lax.axis_index(axis)
    other = swap(take(value, 1 - index, dim), axis)
    return take(value, index, dim).astype(F32) + other.astype(F32)


def line_scatter(value, axis, dim):
    index = lax.axis_index(axis)
    up = [(k, k + 1) for k in range(LINE - 1)]
    down = [(k + 1, k) for k in range(LINE - 1)]
    rising = falling = None
    for step in range(1, LINE):
        going_up = take(value, jnp.minimum(index + LINE - step, LINE - 1), dim)
        going_down = take(value, jnp.maximum(index - (LINE - step), 0), dim)
        if step > 1:
            going_up = (going_up.astype(F32) + rising.astype(F32)).astype(value.dtype)
            going_down = (going_down.astype(F32) + falling.astype(F32)).astype(value.dtype)
        rising = lax.ppermute(going_up, axis, up[:step])
        falling = lax.ppermute(going_down, axis, down[LINE - 1 - step :])
    return take(value, index, dim).astype(F32) + rising.astype(F32) + falling.astype(F32)


def scatter_axis(value, axis, dim):
    return line_scatter(value, axis, dim) if axis == "z" else pair_scatter(value, axis, dim)


def cuts_of(rows):
    unit = rows // 8
    return (0, 2 * unit, 5 * unit, rows)


def gather_group(shard):
    rows, width = shard.shape
    cuts = cuts_of(rows)
    pieces = []
    for piece, order in enumerate(ORDERS):
        value = shard[cuts[piece] : cuts[piece + 1]]
        axes = []
        for axis in order + ("c",):
            value = gather_axis(value, axis)
            axes.insert(0, axis)
        turned = [axes.index(axis) for axis in ("z", "y", "c", "x")]
        value = value.transpose(*turned, 4, 5)
        pieces.append(value.reshape(8 * LINE, cuts[piece + 1] - cuts[piece], width))
    return jnp.concatenate(pieces, 1).reshape(8 * LINE * rows, width)


def scatter_group(partial_rows):
    total, width = partial_rows.shape
    rows = total // (8 * LINE)
    cuts = cuts_of(rows)
    whole = partial_rows.reshape(LINE, 2, 2, 2, rows, width)
    pieces = []
    for piece, order in enumerate(ORDERS):
        value = whole[:, :, :, :, cuts[piece] : cuts[piece + 1]]
        axes = ["z", "y", "c", "x"]
        for axis in ("c",) + order[::-1]:
            dim = axes.index(axis)
            value = scatter_axis(value, axis, dim)
            axes.pop(dim)
            if axes:
                value = value.astype(BF16)
        pieces.append(value)
    return jnp.concatenate(pieces, 0)


def gather_plane(shard):
    rows, width = shard.shape
    half = rows // 2
    pieces = []
    for piece, order in enumerate((("x", "y"), ("y", "x"))):
        value = shard[piece * half : (piece + 1) * half]
        for axis in order:
            value = pair_gather(value, axis)
        if piece == 0:
            value = pair_gather(value, "c").transpose(1, 0, 2, 3, 4)
        else:
            value = pair_gather(value, "c").transpose(2, 0, 1, 3, 4)
        pieces.append(value.reshape(8, half, width))
    return jnp.concatenate(pieces, 1).reshape(8 * rows, width)


def scatter_plane(partial_rows):
    total, width = partial_rows.shape
    rows = total // 8
    half = rows // 2
    whole = partial_rows.reshape(2, 2, 2, rows, width)
    pieces = []
    for piece, order in enumerate((("y", "x"), ("x", "y"))):
        value = whole[:, :, :, piece * half : (piece + 1) * half]
        axes = ["y", "c", "x"]
        for axis in ("c",) + order:
            dim = axes.index(axis)
            value = pair_scatter(value, axis, dim)
            axes.pop(dim)
            if axes:
                value = value.astype(BF16)
        pieces.append(value)
    return jnp.concatenate(pieces, 0)


def exchange(value, axes):
    return lax.all_to_all(value, axes, split_axis=0, concat_axis=0, tiled=True)


def turn(value, cosine, sine):
    return value * cosine + pltpu.roll(value, HEAD // 2, 1) * sine


def turn_back(value, cosine, sine):
    return value * cosine - pltpu.roll(value, HEAD // 2, 1) * sine


def project_kernel(heads, rows_ref, weight_ref, bias_ref, cos_ref, sin_ref, out_ref):
    projected = (
        jnp.dot(rows_ref[...], weight_ref[...], preferred_element_type=F32) + bias_ref[...]
    )
    for part in range(3 * heads):
        block = projected[:, part * HEAD : (part + 1) * HEAD]
        if part < 2 * heads:
            block = turn(block, cos_ref[...], sin_ref[...])
        out_ref[:, part * HEAD : (part + 1) * HEAD] = block.astype(BF16)


def project(rows, weight, bias, cosine, sine):
    count, model = rows.shape
    width = weight.shape[1]
    step = count // 4
    return pl.pallas_call(
        functools.partial(project_kernel, width // (3 * HEAD)),
        grid=(4,),
        in_specs=[
            pl.BlockSpec((step, model), lambda i: (i, 0)),
            pl.BlockSpec((model, width), lambda i: (0, 0)),
            pl.BlockSpec((1, width), lambda i: (0, 0)),
            pl.BlockSpec((step, HEAD), lambda i: (i, 0)),
            pl.BlockSpec((step, HEAD), lambda i: (i, 0)),
        ],
        out_specs=pl.BlockSpec((step, width), lambda i: (i, 0)),
        out_shape=jax.ShapeDtypeStruct((count, width), BF16),
        compiler_params=pltpu.CompilerParams(vmem_limit_bytes=VMEM_LIMIT),
        cost_estimate=pl.CostEstimate(
            flops=2 * count * model * width,
            bytes_accessed=2 * (count * model + model * width + count * width),
            transcendentals=0,
        ),
        name="project",
    )(rows, weight, bias, cosine, sine)


def block_probs(query, keys, seg_q, seg_k, valid_k, first, reach):
    rows, span = query.shape[0], keys.shape[0]
    scores = lax.dot_general(query, keys, (((1,), (1,)), ((), ())), preferred_element_type=F32)
    scores = scores * (HEAD ** (-0.5))
    distance = (
        reach
        + lax.broadcasted_iota(jnp.int32, (rows, span), 0)
        - lax.broadcasted_iota(jnp.int32, (rows, span), 1)
    )
    allowed = (
        (distance >= 0)
        & (distance < WINDOW)
        & (seg_q == seg_k)
        & ((valid_k == 1) | (distance == 0))
    )
    scores = jnp.where(allowed, scores, MASKED)
    powers = jnp.exp(scores - jnp.max(scores, axis=-1, keepdims=True))
    return powers / jnp.sum(powers, axis=-1, keepdims=True)


def attend_kernel(step, reach, q_ref, k_ref, v_ref, segq_ref, segk_ref, valid_ref, out_ref):
    first = pl.multiple_of(pl.program_id(1) * step, step)
    span = pl.ds(first, step + reach)
    probs = block_probs(
        q_ref[...], k_ref[span, :], segq_ref[...], segk_ref[:, span], valid_ref[:, span], first, reach
    )
    out_ref[...] = jnp.dot(
        probs.astype(BF16), v_ref[span, :], preferred_element_type=F32
    ).astype(BF16)


def attend(queries, keys, values, seg_q, seg_k, valid_k):
    count, width = queries.shape
    held = keys.shape[0]
    reach = held - count
    step = count // 4
    heads = width // HEAD
    flops = 4 * count * (step + reach) * width
    return pl.pallas_call(
        functools.partial(attend_kernel, step, reach),
        grid=(heads, 4),
        in_specs=[
            pl.BlockSpec((step, HEAD), lambda h, i: (i, h)),
            pl.BlockSpec((held, HEAD), lambda h, i: (0, h)),
            pl.BlockSpec((held, HEAD), lambda h, i: (0, h)),
            pl.BlockSpec((step, 1), lambda h, i: (i, 0)),
            pl.BlockSpec((1, held), lambda h, i: (0, 0)),
            pl.BlockSpec((1, held), lambda h, i: (0, 0)),
        ],
        out_specs=pl.BlockSpec((step, HEAD), lambda h, i: (i, h)),
        out_shape=jax.ShapeDtypeStruct((count, width), BF16),
        compiler_params=pltpu.CompilerParams(vmem_limit_bytes=VMEM_LIMIT),
        cost_estimate=pl.CostEstimate(
            flops=flops, bytes_accessed=8 * held * width, transcendentals=flops // (4 * HEAD)
        ),
        name="attend",
    )(queries, keys, values, seg_q, seg_k, valid_k)


def attend_back_kernel(
    step, reach, q_ref, k_ref, v_ref, g_ref, segq_ref, segk_ref, valid_ref, cos_ref, sin_ref,
    dq_ref, dk_ref, dv_ref,
):
    block = pl.program_id(1)
    first = pl.multiple_of(block * step, step)
    span = pl.ds(first, step + reach)

    @pl.when(block == 0)
    def _():
        dk_ref[...] = jnp.zeros_like(dk_ref)
        dv_ref[...] = jnp.zeros_like(dv_ref)

    query, keys, grad = q_ref[...], k_ref[span, :], g_ref[...]
    probs = block_probs(
        query, keys, segq_ref[...], segk_ref[:, span], valid_ref[:, span], first, reach
    )
    g_probs = lax.dot_general(
        grad, v_ref[span, :], (((1,), (1,)), ((), ())), preferred_element_type=F32
    )
    inner = jnp.sum(probs * g_probs, axis=-1, keepdims=True)
    g_scores = (probs * (g_probs - inner)).astype(BF16)
    scale = HEAD ** (-0.5)
    dq = jnp.dot(g_scores, keys, preferred_element_type=F32) * scale
    here = pl.ds(pl.multiple_of(first + reach, step), step)
    dq_ref[...] = turn_back(dq, cos_ref[here, :], sin_ref[here, :]).astype(BF16)
    dk_ref[span, :] += (
        lax.dot_general(g_scores, query, (((0,), (0,)), ((), ())), preferred_element_type=F32)
        * scale
    )
    dv_ref[span, :] += lax.dot_general(
        probs.astype(BF16), grad, (((0,), (0,)), ((), ())), preferred_element_type=F32
    )

    @pl.when(block == pl.num_programs(1) - 1)
    def _():
        dk_ref[...] = turn_back(dk_ref[...], cos_ref[...], sin_ref[...])


def attend_back(queries, keys, values, grad, seg_q, seg_k, valid_k, cosine, sine):
    count, width = queries.shape
    held = keys.shape[0]
    reach = held - count
    step = count // 4
    heads = width // HEAD
    flops = 10 * count * (step + reach) * width
    head_rows = pl.BlockSpec((step, HEAD), lambda h, i: (i, h))
    head_all = pl.BlockSpec((held, HEAD), lambda h, i: (0, h))
    return pl.pallas_call(
        functools.partial(attend_back_kernel, step, reach),
        grid=(heads, 4),
        in_specs=[
            head_rows,
            head_all,
            head_all,
            head_rows,
            pl.BlockSpec((step, 1), lambda h, i: (i, 0)),
            pl.BlockSpec((1, held), lambda h, i: (0, 0)),
            pl.BlockSpec((1, held), lambda h, i: (0, 0)),
            pl.BlockSpec((held, HEAD), lambda h, i: (0, 0)),
            pl.BlockSpec((held, HEAD), lambda h, i: (0, 0)),
        ],
        out_specs=[head_rows, head_all, head_all],
        out_shape=[
            jax.ShapeDtypeStruct((count, width), BF16),
            jax.ShapeDtypeStruct((held, width), F32),
            jax.ShapeDtypeStruct((held, width), F32),
        ],
        compiler_params=pltpu.CompilerParams(vmem_limit_bytes=VMEM_LIMIT),
        cost_estimate=pl.CostEstimate(
            flops=flops, bytes_accessed=24 * held * width, transcendentals=flops // (10 * HEAD)
        ),
        name="attend_back",
    )(queries, keys, values, grad, seg_q, seg_k, valid_k, cosine, sine)


def combine_kernel(hidden_ref, weight_ref, place_ref, rows_ref, out_ref):
    own = jnp.dot(hidden_ref[...], weight_ref[...], preferred_element_type=F32)
    routed = lax.dot_general(
        place_ref[0], rows_ref[0], (((0,), (0,)), ((), ())), preferred_element_type=F32
    )
    out_ref[...] = (own + routed).astype(BF16)


def combine(hidden, weight, place, rows):
    count, inner = hidden.shape
    model = weight.shape[1]
    blocks, slots, step = place.shape
    return pl.pallas_call(
        combine_kernel,
        grid=(blocks,),
        in_specs=[
            pl.BlockSpec((step, inner), lambda i: (i, 0)),
            pl.BlockSpec((inner, model), lambda i: (0, 0)),
            pl.BlockSpec((1, slots, step), lambda i: (i, 0, 0)),
            pl.BlockSpec((1, slots, model), lambda i: (i, 0, 0)),
        ],
        out_specs=pl.BlockSpec((step, model), lambda i: (i, 0)),
        out_shape=jax.ShapeDtypeStruct((count, model), BF16),
        compiler_params=pltpu.CompilerParams(vmem_limit_bytes=VMEM_LIMIT),
        cost_estimate=pl.CostEstimate(
            flops=2 * count * model * (inner + slots),
            bytes_accessed=2 * (count * model + count * inner + blocks * slots * model),
            transcendentals=0,
        ),
        name="combine",
    )(hidden, weight, place, rows)


def norm_scale(rows_in):
    return lax.rsqrt(jnp.mean(rows_in * rows_in, axis=-1, keepdims=True) + EPSILON)


def norm_back(rows_in, scaling, gain, grad):
    unit_rows = rows_in * scaling
    grad_unit = grad * gain
    return scaling * (
        grad_unit - unit_rows * jnp.mean(grad_unit * unit_rows, axis=-1, keepdims=True)
    )


def swish(gate_in):
    return gate_in * jax.nn.sigmoid(gate_in)


def swish_back(gate_in, up_in, grad):
    sigma = jax.nn.sigmoid(gate_in)
    grad_gate = grad * up_in * sigma * (1.0 + gate_in * (1.0 - sigma))
    return (grad_gate, grad * gate_in * sigma)


def rope_tables(first_row, row_count):
    placing = (first_row + jnp.arange(row_count, dtype=jnp.int32)) % SEQ
    frequency = ROPE_BASE ** (-(jnp.arange(HEAD // 2, dtype=F32) * 2.0 / HEAD))
    angles = placing.astype(F32)[:, None] * frequency[None, :]
    cosine, sine = jnp.cos(angles), jnp.sin(angles)
    return (
        jnp.concatenate([cosine, cosine], 1),
        jnp.concatenate([-sine, sine], 1),
    )


def per_device(
    hidden_in,
    cotangent,
    norm_gains,
    qkv_weight,
    qkv_bias,
    out_weight,
    router_weight,
    shared_gate_vec,
    shared_gate_up,
    shared_down,
    expert_gate_up,
    expert_down,
    segments,
    valid_mask,
    routes,
    slots,
):
    groups = lax.axis_size("g")
    blocks = segments.shape[0]
    rows_here, model = hidden_in.shape
    weight_rows, local_cols = qkv_weight.shape[1:]
    shared_cols = shared_gate_up.shape[2]
    experts = router_weight.shape[1]
    in_group = 4 * LINE
    cols = local_cols // 4
    hidden_own = shared_cols // in_group
    expert_cols = expert_down.shape[1]
    capacity = -(-(blocks * routes.shape[1] * 4 // (3 * experts)) // 16) * 16
    plane_rows = 4 * blocks
    group_rows = in_group * blocks
    z, y, c, x = (lax.axis_index(axis) for axis in ("z", "y", "c", "x"))
    g = lax.axis_index("g")
    expert = ((g * LINE + z) * 2 + y) * 2 + c

    numbers = jnp.concatenate([segments[None], valid_mask[None], routes.T, slots.T], 0)
    numbers = lax.all_gather(numbers, ("g",) + GROUP, axis=0)
    top = routes.shape[1]

    residual = hidden_in.astype(F32)
    gain_attn, gain_moe = norm_gains[0], norm_gains[1]
    scale_attn = norm_scale(residual)
    rows_attn = gather_plane((residual * scale_attn * gain_attn).astype(BF16))
    qkv_cut = (
        qkv_weight.reshape(3, weight_rows, 4, cols)
        .transpose(2, 1, 0, 3)
        .reshape(4, weight_rows, 3 * cols)
    )
    w_qkv = exchange(qkv_cut, ("y", "c")).reshape(4 * weight_rows, 3 * cols)
    w_qkv = lax.all_gather(w_qkv, ("g", "z"), axis=0, tiled=True)
    w_out = lax.all_gather(out_weight.T, ("x", "g") + GROUP, axis=0, tiled=True)
    w_out = w_out.reshape(2, model, local_cols)
    shared_cut = jnp.concatenate(
        [
            shared_gate_up[0].reshape(weight_rows, in_group, hidden_own),
            shared_gate_up[1].reshape(weight_rows, in_group, hidden_own),
            shared_down.T.reshape(weight_rows, in_group, hidden_own),
        ],
        2,
    ).transpose(1, 0, 2)
    w_shared = exchange(shared_cut, GROUP).reshape(in_group * weight_rows, 3 * hidden_own)
    w_shared = lax.all_gather(w_shared, "g", axis=0, tiled=True) if groups > 1 else w_shared

    here = x * local_cols + (y * 2 + c) * cols
    bias = lax.dynamic_slice_in_dim(qkv_bias, here, cols, 1).astype(F32).reshape(1, 3 * cols)
    cosine, sine = rope_tables((z + LINE - 1) * plane_rows, 2 * plane_rows)
    projected = project(rows_attn, w_qkv, bias, cosine[plane_rows:], sine[plane_rows:])
    queries = projected[:, :cols]
    ahead = [(k, k + 1) for k in range(LINE - 1)]
    key_value = projected[:, cols:]
    before = lax.ppermute(key_value, "z", ahead)
    key_value = jnp.concatenate([before, key_value], 0)
    keys, values = key_value[:, :cols], key_value[:, cols:]
    group_numbers = lax.dynamic_slice_in_dim(numbers, g * in_group, in_group, 0)
    padded = jnp.concatenate([jnp.full((4, 2, blocks), -1, jnp.int32), group_numbers[:, :2]], 0)
    near = lax.dynamic_slice_in_dim(padded, z * 4, 8, 0)
    seg_k = near[:, 0].reshape(1, 2 * plane_rows)
    valid_k = near[:, 1].reshape(1, 2 * plane_rows)
    seg_q = near[4:, 0].reshape(plane_rows, 1)
    attended = attend(queries, keys, values, seg_q, seg_k, valid_k)
    leaving = attended.reshape(2, 2, 2, rows_here, cols).transpose(2, 0, 1, 3, 4)
    arrived = exchange(leaving.reshape(8, rows_here, cols), ("x", "y", "c"))
    attn_flat = arrived.reshape(2, 4, rows_here, cols).transpose(0, 2, 1, 3)
    attn_flat = attn_flat.reshape(2, rows_here, local_cols)
    attn_rows = jnp.einsum("xtc,xdc->td", attn_flat, w_out, preferred_element_type=F32)
    middle = residual + attn_rows
    scale_moe = norm_scale(middle)
    own_moe = (middle * scale_moe * gain_moe).astype(BF16)

    rows_moe = gather_group(own_moe)
    rows_grad = gather_group(cotangent)
    if groups > 1:
        all_moe = lax.all_gather(rows_moe, "g", axis=0, tiled=True)
        all_grad = lax.all_gather(rows_grad, "g", axis=0, tiled=True)
    else:
        all_moe, all_grad = rows_moe, rows_grad
    block_count = numbers.shape[0]

    shared_gu = w_shared[:, : 2 * hidden_own]
    shared_dn = w_shared[:, 2 * hidden_own :]
    gate_vec = shared_gate_vec.astype(F32)
    small = jnp.concatenate([router_weight, shared_gate_vec[:, None]], 1)
    shared_in = jnp.dot(rows_moe, shared_gu, preferred_element_type=F32)
    shared_raw = jnp.dot(rows_grad, shared_dn, preferred_element_type=F32)
    logits_all = jnp.dot(all_moe, small, preferred_element_type=F32)
    router_all = jax.nn.softmax(logits_all[:, :experts], axis=-1)
    picks_here = jnp.arange(experts, dtype=jnp.int32)[None, :] == expert
    gate_all = jnp.sum(jnp.where(picks_here, router_all, 0.0), axis=-1)
    shared_gate = jax.nn.sigmoid(
        lax.dynamic_slice_in_dim(logits_all[:, experts], g * group_rows, group_rows, 0)
    )
    sh_gate, sh_up = shared_in[:, :hidden_own], shared_in[:, hidden_own:]
    shared_hidden = swish(sh_gate) * sh_up
    scaled_hidden = (shared_gate[:, None] * shared_hidden).astype(BF16)
    grad_hidden = shared_gate[:, None] * shared_raw
    signal_part = jnp.sum(shared_hidden * grad_hidden, axis=-1) * (1.0 - shared_gate)
    grad_shared_in = jnp.concatenate(swish_back(sh_gate, sh_up, grad_hidden), 1).astype(BF16)

    slot_here = jnp.max(jnp.where(numbers[:, 2 : 2 + top] == expert, numbers[:, 2 + top :], -1), 1)
    chosen = slot_here[:, None, :] == jnp.arange(capacity, dtype=jnp.int32)[None, :, None]
    place = chosen.astype(BF16)
    gate_blocks = gate_all.reshape(block_count, 1, blocks)
    gate_rows = jnp.sum(jnp.where(chosen, gate_blocks, 0.0), axis=-1).reshape(-1, 1)

    def to_rows(tokens):
        picked = jnp.einsum(
            "bst,btd->bsd",
            place,
            tokens.reshape(block_count, blocks, model),
            preferred_element_type=BF16,
        )
        return picked.reshape(block_count * capacity, model)

    expert_in = to_rows(all_moe)
    expert_grad = to_rows(all_grad)
    w_gate, w_up, w_down = expert_gate_up[0, 0], expert_gate_up[0, 1], expert_down[0]
    ex_gate = jnp.dot(expert_in, w_gate, preferred_element_type=F32)
    ex_up = jnp.dot(expert_in, w_up, preferred_element_type=F32)
    ex_raw = jnp.einsum("rd,fd->rf", expert_grad, w_down, preferred_element_type=F32)
    expert_hidden = swish(ex_gate) * ex_up
    scaled_expert = (gate_rows * expert_hidden).astype(BF16)
    gate_grad_rows = jnp.sum(expert_hidden * ex_raw, axis=-1)
    grad_ex_gate, grad_ex_up = swish_back(ex_gate, ex_up, gate_rows * ex_raw)
    grad_ex_gate, grad_ex_up = grad_ex_gate.astype(BF16), grad_ex_up.astype(BF16)
    grad_rows = jnp.einsum("rf,df->rd", grad_ex_gate, w_gate, preferred_element_type=F32)
    grad_rows = grad_rows + jnp.einsum("rf,df->rd", grad_ex_up, w_up, preferred_element_type=F32)
    grad_rows = grad_rows.astype(BF16).reshape(block_count, capacity, model)

    gate_grad = jnp.sum(
        jnp.where(chosen, gate_grad_rows.reshape(block_count, capacity, 1), 0.0), axis=1
    ).reshape(-1)
    signal_all = signal_part
    if groups > 1:
        signal_all = lax.dynamic_update_slice_in_dim(
            jnp.zeros((groups * group_rows,), F32), signal_part, g * group_rows, 0
        )
    signals = jnp.stack([gate_grad, signal_all]).reshape(2, -1, rows_here).transpose(1, 0, 2)
    signals = exchange(signals, EVERY).reshape(experts, 2, 2, rows_here)
    grad_router_probs = jnp.sum(signals[:, :, 0], axis=1).T
    gate_signal = jnp.sum(signals[:, :, 1], axis=(0, 1))

    def to_owners(hidden, weight, rows):
        if groups == 1:
            return scatter_group(combine(hidden, weight, place, rows))
        routed = jnp.einsum("bst,bsd->btd", place, rows, preferred_element_type=BF16)
        routed = lax.psum_scatter(
            routed.reshape(-1, model), "g", scatter_dimension=0, tiled=True
        )
        own = jnp.dot(hidden, weight, preferred_element_type=F32)
        return scatter_group((own + routed.astype(F32)).astype(BF16))

    grad_normed = to_owners(grad_shared_in, shared_gu.T, grad_rows)

    own_logits = jnp.dot(own_moe, router_weight, preferred_element_type=F32)
    router_probs = jax.nn.softmax(own_logits, axis=-1)
    grad_logits = router_probs * (
        grad_router_probs - jnp.sum(router_probs * grad_router_probs, axis=-1, keepdims=True)
    )
    grad_normed = (
        grad_normed
        + gate_signal[:, None] * gate_vec[None, :]
        + jnp.einsum("te,de->td", grad_logits, router_weight.astype(F32))
    )
    own_float = own_moe.astype(F32)
    grad_router = jnp.einsum("td,te->de", own_float, grad_logits)
    grad_gate_vec = jnp.sum(gate_signal[:, None] * own_float, axis=0)
    grad_gain_moe = jnp.sum(grad_normed * (middle * scale_moe), axis=0)
    grad_middle = cotangent.astype(F32) + norm_back(middle, scale_moe, gain_moe, grad_normed)
    grad_attn = grad_middle.astype(BF16)

    grad_attended = jnp.einsum("td,xdc->xtc", grad_attn, w_out, preferred_element_type=F32)
    grad_attended = grad_attended.astype(BF16).reshape(2, rows_here, 4, cols)
    grad_attended = grad_attended.transpose(0, 2, 1, 3).reshape(8, rows_here, cols)
    grad_attended = exchange(grad_attended, ("x", "y", "c")).reshape(2, 4, rows_here, cols)
    grad_attended = grad_attended.transpose(1, 0, 2, 3).reshape(plane_rows, cols)
    dq, dk, dv = attend_back(
        queries, keys, values, grad_attended, seg_q, seg_k, valid_k, cosine, sine
    )
    behind = [(k + 1, k) for k in range(LINE - 1)]
    sent = jnp.concatenate([dk[:plane_rows], dv[:plane_rows]], 1).astype(BF16)
    sent = lax.ppermute(sent, "z", behind).astype(F32)
    grad_projected = jnp.concatenate(
        [
            dq,
            (dk[plane_rows:] + sent[:, :cols]).astype(BF16),
            (dv[plane_rows:] + sent[:, cols:]).astype(BF16),
        ],
        1,
    )
    back_rows = jnp.einsum("tc,dc->td", grad_projected, w_qkv, preferred_element_type=F32)
    gain_sum = jnp.sum(back_rows * rows_attn.astype(F32), axis=0) / gain_attn
    back_own = scatter_plane(back_rows.astype(BF16))
    input_grad = grad_middle + norm_back(residual, scale_attn, gain_attn, back_own)
    bias_sum = jnp.sum(grad_projected.astype(F32), axis=0).reshape(3, cols)
    grad_bias = lax.dynamic_update_slice_in_dim(jnp.zeros((3, model), F32), bias_sum, here, 1)

    out_rows = jnp.dot(scaled_expert, w_down, preferred_element_type=F32)
    out_rows = out_rows.astype(BF16).reshape(block_count, capacity, model)
    moe_rows = to_owners(scaled_hidden, shared_dn.T, out_rows)
    output = (middle + moe_rows).astype(BF16)

    grad_egu = jnp.stack(
        [
            jnp.einsum("rd,rf->df", expert_in, grad, preferred_element_type=F32)
            for grad in (grad_ex_gate, grad_ex_up)
        ]
    )[None]
    grad_edown = jnp.einsum("rf,rd->fd", scaled_expert, expert_grad, preferred_element_type=F32)
    shared_grad = jnp.concatenate(
        [
            jnp.einsum("td,tf->df", rows_moe, grad_shared_in, preferred_element_type=F32),
            jnp.einsum("td,tf->df", rows_grad, scaled_hidden, preferred_element_type=F32),
        ],
        1,
    ).astype(BF16)
    if groups > 1:
        shared_grad = lax.psum_scatter(shared_grad, "g", scatter_dimension=0, tiled=True)
    shared_grad = exchange(shared_grad.reshape(in_group, weight_rows, 3 * hidden_own), GROUP)
    shared_grad = shared_grad.reshape(in_group, weight_rows, 3, hidden_own)
    shared_grad = shared_grad.transpose(2, 1, 0, 3).reshape(3, weight_rows, shared_cols)
    shared_grad = shared_grad.astype(F32)
    plane_grad = gather_plane(grad_attn)
    attn_grad = jnp.concatenate(
        [
            jnp.einsum("td,tc->dc", rows_attn, grad_projected, preferred_element_type=F32),
            jnp.einsum("td,tc->dc", plane_grad, attended, preferred_element_type=F32),
        ],
        1,
    ).astype(BF16)
    attn_grad = lax.psum_scatter(attn_grad, ("g", "z"), scatter_dimension=0, tiled=True)
    attn_grad = exchange(attn_grad.reshape(4, weight_rows, 4 * cols), ("y", "c"))
    attn_grad = attn_grad.reshape(4, weight_rows, 4, cols).astype(F32)
    attn_grad = attn_grad.transpose(2, 1, 0, 3).reshape(4, weight_rows, local_cols)

    valid_rows = lax.dynamic_slice_in_dim(valid_mask, x * rows_here, rows_here, 0).astype(F32)
    valid_rows = valid_rows[:, None]
    early = lax.psum(
        (
            grad_gain_moe,
            grad_router,
            grad_gate_vec,
            jnp.stack(
                [
                    jnp.sum(valid_rows * residual * residual),
                    jnp.sum(valid_rows * attn_rows * attn_rows),
                    jnp.sum(valid_rows),
                ]
            ),
        ),
        EVERY,
    )
    late = lax.psum((gain_sum, grad_bias, jnp.sum(valid_rows * moe_rows * moe_rows)), EVERY)
    valid_count = jnp.maximum(early[3][2], 1.0) * model
    return (
        output,
        input_grad,
        jnp.stack([late[0], early[0]]),
        attn_grad[:3],
        late[1],
        attn_grad[3].T,
        early[1],
        early[2],
        shared_grad[:2],
        shared_grad[2].T,
        grad_egu,
        grad_edown[None],
        jnp.sqrt(early[3][0] / valid_count),
        jnp.sqrt(early[3][1] / valid_count),
        jnp.sqrt(late[2] / valid_count),
    )


def solution(mesh):
    dp, mp = mesh.shape["dp"], mesh.shape["mp"]
    inner = Mesh(mesh.devices.reshape(dp // (4 * LINE), LINE, 2, 2, mp), EVERY)
    d = ("g",) + GROUP
    placed = (
        P(EVERY, None),
        P(EVERY, None),
        P(),
        P(None, d, "x"),
        P(),
        P("x", d),
        P(),
        P(),
        P(None, d, "x"),
        P("x", d),
        P(d, None, None, "x"),
        P(d, "x", None),
        P(d),
        P(d),
        P(d, None),
        P(d, None),
    )
    return jax.shard_map(
        per_device,
        mesh=inner,
        in_specs=placed,
        out_specs=(
            P(EVERY, None),
            P(EVERY, None),
            P(),
            P(None, d, "x"),
            P(),
            P("x", d),
            P(),
            P(),
            P(None, d, "x"),
            P("x", d),
            P(d, None, None, "x"),
            P(d, "x", None),
            P(),
            P(),
            P(),
        ),
        check_vma=False,
    )
```

time: 2480 us -> 1490 us (0.60)
  waiting for transfers between devices: 1640 us -> 378 us
  starting transfers between devices: 190 us -> 279 us
  blocking collectives: 62 us -> 143 us
  Pallas kernels: 0 us -> 77.9 us
  matrix products: 240 us -> 184 us
  other arithmetic: 141 us -> 189 us
    reduce_scatter x5 -> x1, waiting for transfers between devices: 942 us -> 0.01 us  [per_device(): lax.psum_scatter(attn_grad, ('g', 'z'), scatter_dimension=0, tiled=True)]
    all_to_all x4 -> x6, waiting for transfers between devices: 379 us -> 18.7 us  [exchange(): return lax.all_to_all(value, axes, split_axis=0, concat_axis=0, tiled=True)]
    ppermute x24 -> x128, waiting for transfers between devices: 65.5 us -> 359 us  [the longest x54 123 us: swap(): return lax.ppermute(value, axis, SWAP)]
    ppermute x24 -> x128, starting transfers between devices: 89.4 us -> 248 us  [the longest x18 107 us: line_scatter(): rising = lax.ppermute(going_up, axis, up[:step])]
    all_gather x8 -> x2, waiting for transfers between devices: 138 us -> 0.01 us  [the longest x1 0.01 us: per_device(): w_qkv = lax.all_gather(w_qkv, ('g', 'z'), axis=0, tiled=True)]
    psum x1, waiting for transfers between devices: 110 us -> 0.01 us  [per_device(): lax.psum((grad_gain_moe, grad_router, grad_gate_vec, jnp.stack([jnp.sum(v...]
    all_gather x0 -> x1, blocking collectives: none -> 84.6 us  [per_device(): numbers = lax.all_gather(numbers, ('g',) + GROUP, axis=0)]
    pallas_call x0 -> x5, Pallas kernels: none -> 77.9 us  [the longest x2 41.7 us: combine(): pl.pallas_call(combine_kernel, grid=(blocks,), in_specs=[pl.BlockSpec((st...]
  transfers between devices with their start and end apart: 42 -> 138, of which waited for: 19 -> 48; matrix products, arithmetic and copies ran while one was open for 18% -> 28% of each run, Pallas kernels for 0% -> 4%
where the time goes in v1:
time: 1490 us; the launch traced here: 1480 us
  waiting for transfers between devices  378 us (25%)
  starting transfers between devices  279 us (19%)
  local copies, waits for them, and re-layouts  204 us (14%)
  other arithmetic  189 us (13%)
  matrix products  184 us (12%)
  blocking collectives  143 us (10%)
  Pallas kernels  77.9 us (5%)
  between operations  23.5 us (2%)
    ppermute x54, waiting for transfers between devices, swap(): return lax.ppermute(value, axis, SWAP)  123 us
    ppermute x18, starting transfers between devices, line_scatter(): rising = lax.ppermute(going_up, axis, up[:step])  107 us
    ppermute x18, waiting for transfers between devices, line_gather(): falling = lax.ppermute(falling, axis, down[:LINE - step])  90.4 us
    all_gather x1, blocking collectives, per_device(): numbers = lax.all_gather(numbers, ('g',) + GROUP, axis=0)  84.6 us
    ppermute x18, waiting for transfers between devices, line_scatter(): rising = lax.ppermute(going_up, axis, up[:step])  65.8 us
    ppermute x18, starting transfers between devices, line_gather(): rising = lax.ppermute(rising, axis, up[step - 1:])  49.9 us
    ppermute x54, starting transfers between devices, swap(): return lax.ppermute(value, axis, SWAP)  46.1 us
    psum x1, blocking collectives, per_device(): lax.psum((grad_gain_moe, grad_router, grad_gate_vec, jnp.stack([jnp.sum(v...  42.5 us
  transfers between devices with their start and end apart: 138, of which 48 were waited for; matrix products, arithmetic and copies ran while one was open for 28% of the time, Pallas kernels for 4%

profile of v1, /device:TPU:0, one launch (start us, length us, event | category | flops | bytes accessed | tf_op | source)
XLA Modules:
  0.0 1478.3 jit_solution(5463279690289774534)
XLA Ops:
  10.9 15.8 %all_to_all.35 = bf16[4,128,768]{1,2,0:T(8,128)(2,1)} all-to-all(bf16[4,128,768]{1,2,0:T(8,128)(2,1)S(1)} %bitcast.700), channel_id=1, replica_groups=mesh['g'=1,'z'=4,'y'=2,'c'=2,'x'=2] {'y','c'}, dimensions={0} | all-to-all | bytes 1572864 | tf_op jit(solution)/shard_map/all_to_all | solution.py:172
  62.2 84.6 %all-gather.1 = s32[16,10,256]{2,1,0:T(8,128)S(1)} all-gather(s32[1,10,256]{2,1,0:T(8,128)S(1)} %add_bitcast_fusion), channel_id=2, replica_groups=mesh['g'=1,'z'=4,'y'=2,'c'=2,'x'=2] {'g','z','y','c'}, dimensions={0}, use_global_device_ids=true | all-gather | bytes 174080 | tf_op jit(solution)/shard_map/all_gather | solution.py:457
  205.7 15.3 %collective-permute-done.66 = bf16[2,2,32,2048]{3,2,1,0:T(8,128)(2,1)S(1)} collective-permute-done((bf16[2,2,32,2048]{3,2,1,0:T(8,128)(2,1)S(1)}, bf16[2,2,32,2048]{3,2,1,0:T(8,128)(2,1)S(1)}, u32[]{:S(2)}, u32[]{:S(2)}) %collective-permute-start.66) | collective-permute-done | bytes 524320 | tf_op jit(solution)/shard_map/ppermute | solution.py:48
  222.6 11.3 collective-permute-done.74
  238.1 16.3 %collective-permute-done.75 = bf16[2,48,2048]{2,1,0:T(8,128)(2,1)S(1)} collective-permute-done((bf16[2,48,2048]{2,1,0:T(8,128)(2,1)S(1)}, bf16[2,48,2048]{2,1,0:T(8,128)(2,1)S(1)}, u32[]{:S(2)}, u32[]{:S(2)}) %collective-permute-start.75) | collective-permute-done | bytes 393248 | tf_op jit(solution)/shard_map/ppermute | solution.py:48
  287.8 14.0 collective-permute-done.86
  332.2 17.4 %collective-permute-done.6 = bf16[1024,512]{1,0:T(8,128)(2,1)} collective-permute-done((bf16[1024,512]{1,0:T(8,128)(2,1)}, bf16[1024,512]{1,0:T(8,128)(2,1)}, u32[]{:S(2)}, u32[]{:S(2)}) %collective-permute-start.6) | collective-permute-done | bytes 1048608 | tf_op jit(solution)/shard_map/ppermute | solution.py:491
  380.3 11.9 copy.134
  412.4 11.0 collective-permute-start.26
  514.3 11.1 collective-permute-done.32
  535.2 11.2 fusion.45
  546.4 20.8 %copy.163 = bf16[4096,2048]{0,1:T(8,128)(2,1)} copy(bf16[4096,2048]{1,0:T(8,128)(2,1)} %bitcast.644) | data formatting | bytes 33554432 | tf_op jit(solution)/shard_map/reshape | solution.py:114
  636.5 12.3 fusion.54
  675.5 11.7 fusion.24
  687.1 13.9 multiply_reduce_fusion.2
  713.8 22.3 %combine.3 = bf16[4096,2048]{1,0:T(8,128)(2,1)} custom-call(bf16[4096,352]{1,0:T(8,128)(2,1)} %pad_maximum_fusion.5.hidden_ref, bf16[352,2048]{1,0:T(8,128)(2,1)} %slice_bitcast_fusion.weight_ref, bf16[16,96,256]{2,1,0:T(8,128)(2,1)} %fusion.47.place_ref, bf16[16,96,2048]{2,1,0:T(8,128)(2,1)} %bitcast.680), custom_call_target="tpu_custom_call" | custom-call | flops 7516192768 | bytes 25952256 | tf_op jit(solution)/shard_map/combine/pallas_call | solution.py:367
  775.2 19.4 %combine.2 = bf16[4096,2048]{1,0:T(8,128)(2,1)} custom-call(bf16[4096,176]{1,0:T(8,128)(2,1)} %get-tuple-element.99.hidden_ref, bf16[176,2048]{1,0:T(8,128)(2,1)} %slice_bitcast_fusion.1.weight_ref, bf16[16,96,256]{2,1,0:T(8,128)(2,1)} %fusion.47.place_ref, bf16[16,96,2048]{2,1,0:T(8,128)(2,1)} %bitcast.681), custom_call_target="tpu_custom_call" | custom-call | flops 4563402752 | bytes 24510464 | tf_op jit(solution)/shard_map/combine/pallas_call | solution.py:367
  836.8 20.7 %copy.162 = bf16[4096,2048]{0,1:T(8,128)(2,1)} copy(bf16[4096,2048]{1,0:T(8,128)(2,1)} %bitcast.639) | data formatting | bytes 33554432 | tf_op jit(solution)/shard_map/reshape | solution.py:114
  876.6 18.4 %collective-permute-done.94 = bf16[2,2,32,2048]{3,2,1,0:T(8,128)(2,1)S(1)} collective-permute-done((bf16[2,2,32,2048]{3,2,1,0:T(8,128)(2,1)S(1)}, bf16[2,2,32,2048]{3,2,1,0:T(8,128)(2,1)S(1)}, u32[]{:S(2)}, u32[]{:S(2)}) %collective-permute-start.94) | collective-permute-done | bytes 524320 | tf_op jit(solution)/shard_map/ppermute | solution.py:88
  897.6 13.6 collective-permute-done.95
  914.1 22.1 %collective-permute-done.96 = bf16[32,2048]{1,0:T(8,128)(2,1)S(1)} collective-permute-done((bf16[32,2048]{1,0:T(8,128)(2,1)S(1)}, bf16[32,2048]{1,0:T(8,128)(2,1)S(1)}, u32[]{:S(2)}, u32[]{:S(2)}) %collective-permute-start.96) | collective-permute-done | bytes 131104 | tf_op jit(solution)/shard_map/ppermute | solution.py:31
  974.5 16.8 %collective-permute-start.111 = (bf16[48,2048]{1,0:T(8,128)(2,1)S(1)}, bf16[48,2048]{1,0:T(8,128)(2,1)S(1)}, u32[]{:S(2)}, u32[]{:S(2)}) collective-permute-start(bf16[48,2048]{1,0:T(8,128)(2,1)S(1)} %get-tuple-element.170), channel_id=1, source_target_pairs={{0,8},{8,16},{16,24},{1,9},{9,17},{17,25},{2,10},{10,18},{18,26},{... | collective-permute-start | bytes 589832 | tf_op jit(solution)/shard_map/ppermute | solution.py:87
  1022.6 17.5 %attend_back.1 = (bf16[1024,256]{1,0:T(8,128)(2,1)}, f32[2048,256]{1,0:T(8,128)}, f32[2048,256]{1,0:T(8,128)}) custom-call(bf16[1024,256]{1,0:T(8,128)(2,1)} %slice.262.q_ref, bf16[2048,256]{1,0:T(8,128)(2,1)} %get-tuple-element.127.k_ref, bf16[2048,256]{1,0:T(8,128)(2,1)} %get-tuple-element.126.v_ref, bf16[1024,256]{1,0:T(8,128)(2,1)} %bitcast.738, ...), custom_call_target="tpu_custom_call" | custom-call | flops 3355443200 | bytes 12582912 | tf_op jit(solution)/shard_map/attend_back/pallas_call | solution.py:327
  1049.8 21.4 %collective-permute-done.115 = bf16[1024,512]{1,0:T(8,128)(2,1)S(1)} collective-permute-done((bf16[1024,512]{1,0:T(8,128)(2,1)S(1)}, bf16[1024,512]{1,0:T(8,128)(2,1)S(1)}, u32[]{:S(2)}, u32[]{:S(2)}) %collective-permute-start.115) | collective-permute-done | bytes 1048608 | tf_op jit(solution)/shard_map/ppermute | solution.py:621
  1175.7 38.7 %collective-permute-done.36 = bf16[2,2,32,2048]{3,2,1,0:T(8,128)(2,1)} collective-permute-done((bf16[2,2,32,2048]{3,2,1,0:T(8,128)(2,1)S(1)}, bf16[2,2,32,2048]{3,2,1,0:T(8,128)(2,1)}, u32[]{:S(2)}, u32[]{:S(2)}) %collective-permute-start.36) | collective-permute-done | bytes 524320 | tf_op jit(solution)/shard_map/ppermute | solution.py:87
  1236.6 15.0 %collective-permute-done.40 = bf16[2,2,32,2048]{3,2,1,0:T(8,128)(2,1)S(1)} collective-permute-done((bf16[2,2,32,2048]{3,2,1,0:T(8,128)(2,1)S(1)}, bf16[2,2,32,2048]{3,2,1,0:T(8,128)(2,1)S(1)}, u32[]{:S(2)}, u32[]{:S(2)}) %collective-permute-start.40) | collective-permute-done | bytes 524320 | tf_op jit(solution)/shard_map/ppermute | solution.py:88
  1261.7 14.3 collective-permute-done.41
  1284.2 11.8 collective-permute-start.45
  1298.5 12.5 collective-permute-start.55
  1331.7 13.4 collective-permute-start.57
  1389.7 42.5 %all-reduce.1 = (f32[1,2048]{1,0:T(1,128)S(1)}, f32[1,2048]{1,0:T(1,128)S(1)}, f32[3,2048]{1,0:T(4,128)}, f32[2048]{0:T(1024)}, f32[3]{0:T(128)S(1)}, /*index=5*/f32[]{:T(128)}) all-reduce(f32[1,2048]{1,0:T(1,128)S(1)} %bitcast.758, ...), channel_id=1, replica_groups=mesh['g'=1,'z'=4,'y'=2,'c'=2,'x'=2] {'g','z','y','c','x'}, use_global_device_ids=true, to_apply=%region_20.21 | all-reduce | flops 12292 | bytes 98336 | tf_op jit(solution)/shard_map/psum | solution.py:677
  1445.8 11.5 all-to-all-done.5
  (797 shorter events, 844.3 us)
Async XLA Ops:
  7.2 307.4 %all-gather.5.cloned.1.call-start = ((), (), s32[]{:S(2)}) async-start(), calls=%async_computation.8 | async-start | bytes 3932160 | tf_op jit(solution)/shard_map/all_gather | solution.py:470
  29.0 351.2 %all-gather.7.cloned.1.call-start = ((), (), s32[]{:S(2)}) async-start(), calls=%async_computation.9 | async-start | bytes 8650752 | tf_op jit(solution)/shard_map/all_gather | solution.py:471
  30.7 134.0 %collective-permute-start.82 = (bf16[48,2048]{1,0:T(8,128)(2,1)}, bf16[48,2048]{1,0:T(8,128)(2,1)}, u32[]{:S(2)}, u32[]{:S(2)}) collective-permute-start(bf16[48,2048]{1,0:T(8,128)(2,1)} %slice.227), channel_id=1, source_target_pairs={{8,0},{16,8},{24,16},{9,1},{17,9},{25,17},{10,2},{18,10},{26,18},{... | collective-permute-start | bytes 589832 | tf_op jit(solution)/shard_map/ppermute | solution.py:48
  32.0 134.0 %collective-permute-start.79 = (bf16[48,2048]{1,0:T(8,128)(2,1)}, bf16[48,2048]{1,0:T(8,128)(2,1)}, u32[]{:S(2)}, u32[]{:S(2)}) collective-permute-start(bf16[48,2048]{1,0:T(8,128)(2,1)} %slice.227), channel_id=1, source_target_pairs={{0,8},{8,16},{16,24},{1,9},{9,17},{17,25},{2,10},{10,18},{18,26},{... | collective-permute-start | bytes 589832 | tf_op jit(solution)/shard_map/ppermute | solution.py:47
  39.1 124.0 %collective-permute-start.61 = (bf16[32,2048]{1,0:T(8,128)(2,1)}, bf16[32,2048]{1,0:T(8,128)(2,1)S(1)}, u32[]{:S(2)}, u32[]{:S(2)}) collective-permute-start(bf16[32,2048]{1,0:T(8,128)(2,1)} %get-tuple-element.196), channel_id=1, source_target_pairs={{0,1},{1,0},{2,3},{3,2},{4,5},{5,4},{6,7},{7,6},{8,9},{9,8},{10,11... | collective-permute-start | bytes 393224 | tf_op jit(solution)/shard_map/ppermute | solution.py:31
  44.1 124.3 %collective-permute-start.3 = (bf16[64,2048]{1,0:T(8,128)(2,1)}, bf16[64,2048]{1,0:T(8,128)(2,1)}, u32[]{:S(2)}, u32[]{:S(2)}) collective-permute-start(bf16[64,2048]{1,0:T(8,128)(2,1)} %get-tuple-element.208), channel_id=1, source_target_pairs={{0,4},{4,0},{1,5},{5,1},{2,6},{6,2},{3,7},{7,3},{8,12},{12,8},{9,1... | collective-permute-start | bytes 786440 | tf_op jit(solution)/shard_map/ppermute | solution.py:31
  44.5 122.3 %collective-permute-start = (bf16[64,2048]{1,0:T(8,128)(2,1)}, bf16[64,2048]{1,0:T(8,128)(2,1)}, u32[]{:S(2)}, u32[]{:S(2)}) collective-permute-start(bf16[64,2048]{1,0:T(8,128)(2,1)} %get-tuple-element.209), channel_id=1, source_target_pairs={{0,1},{1,0},{2,3},{3,2},{4,5},{5,4},{6,7},{7,6},{8,9},{9,8},{10,11... | collective-permute-start | bytes 786440 | tf_op jit(solution)/shard_map/ppermute | solution.py:31
  53.3 273.9 %all-to-all-start.2 = ((bf16[16,128,528]{1,2,0:T(8,128)(2,1)}), bf16[16,128,528]{1,2,0:T(8,128)(2,1)}, u32[]{:S(2)}, u32[]{:S(2)}) async-start(bf16[16,128,528]{1,2,0:T(8,128)(2,1)} %maximum_bitcast_fusion.1), calls=%async_computation.2 | async-start | bytes 4325376 | tf_op jit(solution)/shard_map/all_to_all | solution.py:172
  196.3 60.4 %collective-permute-start.5 = (bf16[2,2,64,2048]{3,2,1,0:T(8,128)(2,1)S(1)}, bf16[2,2,64,2048]{3,2,1,0:T(8,128)(2,1)S(1)}, u32[]{:S(2)}, u32[]{:S(2)}) collective-permute-start(bf16[2,2,64,2048]{3,2,1,0:T(8,128)(2,1)S(1)} %maximum_select_fusion.25), channel_id=1, source_target_pairs={{0,2},{2,0},{1,3},{3,1},{4,6},{6,4},{5,7},{7,5},{8,10},{10,8},{9,1... | collective-permute-start | bytes 3145736 | tf_op jit(solution)/shard_map/ppermute | solution.py:31
  287.8 120.6 %collective-permute-start.69 = (bf16[4,2,2,32,2048]{4,3,2,1,0:T(8,128)(2,1)}, bf16[4,2,2,32,2048]{4,3,2,1,0:T(8,128)(2,1)}, u32[]{:S(2)}, u32[]{:S(2)}) collective-permute-start(bf16[4,2,2,32,2048]{4,3,2,1,0:T(8,128)(2,1)} %get-tuple-element.123), channel_id=1, source_target_pairs={{0,2},{2,0},{1,3},{3,1},{4,6},{6,4},{5,7},{7,5},{8,10},{10,8},{9,1... | collective-permute-start | bytes 6291464 | tf_op jit(solution)/shard_map/ppermute | solution.py:31
  303.6 152.9 %collective-permute-start.87 = (bf16[2,2,4,48,2048]{4,3,2,1,0:T(8,128)(2,1)}, bf16[2,2,4,48,2048]{4,3,2,1,0:T(8,128)(2,1)}, u32[]{:S(2)}, u32[]{:S(2)}) collective-permute-start(bf16[2,2,4,48,2048]{4,3,2,1,0:T(8,128)(2,1)} %maximum_select_fusion.13), channel_id=1, source_target_pairs={{0,2},{2,0},{1,3},{3,1},{4,6},{6,4},{5,7},{7,5},{8,10},{10,8},{9,1... | collective-permute-start | bytes 9437192 | tf_op jit(solution)/shard_map/ppermute | solution.py:31
  312.7 149.1 %collective-permute-start.78 = (bf16[2,4,2,48,2048]{4,3,2,1,0:T(8,128)(2,1)}, bf16[2,4,2,48,2048]{4,3,2,1,0:T(8,128)(2,1)}, u32[]{:S(2)}, u32[]{:S(2)}) collective-permute-start(bf16[2,4,2,48,2048]{4,3,2,1,0:T(8,128)(2,1)} %maximum_select_fusion.11), channel_id=1, source_target_pairs={{0,2},{2,0},{1,3},{3,1},{4,6},{6,4},{5,7},{7,5},{8,10},{10,8},{9,1... | collective-permute-start | bytes 9437192 | tf_op jit(solution)/shard_map/ppermute | solution.py:31
  514.2 60.3 %collective-permute-start.15 = (bf16[4,2,2,32,2048]{4,3,2,1,0:T(8,128)(2,1)}, bf16[4,2,2,32,2048]{4,3,2,1,0:T(8,128)(2,1)}, u32[]{:S(2)}, u32[]{:S(2)}) collective-permute-start(bf16[4,2,2,32,2048]{4,3,2,1,0:T(8,128)(2,1)} %get-tuple-element.125), channel_id=1, source_target_pairs={{0,2},{2,0},{1,3},{3,1},{4,6},{6,4},{5,7},{7,5},{8,10},{10,8},{9,1... | collective-permute-start | bytes 6291464 | tf_op jit(solution)/shard_map/ppermute | solution.py:31
  527.5 52.9 %collective-permute-start.33 = (bf16[2,2,4,48,2048]{4,3,2,1,0:T(8,128)(2,1)}, bf16[2,2,4,48,2048]{4,3,2,1,0:T(8,128)(2,1)}, u32[]{:S(2)}, u32[]{:S(2)}) collective-permute-start(bf16[2,2,4,48,2048]{4,3,2,1,0:T(8,128)(2,1)} %maximum_select_fusion.9), channel_id=1, source_target_pairs={{0,2},{2,0},{1,3},{3,1},{4,6},{6,4},{5,7},{7,5},{8,10},{10,8},{9,1... | collective-permute-start | bytes 9437192 | tf_op jit(solution)/shard_map/ppermute | solution.py:31
  535.2 50.3 %collective-permute-start.24 = (bf16[2,4,2,48,2048]{4,3,2,1,0:T(8,128)(2,1)}, bf16[2,4,2,48,2048]{4,3,2,1,0:T(8,128)(2,1)}, u32[]{:S(2)}, u32[]{:S(2)}) collective-permute-start(bf16[2,4,2,48,2048]{4,3,2,1,0:T(8,128)(2,1)} %maximum_select_fusion.7), channel_id=1, source_target_pairs={{0,2},{2,0},{1,3},{3,1},{4,6},{6,4},{5,7},{7,5},{8,10},{10,8},{9,1... | collective-permute-start | bytes 9437192 | tf_op jit(solution)/shard_map/ppermute | solution.py:31
  752.3 109.1 %all-to-all-start.3 = ((f32[32,2,128]{2,1,0:T(2,128)}), f32[32,2,128]{2,1,0:T(2,128)S(1)}, u32[]{:S(2)}, u32[]{:S(2)}) async-start(f32[32,2,128]{2,1,0:T(2,128)} %maximum_bitcast_fusion.2), calls=%async_computation.3 | async-start | bytes 65536 | tf_op jit(solution)/shard_map/all_to_all | solution.py:172
  762.5 41.5 %collective-permute-start.88 = (bf16[4,2,2,32,2048]{4,3,2,1,0:T(8,128)(2,1)S(1)}, bf16[4,2,2,32,2048]{4,3,2,1,0:T(8,128)(2,1)S(1)}, u32[]{:S(2)}, u32[]{:S(2)}) collective-permute-start(bf16[4,2,2,32,2048]{4,3,2,1,0:T(8,128)(2,1)S(1)} %dynamic-slice_bitcast_fusion), channel_id=1, source_target_pairs={{0,2},{2,0},{1,3},{3,1},{4,6},{6,4},{5,7},{7,5},{8,10},{10,8},{9,1... | collective-permute-start | bytes 6291464 | tf_op jit(solution)/shard_map/ppermute | solution.py:31
  774.7 96.2 %collective-permute-start.97 = (bf16[4,2,2,48,2048]{4,3,1,0,2:T(8,128)(2,1)}, bf16[4,2,2,48,2048]{4,3,1,0,2:T(8,128)(2,1)}, u32[]{:S(2)}, u32[]{:S(2)}) collective-permute-start(bf16[4,2,2,48,2048]{4,3,1,0,2:T(8,128)(2,1)} %bitcast.633), channel_id=1, source_target_pairs={{0,2},{2,0},{1,3},{3,1},{4,6},{6,4},{5,7},{7,5},{8,10},{10,8},{9,1... | collective-permute-start | bytes 9437192 | tf_op jit(solution)/shard_map/ppermute | solution.py:31
  774.8 90.3 %collective-permute-start.106 = (bf16[4,2,2,48,2048]{4,3,0,2,1:T(8,128)(2,1)}, bf16[4,2,2,48,2048]{4,3,0,2,1:T(8,128)(2,1)}, u32[]{:S(2)}, u32[]{:S(2)}) collective-permute-start(bf16[4,2,2,48,2048]{4,3,0,2,1:T(8,128)(2,1)} %bitcast.632), channel_id=1, source_target_pairs={{0,2},{2,0},{1,3},{3,1},{4,6},{6,4},{5,7},{7,5},{8,10},{10,8},{9,1... | collective-permute-start | bytes 9437192 | tf_op jit(solution)/shard_map/ppermute | solution.py:31
  814.2 47.3 %collective-permute-start.92 = (bf16[2,2,32,2048]{3,2,1,0:T(8,128)(2,1)}, bf16[2,2,32,2048]{3,2,1,0:T(8,128)(2,1)S(1)}, u32[]{:S(2)}, u32[]{:S(2)}) collective-permute-start(bf16[2,2,32,2048]{3,2,1,0:T(8,128)(2,1)} %get-tuple-element.117), channel_id=1, source_target_pairs={{24,16},{25,17},{26,18},{27,19},{28,20},{29,21},{30,22},{31,23}} | collective-permute-start | bytes 1572872 | tf_op jit(solution)/shard_map/ppermute | solution.py:88
  821.1 41.0 %collective-permute-start.90 = (bf16[2,2,32,2048]{3,2,1,0:T(8,128)(2,1)S(1)}, bf16[2,2,32,2048]{3,2,1,0:T(8,128)(2,1)}, u32[]{:S(2)}, u32[]{:S(2)}) collective-permute-start(bf16[2,2,32,2048]{3,2,1,0:T(8,128)(2,1)S(1)} %fusion.74), channel_id=1, source_target_pairs={{0,8},{8,16},{1,9},{9,17},{2,10},{10,18},{3,11},{11,19},{4,12},{12... | collective-permute-start | bytes 1572872 | tf_op jit(solution)/shard_map/ppermute | solution.py:87
  857.4 269.2 %collective-permute-start.34 = (bf16[4,2,2,32,2048]{4,3,2,1,0:T(8,128)(2,1)}, bf16[4,2,2,32,2048]{4,3,2,1,0:T(8,128)(2,1)}, u32[]{:S(2)}, u32[]{:S(2)}) collective-permute-start(bf16[4,2,2,32,2048]{4,3,2,1,0:T(8,128)(2,1)} %dynamic-slice_bitcast_fusion.1), channel_id=1, source_target_pairs={{0,2},{2,0},{1,3},{3,1},{4,6},{6,4},{5,7},{7,5},{8,10},{10,8},{9,1... | collective-permute-start | bytes 6291464 | tf_op jit(solution)/shard_map/ppermute | solution.py:31
  861.5 360.0 %collective-permute-start.43 = (bf16[4,2,2,48,2048]{4,3,1,0,2:T(8,128)(2,1)}, bf16[4,2,2,48,2048]{4,3,1,0,2:T(8,128)(2,1)}, u32[]{:S(2)}, u32[]{:S(2)}) collective-permute-start(bf16[4,2,2,48,2048]{4,3,1,0,2:T(8,128)(2,1)} %bitcast.698), channel_id=1, source_target_pairs={{0,2},{2,0},{1,3},{3,1},{4,6},{6,4},{5,7},{7,5},{8,10},{10,8},{9,1... | collective-permute-start | bytes 9437192 | tf_op jit(solution)/shard_map/ppermute | solution.py:31
  869.3 43.5 %collective-permute-start.107 = (bf16[4,2,48,2048]{3,2,0,1:T(8,128)(2,1)S(1)}, bf16[4,2,48,2048]{3,2,0,1:T(8,128)(2,1)S(1)}, u32[]{:S(2)}, u32[]{:S(2)}) collective-permute-start(bf16[4,2,48,2048]{3,2,0,1:T(8,128)(2,1)S(1)} %dynamic-slice_bitcast_fusion.2), channel_id=1, source_target_pairs={{0,4},{4,0},{1,5},{5,1},{2,6},{6,2},{3,7},{7,3},{8,12},{12,8},{9,1... | collective-permute-start | bytes 4718600 | tf_op jit(solution)/shard_map/ppermute | solution.py:31
  896.0 40.2 %collective-permute-start.98 = (bf16[4,2,48,2048]{3,2,1,0:T(8,128)(2,1)S(1)}, bf16[4,2,48,2048]{3,2,1,0:T(8,128)(2,1)S(1)}, u32[]{:S(2)}, u32[]{:S(2)}) collective-permute-start(bf16[4,2,48,2048]{3,2,1,0:T(8,128)(2,1)S(1)} %dynamic-slice_bitcast_fusion.3), channel_id=1, source_target_pairs={{0,1},{1,0},{2,3},{3,2},{4,5},{5,4},{6,7},{7,6},{8,9},{9,8},{10,11... | collective-permute-start | bytes 4718600 | tf_op jit(solution)/shard_map/ppermute | solution.py:31
  1011.4 424.8 %reduce-scatter.2.cloned.1.call-start = ((), (), s32[]{:S(2)}) async-start(), calls=%async_computation.10 | async-start | bytes 5242880 | tf_op jit(solution)/shard_map/reduce_scatter | solution.py:670
  1137.5 116.0 %all-to-all-start.6 = ((bf16[16,128,528]{1,2,0:T(8,128)(2,1)}), bf16[16,128,528]{1,2,0:T(8,128)(2,1)}, u32[]{:S(2)}, u32[]{:S(2)}) async-start(bf16[16,128,528]{1,2,0:T(8,128)(2,1)} %pad_maximum_fusion.6), calls=%async_computation.7 | async-start | bytes 4325376 | tf_op jit(solution)/shard_map/all_to_all | solution.py:172
  1141.9 324.6 %all-reduce.4.cloned.1.call-start = ((), (), s32[]{:S(2)}) async-start(), calls=%async_computation.11 | async-start | bytes 262144 | tf_op jit(solution)/shard_map/psum | solution.py:677
  1149.5 80.5 %collective-permute-start.52 = (bf16[4,2,2,48,2048]{4,3,0,2,1:T(8,128)(2,1)}, bf16[4,2,2,48,2048]{4,3,0,2,1:T(8,128)(2,1)}, u32[]{:S(2)}, u32[]{:S(2)}) collective-permute-start(bf16[4,2,2,48,2048]{4,3,0,2,1:T(8,128)(2,1)} %bitcast.634), channel_id=1, source_target_pairs={{0,2},{2,0},{1,3},{3,1},{4,6},{6,4},{5,7},{7,5},{8,10},{10,8},{9,1... | collective-permute-start | bytes 9437192 | tf_op jit(solution)/shard_map/ppermute | solution.py:31
  1160.5 53.9 %collective-permute-start.36 = (bf16[2,2,32,2048]{3,2,1,0:T(8,128)(2,1)S(1)}, bf16[2,2,32,2048]{3,2,1,0:T(8,128)(2,1)}, u32[]{:S(2)}, u32[]{:S(2)}) collective-permute-start(bf16[2,2,32,2048]{3,2,1,0:T(8,128)(2,1)S(1)} %fusion.80), channel_id=1, source_target_pairs={{0,8},{8,16},{1,9},{9,17},{2,10},{10,18},{3,11},{11,19},{4,12},{12... | collective-permute-start | bytes 1572872 | tf_op jit(solution)/shard_map/ppermute | solution.py:87
  1226.3 55.8 %collective-permute-start.44 = (bf16[4,2,48,2048]{3,2,1,0:T(8,128)(2,1)}, bf16[4,2,48,2048]{3,2,1,0:T(8,128)(2,1)}, u32[]{:S(2)}, u32[]{:S(2)}) collective-permute-start(bf16[4,2,48,2048]{3,2,1,0:T(8,128)(2,1)} %dynamic-slice_bitcast_fusion.5), channel_id=1, source_target_pairs={{0,1},{1,0},{2,3},{3,2},{4,5},{5,4},{6,7},{7,6},{8,9},{9,8},{10,11... | collective-permute-start | bytes 4718600 | tf_op jit(solution)/shard_map/ppermute | solution.py:31
  1234.6 43.1 %collective-permute-start.53 = (bf16[4,2,48,2048]{3,2,0,1:T(8,128)(2,1)}, bf16[4,2,48,2048]{3,2,0,1:T(8,128)(2,1)}, u32[]{:S(2)}, u32[]{:S(2)}) collective-permute-start(bf16[4,2,48,2048]{3,2,0,1:T(8,128)(2,1)} %dynamic-slice_bitcast_fusion.4), channel_id=1, source_target_pairs={{0,4},{4,0},{1,5},{5,1},{2,6},{6,2},{3,7},{7,3},{8,12},{12,8},{9,1... | collective-permute-start | bytes 4718600 | tf_op jit(solution)/shard_map/ppermute | solution.py:31
  (228 other events, 4263.4 us)
Sparse Core Ops, SparseCore 0:
  29.2 102.3 all-gather.4
  134.4 122.2 all-gather.6
  1084.5 95.2 reduce-scatter.1
  1186.7 130.7 all-reduce.3

commit v2 on v1

v2 whole, which is shorter than its diff:
```python
import functools

import jax
import jax.numpy as jnp
from jax import lax
from jax.experimental import pallas as pl
from jax.experimental.pallas import tpu as pltpu
from jax.sharding import Mesh
from jax.sharding import PartitionSpec as P

HEAD = 128
SEQ = 4096
WINDOW = 1024

EPSILON = 1e-06
ROPE_BASE = 1000000.0
MASKED = -1e30

LINE = 4
OFFSETS = (0, 2, 1, 3)
GROUP = ("z", "y", "c")
EVERY = ("g", "z", "y", "c", "x")
SWAP = [(0, 1), (1, 0)]
VMEM_LIMIT = 56 * 1024 * 1024

F32 = jnp.float32
BF16 = jnp.bfloat16


def swap(value, axis):
    return lax.ppermute(value, axis, SWAP)


def cross(value, offset):
    return lax.ppermute(value, "z", [(k, k ^ offset) for k in range(LINE)])


def take(value, index, dim):
    return lax.dynamic_index_in_dim(value, index, dim, keepdims=False)


def split(value, index, dim):
    return take(value, index, dim), take(value, 1 - index, dim)


def stage(kernel, after, inputs, outputs, name):
    count, _, width = inputs[0].shape
    part = width // 4

    def spec(rows):
        return pl.BlockSpec((1, rows, part), lambda i, j: (i, 0, j))

    return pl.pallas_call(
        kernel,
        grid=(count, 4),
        in_specs=[pl.BlockSpec(memory_space=pltpu.SMEM)] + [spec(v.shape[1]) for v in inputs],
        out_specs=[spec(rows) for rows, _ in outputs],
        out_shape=[jax.ShapeDtypeStruct((count, rows, width), kind) for rows, kind in outputs],
        compiler_params=pltpu.CompilerParams(vmem_limit_bytes=VMEM_LIMIT),
        name=name,
    )(after.reshape(1), *inputs)


def pair_kernel(after_ref, first, first_x, second, second_y, out_first, out_second):
    half = first.shape[1]
    out_first[0, :half] = first[0]
    out_first[0, half:] = first_x[0]
    out_second[0, :half] = second[0]
    out_second[0, half:] = second_y[0]


def plane_kernel(after_ref, first, first_y, second, second_x, out):
    rows = first.shape[1]
    half = rows // 2
    for y, source in enumerate((first, first_y)):
        out[0, 2 * y * rows : (2 * y + 1) * rows] = source[0]
    for x, source in enumerate((second, second_x)):
        for y in range(2):
            start = (2 * y + 1) * rows + x * half
            out[0, start : start + half] = source[0, y * half : (y + 1) * half]


def slot_gather(shards, after_pair, after_plane):
    rows = shards.shape[1]
    half = rows // 2
    first, second = shards[:, :half], shards[:, half:]
    first, second = stage(
        pair_kernel,
        after_pair,
        [first, swap(first, "x"), second, swap(second, "y")],
        [(rows, BF16)] * 2,
        "pair",
    )
    (own,) = stage(
        plane_kernel,
        after_plane,
        [first, swap(first, "y"), second, swap(second, "x")],
        [(4 * rows, BF16)],
        "plane",
    )
    return (own, swap(own, "c")), (first, own)


def core_sum_kernel(after_ref, keep, arrived, first, first_send, second, second_send):
    rows = first.shape[1]
    half = rows // 2

    def total(start, count):
        here = slice(start, start + count)
        return keep[0, here].astype(F32) + arrived[0, here].astype(F32)

    first[0] = total(0, rows)
    first_send[0] = total(2 * rows, rows).astype(BF16)
    for y in range(2):
        start = (2 * y + 1) * rows
        second[0, y * half : (y + 1) * half] = total(start, half)
        second_send[0, y * half : (y + 1) * half] = total(start + half, half).astype(BF16)


def pair_sum_kernel(after_ref, first, first_y, second, second_x, first_keep, first_send, second_keep, second_send):
    half = first_keep.shape[1]
    for value, arrived, keep, send in (
        (first, first_y, first_keep, first_send),
        (second, second_x, second_keep, second_send),
    ):
        keep[0] = value[0, :half] + arrived[0, :half].astype(F32)
        send[0] = (value[0, half:] + arrived[0, half:].astype(F32)).astype(BF16)


def last_sum_kernel(after_ref, first, first_x, second, second_y, out):
    half = first.shape[1]
    out[0, :half] = first[0] + first_x[0].astype(F32)
    out[0, half:] = second[0] + second_y[0].astype(F32)


def slot_scatter(keep, send, after_core, after_pair, after_last):
    rows = keep.shape[1] // 4
    first, first_send, second, second_send = stage(
        core_sum_kernel,
        after_core,
        [keep, swap(send, "c")],
        [(rows, F32), (rows, BF16)] * 2,
        "core_sum",
    )
    first_y, second_x = swap(first_send, "y"), swap(second_send, "x")
    first_keep, first_send, second_keep, second_send = stage(
        pair_sum_kernel,
        after_pair,
        [first, first_y, second, second_x],
        [(rows // 2, F32), (rows // 2, BF16)] * 2,
        "pair_sum",
    )
    first_x, second_y = swap(first_send, "x"), swap(second_send, "y")
    (whole,) = stage(
        last_sum_kernel,
        after_last,
        [first_keep, first_x, second_keep, second_y],
        [(rows, F32)],
        "last_sum",
    )
    return whole, (first, first_y, first_keep, first_x)


def tick_kernel(marker_ref, out_ref):
    corner = marker_ref[...].astype(F32)
    out_ref[0, 0] = jnp.where(jnp.max(corner) <= 3.4e38, 0, 1).astype(jnp.int32)


def tick(marker):
    lead = marker.ndim - 2
    block = (1,) * lead + (min(16, marker.shape[-2]), min(HEAD, marker.shape[-1]))
    flag = pl.pallas_call(
        tick_kernel,
        grid=(1,),
        in_specs=[pl.BlockSpec(block, lambda i: (0,) * marker.ndim)],
        out_specs=pl.BlockSpec(memory_space=pltpu.SMEM),
        out_shape=jax.ShapeDtypeStruct((1, 1), jnp.int32),
        name="tick",
    )(marker)
    return flag[0, 0]


def hold(value, flag):
    return jnp.where(flag == 0, value, jnp.zeros_like(value))


def all_sum(value):
    for axis in ("c", "x", "y"):
        value = value + swap(value, axis)
    for offset in (1, 2):
        value = value + cross(value, offset)
    return lax.psum(value, "g") if lax.axis_size("g") > 1 else value


def flip(value, index, dim):
    return jnp.where(index == 0, value, jnp.flip(value, dim))


def slot_shards(shard):
    return jnp.stack([shard] + [cross(shard, offset) for offset in OFFSETS[1:]])


def from_slots(near, far):
    arrived = cross(far.astype(BF16), 1)
    pair = near + arrived.astype(F32)
    return pair[0] + cross(pair[1].astype(BF16), 2).astype(F32), arrived


def gather_line(value, flag):
    z = lax.axis_index("z")
    across = cross(value, 2)
    others = cross(jnp.stack([value, across]), 1)
    held = [[value, others[0]], [across, others[1]]]
    placed = []
    for high in range(2):
        for low in range(2):
            rows = [jnp.where(z % 2 == low, held[k][0], held[k][1]) for k in range(2)]
            placed.append(jnp.where(z // 2 == high, rows[0], rows[1]))
    return hold(jnp.concatenate(placed, 0), flag)


def scatter_line(value):
    z = lax.axis_index("z")
    parts = value.reshape(2, 2, -1, value.shape[-1])
    keep, send = split(parts, z % 2, 1)
    arrived = cross(send, 1)
    keep = keep.astype(F32) + arrived.astype(F32)
    keep, send = split(keep, z // 2, 0)
    return keep + cross(send.astype(BF16), 2).astype(F32), arrived


def exchange(value, axes):
    return lax.all_to_all(value, axes, split_axis=0, concat_axis=0, tiled=True)


def turn(value, cosine, sine):
    return value * cosine + pltpu.roll(value, HEAD // 2, 1) * sine


def turn_back(value, cosine, sine):
    return value * cosine - pltpu.roll(value, HEAD // 2, 1) * sine


def own_order(target_ref, source_ref, x):
    part = source_ref.shape[0] // 4
    for half in range(2):
        for offset in range(2):
            side = x if offset == 0 else 1 - x
            place = pl.multiple_of((side * 2 + half) * part, part)
            start = (half * 2 + offset) * part
            target_ref[pl.ds(place, part), :] = source_ref[start : start + part, :]


def offset_order(target_ref, source_ref, x):
    part = source_ref.shape[0] // 4
    for half in range(2):
        for offset in range(2):
            side = x if offset == 0 else 1 - x
            place = pl.multiple_of((side * 2 + half) * part, part)
            start = (half * 2 + offset) * part
            target_ref[start : start + part, :] = source_ref[pl.ds(place, part), :]


def place_block(own_ref, halves, half_steps, x):
    for half, source in enumerate(halves):

        @pl.when(pl.program_id(0) // half_steps == half)
        def _():
            own_order(own_ref, source, x)


def project_kernel(heads, half_steps, order_ref, rows_ref, other_ref, weight_ref, bias_ref, cos_ref, sin_ref, own_ref, out_ref):
    place_block(own_ref, (rows_ref, other_ref), half_steps, order_ref[0])
    projected = (
        jnp.dot(own_ref[...], weight_ref[...], preferred_element_type=F32) + bias_ref[...]
    )
    for part in range(3 * heads):
        block = projected[:, part * HEAD : (part + 1) * HEAD]
        if part < 2 * heads:
            block = turn(block, cos_ref[...], sin_ref[...])
        out_ref[:, part * HEAD : (part + 1) * HEAD] = block.astype(BF16)


def plain_kernel(half_steps, order_ref, rows_ref, other_ref, weight_ref, own_ref, out_ref):
    place_block(own_ref, (rows_ref, other_ref), half_steps, order_ref[0])
    out_ref[...] = jnp.dot(
        own_ref[...], weight_ref[...], preferred_element_type=F32
    ).astype(BF16)


def project(order, halves, weight, bias=None, cosine=None, sine=None):
    slots, half_rows, model = halves[0].shape
    halves = [half.reshape(slots * half_rows, model) for half in halves]
    count = 2 * slots * half_rows
    width = weight.shape[1]
    step = half_rows // 2
    steps = 2 * slots
    arrived = [
        pl.BlockSpec((step, model), lambda i, order: (jnp.minimum(i, steps - 1), 0)),
        pl.BlockSpec((step, model), lambda i, order: (jnp.maximum(i - steps, 0), 0)),
    ]
    whole = pl.BlockSpec((model, width), lambda i, order: (0, 0))

    def placed(columns):
        return pl.BlockSpec((step, columns), lambda i, order: (order[i + 1], 0))

    if bias is None:
        kernel, specs, extra = functools.partial(plain_kernel, steps), arrived + [whole], ()
    else:
        kernel = functools.partial(project_kernel, width // (3 * HEAD), steps)
        row = pl.BlockSpec((1, width), lambda i, order: (0, 0))
        specs = arrived + [whole, row, placed(HEAD), placed(HEAD)]
        extra = (bias, cosine, sine)
    return pl.pallas_call(
        kernel,
        grid_spec=pltpu.PrefetchScalarGridSpec(
            num_scalar_prefetch=1,
            grid=(2 * steps,),
            in_specs=specs,
            out_specs=[placed(model), placed(width)],
        ),
        out_shape=[
            jax.ShapeDtypeStruct((count, model), BF16),
            jax.ShapeDtypeStruct((count, width), BF16),
        ],
        compiler_params=pltpu.CompilerParams(vmem_limit_bytes=VMEM_LIMIT),
        cost_estimate=pl.CostEstimate(
            flops=2 * count * model * width,
            bytes_accessed=2 * (2 * count * model + model * width + count * width),
            transcendentals=0,
        ),
        name="project",
    )(order, *halves, weight, *extra)


def spread_kernel(order_ref, act_ref, weight_ref, rows_ref, out_ref, sum_ref, held_ref):
    offset_order(held_ref, act_ref, order_ref[0])
    partial_rows = jnp.dot(held_ref[...], weight_ref[...], preferred_element_type=F32)
    out_ref[...] = partial_rows.astype(BF16)
    products = jnp.sum(partial_rows * rows_ref[...].astype(F32), axis=0, keepdims=True)

    @pl.when(pl.program_id(0) == 0)
    def _():
        sum_ref[...] = products

    @pl.when(pl.program_id(0) > 0)
    def _():
        sum_ref[...] += products


def spread_plain_kernel(order_ref, act_ref, weight_ref, out_ref, held_ref):
    offset_order(held_ref, act_ref, order_ref[0])
    out_ref[...] = jnp.dot(held_ref[...], weight_ref[...], preferred_element_type=F32).astype(BF16)


def spread(order, act, weight, core, rows=None):
    count, inner = act.shape
    model = weight.shape[1]
    slots = order.shape[0] // 4
    step = count // (4 * slots)

    first = core * 2 * slots + 1
    specs = [
        pl.BlockSpec((step, inner), lambda i, order: (order[first + i], 0)),
        pl.BlockSpec((inner, model), lambda i, order: (0, 0)),
    ]
    out_specs = [pl.BlockSpec((step, model), lambda i, order: (i, 0))]
    out_shape = [jax.ShapeDtypeStruct((count // 2, model), BF16)]
    operands = (order, act, weight)
    if rows is not None:
        specs.append(pl.BlockSpec((step, model), lambda i, order: (i, 0)))
        out_specs.append(pl.BlockSpec((1, model), lambda i, order: (0, 0)))
        out_shape.append(jax.ShapeDtypeStruct((1, model), F32))
        operands = operands + (rows.reshape(count // 2, model),)
    results = pl.pallas_call(
        spread_plain_kernel if rows is None else spread_kernel,
        grid_spec=pltpu.PrefetchScalarGridSpec(
            num_scalar_prefetch=1,
            grid=(2 * slots,),
            in_specs=specs,
            out_specs=out_specs,
            scratch_shapes=[pltpu.VMEM((step, inner), BF16)],
        ),
        out_shape=out_shape,
        compiler_params=pltpu.CompilerParams(vmem_limit_bytes=VMEM_LIMIT),
        cost_estimate=pl.CostEstimate(
            flops=count * model * inner,
            bytes_accessed=2 * (count * model + model * inner),
            transcendentals=0,
        ),
        name="spread",
    )(*operands)
    return (results[0].reshape(slots, -1, model),) + tuple(results[1:])


def block_probs(query, keys, seg_q, seg_k, valid_k, first, reach):
    rows, span = query.shape[0], keys.shape[0]
    scores = lax.dot_general(query, keys, (((1,), (1,)), ((), ())), preferred_element_type=F32)
    scores = scores * (HEAD ** (-0.5))
    distance = (
        reach
        + lax.broadcasted_iota(jnp.int32, (rows, span), 0)
        - lax.broadcasted_iota(jnp.int32, (rows, span), 1)
    )
    allowed = (
        (distance >= 0)
        & (distance < WINDOW)
        & (seg_q == seg_k)
        & ((valid_k == 1) | (distance == 0))
    )
    scores = jnp.where(allowed, scores, MASKED)
    powers = jnp.exp(scores - jnp.max(scores, axis=-1, keepdims=True))
    return powers / jnp.sum(powers, axis=-1, keepdims=True)


def attend_kernel(step, reach, q_ref, k_ref, v_ref, segq_ref, segk_ref, valid_ref, out_ref):
    first = pl.multiple_of(pl.program_id(1) * step, step)
    span = pl.ds(first, step + reach)
    probs = block_probs(
        q_ref[...], k_ref[span, :], segq_ref[...], segk_ref[:, span], valid_ref[:, span], first, reach
    )
    out_ref[...] = jnp.dot(
        probs.astype(BF16), v_ref[span, :], preferred_element_type=F32
    ).astype(BF16)


def head_specs(count, step, heads):
    ahead = count // (2 * step)
    return [
        pl.BlockSpec((step, HEAD), lambda h, i: (i + ahead, h)),
        pl.BlockSpec((count, HEAD), lambda h, i: (0, heads + h)),
        pl.BlockSpec((count, HEAD), lambda h, i: (0, 2 * heads + h)),
    ]


def attend(projected, seg_q, seg_k, valid_k):
    held, width = projected.shape
    count, width = held // 2, width // 3
    step = count // 4
    heads = width // HEAD
    flops = 4 * count * (step + count) * width
    return pl.pallas_call(
        functools.partial(attend_kernel, step, count),
        grid=(heads, 4),
        in_specs=head_specs(held, step, heads)
        + [
            pl.BlockSpec((step, 1), lambda h, i: (i, 0)),
            pl.BlockSpec((1, held), lambda h, i: (0, 0)),
            pl.BlockSpec((1, held), lambda h, i: (0, 0)),
        ],
        out_specs=pl.BlockSpec((step, HEAD), lambda h, i: (i, h)),
        out_shape=jax.ShapeDtypeStruct((count, width), BF16),
        compiler_params=pltpu.CompilerParams(vmem_limit_bytes=VMEM_LIMIT),
        cost_estimate=pl.CostEstimate(
            flops=flops, bytes_accessed=8 * held * width, transcendentals=flops // (4 * HEAD)
        ),
        name="attend",
    )(projected, projected, projected, seg_q, seg_k, valid_k)


def attend_back_kernel(
    step, reach, heads, q_ref, k_ref, v_ref, g_ref, segq_ref, segk_ref, valid_ref, cos_ref, sin_ref,
    out_ref, dk_ref, dv_ref,
):
    head, block = pl.program_id(0), pl.program_id(1)
    first = pl.multiple_of(block * step, step)
    span = pl.ds(first, step + reach)
    columns = [pl.ds(pl.multiple_of((part * heads + head) * HEAD, HEAD), HEAD) for part in range(3)]

    @pl.when(block == 0)
    def _():
        dk_ref[...] = jnp.zeros_like(dk_ref)
        dv_ref[...] = jnp.zeros_like(dv_ref)
        out_ref[0:reach, columns[0]] = jnp.zeros((reach, HEAD), BF16)

    query, keys, grad = q_ref[...], k_ref[span, :], g_ref[...]
    probs = block_probs(
        query, keys, segq_ref[...], segk_ref[:, span], valid_ref[:, span], first, reach
    )
    g_probs = lax.dot_general(
        grad, v_ref[span, :], (((1,), (1,)), ((), ())), preferred_element_type=F32
    )
    inner = jnp.sum(probs * g_probs, axis=-1, keepdims=True)
    g_scores = (probs * (g_probs - inner)).astype(BF16)
    scale = HEAD ** (-0.5)
    dq = jnp.dot(g_scores, keys, preferred_element_type=F32) * scale
    here = pl.ds(pl.multiple_of(first + reach, step), step)
    out_ref[here, columns[0]] = turn_back(dq, cos_ref[here, :], sin_ref[here, :]).astype(BF16)
    dk_ref[span, :] += (
        lax.dot_general(g_scores, query, (((0,), (0,)), ((), ())), preferred_element_type=F32)
        * scale
    )
    dv_ref[span, :] += lax.dot_general(
        probs.astype(BF16), grad, (((0,), (0,)), ((), ())), preferred_element_type=F32
    )

    @pl.when(block == pl.num_programs(1) - 1)
    def _():
        out_ref[:, columns[1]] = turn_back(dk_ref[...], cos_ref[...], sin_ref[...]).astype(BF16)
        out_ref[:, columns[2]] = dv_ref[...].astype(BF16)


def attend_back(projected, grad, seg_q, seg_k, valid_k, cosine, sine):
    held, width = projected.shape
    count, width = held // 2, width // 3
    step = count // 4
    heads = width // HEAD
    flops = 10 * count * (step + count) * width
    return pl.pallas_call(
        functools.partial(attend_back_kernel, step, count, heads),
        grid=(heads, 4),
        in_specs=head_specs(held, step, heads)
        + [
            pl.BlockSpec((step, HEAD), lambda h, i: (i, h)),
            pl.BlockSpec((step, 1), lambda h, i: (i, 0)),
            pl.BlockSpec((1, held), lambda h, i: (0, 0)),
            pl.BlockSpec((1, held), lambda h, i: (0, 0)),
            pl.BlockSpec((held, HEAD), lambda h, i: (0, 0)),
            pl.BlockSpec((held, HEAD), lambda h, i: (0, 0)),
        ],
        out_specs=pl.BlockSpec((held, 3 * width), lambda h, i: (0, 0)),
        out_shape=jax.ShapeDtypeStruct((held, 3 * width), BF16),
        scratch_shapes=[pltpu.VMEM((held, HEAD), F32)] * 2,
        compiler_params=pltpu.CompilerParams(vmem_limit_bytes=VMEM_LIMIT),
        cost_estimate=pl.CostEstimate(
            flops=flops, bytes_accessed=12 * held * width, transcendentals=flops // (10 * HEAD)
        ),
        name="attend_back",
    )(projected, projected, projected, grad, seg_q, seg_k, valid_k, cosine, sine)


def one_hot(slot_row, capacity):
    rows = lax.broadcasted_iota(jnp.int32, (capacity, slot_row.shape[1]), 0)
    return slot_row == rows


def moe_in_kernel(
    shape, expert_ref, rows_ref, other_rows_ref, grad_ref, other_grad_ref, win_ref, wdn_ref, slot_ref,
    act_ref, hid_ref, sig_ref, erow_ref, egrad_ref, egate_ref,
):
    experts, own, held, capacity = shape
    here = pl.program_id(0) < pl.num_programs(0) // 2
    rows = jnp.where(here, rows_ref[...], other_rows_ref[...])
    grad = jnp.where(here, grad_ref[...], other_grad_ref[...])
    inputs = dot_nt(rows, win_ref[...])
    gate_in, up_in = inputs[:, :held], inputs[:, held:]
    raw = dot_nt(grad, wdn_ref[...])
    column = lax.broadcasted_iota(jnp.int32, (1, held), 1)
    is_router = (column >= own) & (column < own + experts)
    logits = jnp.where(is_router, up_in, MASKED)
    powers = jnp.exp(logits - jnp.max(logits, axis=-1, keepdims=True))
    picked = jnp.where(column == own + expert_ref[0], powers, 0.0)
    gate = jnp.sum(picked, axis=-1, keepdims=True) / jnp.sum(powers, axis=-1, keepdims=True)
    shared_in = jnp.sum(jnp.where(column == own + experts, up_in, 0.0), axis=-1, keepdims=True)
    shared_gate = 1.0 / (1.0 + jnp.exp(-shared_in))
    sigma = 1.0 / (1.0 + jnp.exp(-gate_in))
    swished = gate_in * sigma
    hidden = swished * up_in
    grad_hidden = shared_gate * raw
    act_ref[:, :held] = (grad_hidden * up_in * sigma * (1.0 + gate_in * (1.0 - sigma))).astype(BF16)
    act_ref[:, held:] = (grad_hidden * swished).astype(BF16)
    hid_ref[...] = (shared_gate * hidden).astype(BF16)
    sig_ref[...] = jnp.sum(hidden * grad_hidden, axis=-1, keepdims=True) * (1.0 - shared_gate)
    place = jnp.where(one_hot(slot_ref[0], capacity), 1.0, 0.0)
    place_low = place.astype(BF16)
    erow_ref[...] = jnp.dot(place_low, rows, preferred_element_type=F32).astype(BF16)
    egrad_ref[...] = jnp.dot(place_low, grad, preferred_element_type=F32).astype(BF16)
    egate_ref[...] = jnp.dot(
        place,
        jnp.broadcast_to(gate, (gate.shape[0], HEAD)),
        precision=lax.Precision.HIGHEST,
        preferred_element_type=F32,
    )


def moe_in(expert, rows, grads, chunk, w_in, w_dn, slot_rows, experts, own, capacity):
    blocks, _, step = slot_rows.shape
    model = rows[0].shape[1]
    held = w_dn.shape[0]
    count = blocks * step
    half = blocks // 2

    def row_spec(core):
        def block(i):
            return jnp.maximum(i - half, 0) if core else jnp.minimum(i, half - 1)

        return pl.BlockSpec((step, model), lambda i: (block(i), 0))

    def grad_spec(core):
        def block(i):
            i = jnp.maximum(i - half, 0) if core else jnp.minimum(i, half - 1)
            return ((i // 4) * 2 + chunk) * 4 + i % 4

        return pl.BlockSpec((step, model), lambda i: (block(i), 0))

    return pl.pallas_call(
        functools.partial(moe_in_kernel, (experts, own, held, capacity)),
        grid=(blocks,),
        in_specs=[
            pl.BlockSpec(memory_space=pltpu.SMEM),
            row_spec(0),
            row_spec(1),
            grad_spec(0),
            grad_spec(1),
            pl.BlockSpec((2 * held, model), lambda i: (0, 0)),
            pl.BlockSpec((held, model), lambda i: (0, 0)),
            pl.BlockSpec((1, 1, step), lambda i: (i, 0, 0)),
        ],
        out_specs=[
            pl.BlockSpec((step, 2 * held), lambda i: (i, 0)),
            pl.BlockSpec((step, held), lambda i: (i, 0)),
            pl.BlockSpec((step, 1), lambda i: (i, 0)),
            pl.BlockSpec((capacity, model), lambda i: (i, 0)),
            pl.BlockSpec((capacity, model), lambda i: (i, 0)),
            pl.BlockSpec((capacity, HEAD), lambda i: (i, 0)),
        ],
        out_shape=[
            jax.ShapeDtypeStruct((count, 2 * held), BF16),
            jax.ShapeDtypeStruct((count, held), BF16),
            jax.ShapeDtypeStruct((count, 1), F32),
            jax.ShapeDtypeStruct((blocks * capacity, model), BF16),
            jax.ShapeDtypeStruct((blocks * capacity, model), BF16),
            jax.ShapeDtypeStruct((blocks * capacity, HEAD), F32),
        ],
        compiler_params=pltpu.CompilerParams(vmem_limit_bytes=VMEM_LIMIT),
        cost_estimate=pl.CostEstimate(
            flops=2 * count * model * (3 * held + 2 * capacity),
            bytes_accessed=6 * count * model,
            transcendentals=2 * count * held,
        ),
        name="moe_in",
    )(expert, *rows, *grads, w_in, w_dn, slot_rows)


def dot_nt(left, right):
    return lax.dot_general(left, right, (((1,), (1,)), ((), ())), preferred_element_type=F32)


def expert_kernel(
    steps, after_ref, rows_ref, grad_ref, gate_ref, wgu_ref, wd_ref,
    back_ref, out_ref, dgu_ref, hid_ref, ggate_ref, acc_g, acc_u, acc_r,
):
    step = pl.program_id(0)

    @pl.when(step == 0)
    def _():
        acc_g[...] = dot_nt(rows_ref[...], wgu_ref[0])
        acc_u[...] = dot_nt(rows_ref[...], wgu_ref[1])
        acc_r[...] = dot_nt(grad_ref[...], wd_ref[...])

    @pl.when((step > 0) & (step < steps))
    def _():
        acc_g[...] += dot_nt(rows_ref[...], wgu_ref[0])
        acc_u[...] += dot_nt(rows_ref[...], wgu_ref[1])
        acc_r[...] += dot_nt(grad_ref[...], wd_ref[...])

    @pl.when(step == steps)
    def _():
        gate_in, up_in, raw, gates = acc_g[...], acc_u[...], acc_r[...], gate_ref[:, :1]
        sigma = 1.0 / (1.0 + jnp.exp(-gate_in))
        swished = gate_in * sigma
        hidden = swished * up_in
        ggate_ref[...] = jnp.sum(hidden * raw, axis=-1, keepdims=True)
        hid_ref[...] = (gates * hidden).astype(BF16)
        scaled = gates * raw
        dgu_ref[0] = (scaled * up_in * sigma * (1.0 + gate_in * (1.0 - sigma))).astype(BF16)
        dgu_ref[1] = (scaled * swished).astype(BF16)

    @pl.when(step >= steps)
    def _():
        back = jnp.dot(dgu_ref[0], wgu_ref[0], preferred_element_type=F32)
        back = back + jnp.dot(dgu_ref[1], wgu_ref[1], preferred_element_type=F32)
        back_ref[...] = back.astype(BF16)
        out_ref[...] = jnp.dot(hid_ref[...], wd_ref[...], preferred_element_type=F32).astype(BF16)


def run_expert(after, rows, grad, gates, w_gu, w_down):
    count, model = rows.shape
    cols = w_down.shape[0]
    steps = 4
    chunk = model // steps
    return pl.pallas_call(
        functools.partial(expert_kernel, steps),
        grid=(2 * steps,),
        in_specs=[
            pl.BlockSpec(memory_space=pltpu.SMEM),
            pl.BlockSpec((count, chunk), lambda i: (0, jnp.minimum(i, steps - 1))),
            pl.BlockSpec((count, chunk), lambda i: (0, jnp.minimum(i, steps - 1))),
            pl.BlockSpec((count, HEAD), lambda i: (0, 0)),
            pl.BlockSpec((2, cols, chunk), lambda i: (0, 0, i % steps)),
            pl.BlockSpec((cols, chunk), lambda i: (0, i % steps)),
        ],
        out_specs=[
            pl.BlockSpec((count, chunk), lambda i: (0, jnp.maximum(i - steps, 0))),
            pl.BlockSpec((count, chunk), lambda i: (0, jnp.maximum(i - steps, 0))),
            pl.BlockSpec((2, count, cols), lambda i: (0, 0, 0)),
            pl.BlockSpec((count, cols), lambda i: (0, 0)),
            pl.BlockSpec((count, 1), lambda i: (0, 0)),
        ],
        out_shape=[
            jax.ShapeDtypeStruct((count, model), BF16),
            jax.ShapeDtypeStruct((count, model), BF16),
            jax.ShapeDtypeStruct((2, count, cols), BF16),
            jax.ShapeDtypeStruct((count, cols), BF16),
            jax.ShapeDtypeStruct((count, 1), F32),
        ],
        scratch_shapes=[pltpu.VMEM((count, cols), F32)] * 3,
        compiler_params=pltpu.CompilerParams(vmem_limit_bytes=VMEM_LIMIT),
        cost_estimate=pl.CostEstimate(
            flops=12 * count * model * cols,
            bytes_accessed=8 * count * model + 12 * model * cols,
            transcendentals=count * cols,
        ),
        name="run_expert",
    )(after.reshape(1), rows, grad, gates, w_gu, w_down)


def sum_kernel(after_ref, *refs):
    lefts, rights = refs[: len(refs) // 2 - 1], refs[len(refs) // 2 - 1 : -2]
    out_ref, acc_ref = refs[-2:]
    tile = pl.program_id(2)
    total = None
    for left, right in zip(lefts, rights):
        part = lax.dot_general(
            left[0], right[...], (((0,), (0,)), ((), ())), preferred_element_type=F32
        )
        total = part if total is None else total + part

    @pl.when(tile == 0)
    def _():
        acc_ref[...] = total

    @pl.when(tile > 0)
    def _():
        acc_ref[...] += total

    @pl.when(tile == pl.num_programs(2) - 1)
    def _():
        out_ref[0] = acc_ref[...].astype(out_ref.dtype)


def weight_sum(after, terms, tile, steps_of_tiles, dtype):
    parts, _, inner = terms[0][0].shape
    model = terms[0][2].shape[1]
    steps = 4
    width = model // steps

    def left_spec(first):
        return pl.BlockSpec((1, tile, inner), lambda j, d, t: (j, t + first, 0))

    def right_spec(stride, first):
        return pl.BlockSpec((tile, width), lambda j, d, t: (t * stride + first, d))

    return pl.pallas_call(
        sum_kernel,
        grid=(parts, steps, steps_of_tiles),
        in_specs=[pl.BlockSpec(memory_space=pltpu.SMEM)]
        + [left_spec(term[1]) for term in terms]
        + [right_spec(*term[3:]) for term in terms],
        out_specs=pl.BlockSpec((1, inner, width), lambda j, d, t: (j, 0, d)),
        out_shape=jax.ShapeDtypeStruct((parts, inner, model), dtype),
        scratch_shapes=[pltpu.VMEM((inner, width), F32)],
        compiler_params=pltpu.CompilerParams(vmem_limit_bytes=VMEM_LIMIT),
        cost_estimate=pl.CostEstimate(
            flops=2 * len(terms) * parts * steps_of_tiles * tile * inner * model,
            bytes_accessed=len(terms) * 2 * steps_of_tiles * tile * (parts * inner + model)
            + 4 * parts * inner * model,
            transcendentals=0,
        ),
        name="weight_sum",
    )(after.reshape(1), *[term[0] for term in terms], *[term[2] for term in terms])


def combine_kernel(capacity, after_ref, act_ref, weight_ref, slot_ref, rows_ref, out_ref):
    place = jnp.where(one_hot(slot_ref[0], capacity), 1.0, 0.0).astype(BF16)
    routed = lax.dot_general(
        place, rows_ref[...], (((0,), (0,)), ((), ())), preferred_element_type=F32
    )
    own = jnp.dot(act_ref[...], weight_ref[...], preferred_element_type=F32)
    out_ref[...] = (own + routed).astype(BF16)


def combine(after, act, weight, slot_rows, rows, core):
    inner, model = weight.shape
    blocks, _, step = slot_rows.shape
    capacity = rows.shape[0] // blocks
    taken = blocks // 2

    def block(i):
        return core * taken + i

    return pl.pallas_call(
        functools.partial(combine_kernel, capacity),
        grid=(taken,),
        in_specs=[
            pl.BlockSpec(memory_space=pltpu.SMEM),
            pl.BlockSpec((step, inner), lambda i: (block(i), 0)),
            pl.BlockSpec((inner, model), lambda i: (0, 0)),
            pl.BlockSpec((1, 1, step), lambda i: (block(i), 0, 0)),
            pl.BlockSpec((capacity, model), lambda i: (block(i), 0)),
        ],
        out_specs=pl.BlockSpec((step, model), lambda i: (i, 0)),
        out_shape=jax.ShapeDtypeStruct((taken * step, model), BF16),
        compiler_params=pltpu.CompilerParams(vmem_limit_bytes=VMEM_LIMIT),
        cost_estimate=pl.CostEstimate(
            flops=2 * taken * step * model * (inner + capacity),
            bytes_accessed=2 * taken * (step * (model + inner) + capacity * model),
            transcendentals=0,
        ),
        name="combine",
    )(after.reshape(1), act, weight, slot_rows, rows)


def norm_scale(rows_in):
    return lax.rsqrt(jnp.mean(rows_in * rows_in, axis=-1, keepdims=True) + EPSILON)


def norm_back(rows_in, scaling, gain, grad):
    unit_rows = rows_in * scaling
    grad_unit = grad * gain
    return scaling * (
        grad_unit - unit_rows * jnp.mean(grad_unit * unit_rows, axis=-1, keepdims=True)
    )


def swish(gate_in):
    return gate_in * jax.nn.sigmoid(gate_in)


def swish_back(gate_in, up_in, grad):
    sigma = jax.nn.sigmoid(gate_in)
    grad_gate = grad * up_in * sigma * (1.0 + gate_in * (1.0 - sigma))
    return (grad_gate, grad * gate_in * sigma)


def rope_tables(first_row, row_count):
    placing = (first_row + jnp.arange(row_count, dtype=jnp.int32)) % SEQ
    frequency = ROPE_BASE ** (-(jnp.arange(HEAD // 2, dtype=F32) * 2.0 / HEAD))
    angles = placing.astype(F32)[:, None] * frequency[None, :]
    cosine, sine = jnp.cos(angles), jnp.sin(angles)
    return (
        jnp.concatenate([cosine, cosine], 1),
        jnp.concatenate([-sine, sine], 1),
    )


def per_device(
    hidden_in,
    cotangent,
    norm_gains,
    qkv_weight,
    qkv_bias,
    out_weight,
    router_weight,
    shared_gate_vec,
    shared_gate_up,
    shared_down,
    expert_gate_up,
    expert_down,
    segments,
    valid_mask,
    routes,
    slots,
):
    groups = lax.axis_size("g")
    blocks = segments.shape[0]
    rows_here, model = hidden_in.shape
    weight_rows, local_cols = qkv_weight.shape[1:]
    shared_cols = shared_gate_up.shape[2]
    experts, top = router_weight.shape[1], routes.shape[1]
    shares = groups * 4 * LINE
    cols = local_cols // 4
    own = shared_cols // shares
    held = -(-(own + experts + 1) // 128) * 128
    capacity = -(-(blocks * top * 4 // (3 * experts)) // 16) * 16
    plane_rows = 4 * blocks
    everywhere = ("g",) + GROUP
    g, z, y, c, x = (lax.axis_index(axis) for axis in EVERY)
    expert = ((g * LINE + z) * 2 + y) * 2 + c

    ahead = [(k, k + 1) for k in range(LINE - 1)]
    behind = [(k + 1, k) for k in range(LINE - 1)]

    residual = hidden_in.astype(F32)
    gain_attn, gain_moe = norm_gains[0], norm_gains[1]
    scale_attn = norm_scale(residual)
    own_attn = (residual * scale_attn * gain_attn).astype(BF16)
    before = lax.ppermute(own_attn, "z", ahead)
    grad_shards = slot_shards(cotangent)
    now = jnp.zeros((), jnp.int32)
    rows_attn, attn_marks = slot_gather(jnp.stack([before, own_attn]), now, now)
    flag = tick(attn_marks[0])
    slot_grads, grad_marks = slot_gather(hold(grad_shards, flag), now, now)
    slot_grads = [half.reshape(-1, model) for half in slot_grads]

    def cut_heads(value):
        return value.reshape(weight_rows, -1, 4, cols).transpose(2, 0, 1, 3)

    qkv_cut = cut_heads(qkv_weight.transpose(1, 0, 2)).reshape(4, weight_rows, 3 * cols)
    out_cut = cut_heads(out_weight.T).reshape(4, weight_rows, cols)
    w_heads = exchange(jnp.concatenate([qkv_cut, out_cut], 2), ("y", "c"))
    w_heads = w_heads.reshape(4 * weight_rows, 4 * cols)
    w_qkv = gather_line(w_heads[:, : 3 * cols], tick(grad_marks[0]))
    if groups > 1:
        w_qkv = lax.all_gather(w_qkv, "g", axis=0, tiled=True)
    later = tick(w_heads)

    numbers = jnp.concatenate([segments[None], valid_mask[None], routes.T, slots.T], 0) + later
    numbers = jnp.stack([numbers, swap(numbers, "y")])
    numbers = jnp.stack([numbers, swap(numbers, "c")])
    plane_numbers = flip(flip(numbers[:, :, :2], c, 0), y, 1).transpose(1, 0, 2, 3)
    plane_numbers = plane_numbers.reshape(4, 2, blocks).transpose(1, 0, 2).reshape(2, plane_rows)
    numbers = slot_shards(numbers)
    numbers = numbers.reshape(LINE, 1, 4, 2 + 2 * top, blocks)
    if groups > 1:
        numbers = lax.all_gather(numbers, "g", axis=1, tiled=True)
    slot_here = jnp.max(
        jnp.where(numbers[:, :, :, 2 : 2 + top] == expert, numbers[:, :, :, 2 + top :], -1), 3
    )
    slot_here = slot_here.reshape(LINE, groups, 4, 2, 2, rows_here // 2)
    slot_here = flip(slot_here, x, 3).transpose(0, 1, 2, 4, 3, 5)
    slot_here = slot_here.reshape(2, 2, groups, 2, 2, blocks)

    late_gu, late_dn = hold(shared_gate_up, later), hold(shared_down, later)
    shared_cut = jnp.concatenate(
        [
            late_gu[0].T.reshape(shares, own, weight_rows),
            late_gu[1].T.reshape(shares, own, weight_rows),
            late_dn.reshape(shares, own, weight_rows),
        ],
        1,
    )

    here = x * local_cols + (y * 2 + c) * cols
    bias = lax.dynamic_slice_in_dim(qkv_bias, here, cols, 1).astype(F32).reshape(1, 3 * cols)
    cosine, sine = rope_tables((z + LINE - 1) * plane_rows + later, 2 * plane_rows)
    order = jnp.stack([(y ^ j) * 2 + (c ^ i) for i in range(2) for j in range(2)])
    order = order.astype(jnp.int32)
    order_one = jnp.concatenate([x[None], order])
    order_two = jnp.concatenate([x[None], order[:2], order[:2] + 4, order[2:], order[2:] + 4])
    own_rows, projected = project(order_two, rows_attn, w_qkv, bias, cosine, sine)
    w_out = gather_line(hold(w_heads[:, 3 * cols :], tick(w_qkv)), now)
    if groups > 1:
        w_out = lax.all_gather(w_out, "g", axis=0, tiled=True)
    numbers_before = jnp.where(z == 0, -1, lax.ppermute(plane_numbers, "z", ahead))
    near = jnp.concatenate([numbers_before, plane_numbers], 1)
    seg_k, valid_k = near[:1], near[1:]
    seg_q = plane_numbers[0].reshape(plane_rows, 1)
    attended = attend(projected, seg_q, seg_k, valid_k)
    w_out_t = w_out.T
    order_late = order_one + tick(grad_marks[1])
    (send,) = spread(order_late, attended, w_out_t, 1)
    (keep,) = spread(order_late, attended, w_out_t, 0)
    attn_rows = slot_scatter(keep, send, now, now, now)[0][0]
    middle = residual + attn_rows
    scale_moe = norm_scale(middle)
    own_moe = (middle * scale_moe * gain_moe).astype(BF16)

    w_shared = exchange(hold(shared_cut, tick(attended)), everywhere)
    w_shared = w_shared.transpose(1, 0, 2).reshape(3 * own, model)

    def padded(*values):
        value = jnp.concatenate(values, 0)
        return jnp.pad(value, ((0, held - value.shape[0]), (0, 0)))

    shared_in = jnp.concatenate(
        [
            padded(w_shared[:own]),
            padded(w_shared[own : 2 * own], router_weight.T, shared_gate_vec[None]),
        ],
        0,
    )
    shared_dn = padded(w_shared[2 * own :])

    near_shards = jnp.stack([own_moe, cross(own_moe, 2)])
    far_shards = cross(near_shards, 1)
    near_rows, near_marks = slot_gather(near_shards, now, now)
    far_rows, far_marks = slot_gather(hold(far_shards, tick(near_marks[1])), now, now)
    chunk_rows = [[half.reshape(-1, model) for half in rows] for rows in (near_rows, far_rows)]
    if groups > 1:
        chunk_rows = [
            [lax.all_gather(half, "g", axis=0, tiled=True) for half in rows] for rows in chunk_rows
        ]
        slot_grads = [lax.all_gather(half, "g", axis=0, tiled=True) for half in slot_grads]

    w_gu, w_down = expert_gate_up[0].transpose(0, 2, 1), expert_down[0]
    expert_id = expert.reshape(1).astype(jnp.int32)

    def slots_of(table):
        return table.transpose(3, 2, 0, 1, 4, 5).reshape(-1, 1, blocks)

    def to_owners(act, weight, table, rows, after):
        halves = []
        for core in range(2):
            half = combine(after[1 - core], act, weight, table, rows, core)
            if groups > 1:
                half = lax.psum_scatter(half, "g", scatter_dimension=0, tiled=True)
            halves.append(half.reshape(-1, plane_rows // 2, model))
        total, marks = slot_scatter(*halves, *after[2:])
        return total, (halves[0],) + marks

    acts, hiddens, signals, inputs, grads, results = [], [], [], [], [], []
    gate_grads, totals = [], []
    start, begin = tick(far_marks[0]), tick(far_marks[1])
    for chunk, rows in enumerate(chunk_rows):
        table = slots_of(slot_here[chunk : chunk + 1])
        act, hid, sig, erow, egrad, egate = moe_in(
            expert_id + start,
            rows, slot_grads, chunk, shared_in, shared_dn, table, experts, own, capacity,
        )
        back, out, dgu, ehid, ggate = run_expert(now, erow, egrad, egate, w_gu, w_down)
        chosen = table == jnp.arange(capacity, dtype=jnp.int32)[None, :, None]
        ggate = ggate.reshape(-1, capacity, 1)
        gate_grads.append(jnp.sum(jnp.where(chosen, ggate, 0.0), axis=1))
        signals.append(sig.reshape(-1, blocks))
        total, marks = to_owners(act, shared_in, table, back, (begin, now, now, now, now))
        start, begin = tick(marks[1]), tick(marks[3])
        totals.append(total)
        acts.append(act)
        hiddens.append(hid)
        inputs.append((dgu, erow))
        grads.append((ehid, egrad))
        results.append(out)
    grad_normed, last_mark = from_slots(totals[0], totals[1])

    signals = jnp.stack([jnp.stack(gate_grads), jnp.stack(signals)])
    signals = signals.reshape(2, 2, 2, groups, 2, 2, 2, 2, rows_here // 2)
    for dim, index in ((1, z % 2), (2, c), (4, z // 2), (5, y), (7, x)):
        signals = flip(signals, index, dim)
    signals = signals.transpose(3, 4, 1, 5, 2, 7, 0, 6, 8).reshape(2 * shares, 2, rows_here)
    signals = exchange(signals, EVERY).reshape(experts, 2, 2, rows_here)
    grad_router_probs = jnp.sum(signals[:, :, 0], axis=1).T
    gate_signal = jnp.sum(signals[:, :, 1], axis=(0, 1))

    def over_chunks(parts):
        width = parts[0].shape[-1]
        parts = [part.reshape(2, groups, -1, width) for part in parts]
        return jnp.concatenate(parts, 2).reshape(-1, width)

    if groups == 1:
        moe_parts, moe_marks = to_owners(
            over_chunks(hiddens),
            shared_dn,
            slots_of(slot_here),
            over_chunks(results),
            (tick(marks[0]), tick(marks[2]), now, now, now),
        )
        moe_parts = [moe_parts[:2], moe_parts[2:]]
    else:
        moe_parts = []
        for chunk in range(2):
            table = slots_of(slot_here[chunk : chunk + 1])
            after = tick(moe_parts[-1] if moe_parts else last_mark)
            part, moe_marks = to_owners(
                hiddens[chunk], shared_dn, table, results[chunk], (after, after, now, now, now)
            )
            moe_parts.append(part)
    moe_rows, _ = from_slots(*moe_parts)
    output = (middle + moe_rows).astype(BF16)
    tiles = range(2)
    grad_sgu = weight_sum(
        tick(marks[4]),
        [
            (acts[chunk][None], core * groups, chunk_rows[chunk][core], 1, 0)
            for chunk in tiles
            for core in tiles
        ],
        plane_rows,
        groups,
        BF16,
    )[0]
    grad_sdn = weight_sum(
        tick(last_mark),
        [
            (hiddens[chunk][None], core * groups, slot_grads[core], 2, chunk)
            for chunk in tiles
            for core in tiles
        ],
        plane_rows,
        groups,
        BF16,
    )[0]
    shared_grad = jnp.concatenate(
        [grad_sgu[:own], grad_sgu[held : held + own], grad_sdn[:own]], 0
    )
    shared_grad = shared_grad.reshape(3 * own, shares, weight_rows).transpose(1, 0, 2)
    shared_grad = exchange(shared_grad, everywhere)
    shared_mark = tick(shared_grad)
    shared_grad = shared_grad.reshape(shares, 3, own, weight_rows).transpose(1, 0, 2, 3)
    shared_grad = shared_grad.reshape(3, shared_cols, weight_rows).astype(F32)

    own_logits = jnp.dot(own_moe, router_weight, preferred_element_type=F32)
    router_probs = jax.nn.softmax(own_logits, axis=-1)
    grad_logits = router_probs * (
        grad_router_probs - jnp.sum(router_probs * grad_router_probs, axis=-1, keepdims=True)
    )
    grad_normed = (
        grad_normed
        + gate_signal[:, None] * shared_gate_vec.astype(F32)[None, :]
        + jnp.einsum("te,de->td", grad_logits, router_weight.astype(F32))
    )
    own_float = own_moe.astype(F32)
    grad_router = jnp.einsum("td,te->ed", own_float, grad_logits)
    grad_gate_vec = jnp.sum(gate_signal[:, None] * own_float, axis=0)
    grad_gain_moe = jnp.sum(grad_normed * (middle * scale_moe), axis=0)
    grad_middle = cotangent.astype(F32) + norm_back(middle, scale_moe, gain_moe, grad_normed)
    grad_attn = grad_middle.astype(BF16)

    plane_grad, _ = slot_gather(grad_attn[None], now, now)
    plane_grad, grad_attended = project(order_one + tick(moe_marks[1]), plane_grad, w_out)
    grad_projected = attend_back(
        projected, grad_attended, seg_q, seg_k, valid_k, cosine, sine
    )
    w_qkv_t = w_qkv.T
    order_late = order_two + shared_mark
    send, sum_send = spread(order_late, grad_projected, w_qkv_t, 1, rows_attn[1])
    keep, sum_keep = spread(order_late, grad_projected, w_qkv_t, 0, rows_attn[0])
    gain_sum = (sum_send + sum_keep)[0] / gain_attn
    back_both, back_marks = slot_scatter(keep, send, tick(moe_marks[3]), now, now)
    back_own = back_both[1] + lax.ppermute(back_both[0].astype(BF16), "z", behind).astype(F32)
    input_grad = grad_middle + norm_back(residual, scale_attn, gain_attn, back_own)
    bias_sum = jnp.sum(grad_projected.astype(F32), axis=0).reshape(3, cols)
    grad_bias = lax.dynamic_update_slice_in_dim(jnp.zeros((3, model), F32), bias_sum, here, 1)

    def weight_grad(left, right):
        return lax.dot_general(left, right, (((0,), (0,)), ((), ())), preferred_element_type=F32)

    def to_weight_owners(value):
        if groups > 1:
            value = lax.psum_scatter(value, "g", scatter_dimension=0, tiled=True)
        value, mark = scatter_line(value)
        value = exchange(value.astype(BF16).reshape(4, weight_rows, -1), ("y", "c"))
        return value.astype(F32), mark

    grad_out, _ = to_weight_owners(weight_grad(plane_grad, attended).astype(BF16))
    grad_out = grad_out.transpose(1, 0, 2).reshape(weight_rows, local_cols).T
    grad_qkv, qkv_mark = to_weight_owners(weight_grad(own_rows, grad_projected).astype(BF16))
    grad_qkv = grad_qkv.reshape(4, weight_rows, 3, cols).transpose(2, 1, 0, 3)
    grad_qkv = grad_qkv.reshape(3, weight_rows, local_cols)

    tile = inputs[0][1].shape[0]
    grad_egu = weight_sum(
        tick(back_marks[1]), [(left, 0, right, 1, 0) for left, right in inputs], tile, 1, F32
    )
    grad_egu = grad_egu.transpose(0, 2, 1)[None]
    grad_edown = weight_sum(
        tick(qkv_mark), [(left[None], 0, right, 1, 0) for left, right in grads], tile, 1, F32
    )

    valid_rows = lax.dynamic_slice_in_dim(valid_mask, x * rows_here, rows_here, 0).astype(F32)
    valid_rows = valid_rows[:, None]

    def in_lanes(values):
        flat = jnp.stack(values)
        return jnp.pad(flat, (0, model - len(values)))[None]

    sums_of_all = all_sum(
        jnp.concatenate(
            [
                grad_router,
                grad_gate_vec[None],
                grad_gain_moe[None],
                gain_sum[None],
                grad_bias,
                in_lanes(
                    [
                        jnp.sum(valid_rows * residual * residual),
                        jnp.sum(valid_rows * attn_rows * attn_rows),
                        jnp.sum(valid_rows * moe_rows * moe_rows),
                        jnp.sum(valid_rows),
                    ]
                ),
            ],
            0,
        )
    )
    others = sums_of_all[experts:]
    root_means = jnp.sqrt(others[6, :3] / (jnp.maximum(others[6, 3], 1.0) * model))
    return (
        output,
        input_grad,
        jnp.stack([others[2], others[1]]),
        grad_qkv,
        others[3:6],
        grad_out,
        sums_of_all[:experts].T,
        others[0],
        shared_grad[:2].transpose(0, 2, 1),
        shared_grad[2],
        grad_egu,
        grad_edown,
        root_means[0],
        root_means[1],
        root_means[2],
    )


def solution(mesh):
    dp, mp = mesh.shape["dp"], mesh.shape["mp"]
    inner = Mesh(mesh.devices.reshape(dp // (4 * LINE), LINE, 2, 2, mp), EVERY)
    d = ("g",) + GROUP
    placed = (
        P(EVERY, None),
        P(EVERY, None),
        P(),
        P(None, d, "x"),
        P(),
        P("x", d),
        P(),
        P(),
        P(None, d, "x"),
        P("x", d),
        P(d, None, None, "x"),
        P(d, "x", None),
        P(d),
        P(d),
        P(d, None),
        P(d, None),
    )
    return jax.shard_map(
        per_device,
        mesh=inner,
        in_specs=placed,
        out_specs=(
            P(EVERY, None),
            P(EVERY, None),
            P(),
            P(None, d, "x"),
            P(),
            P("x", d),
            P(),
            P(),
            P(None, d, "x"),
            P("x", d),
            P(d, None, None, "x"),
            P(d, "x", None),
            P(),
            P(),
            P(),
        ),
        check_vma=False,
    )
```

time: 1490 us -> 1150 us (0.77)
  Pallas kernels: 77.9 us -> 471 us
  starting transfers between devices: 279 us -> 101 us
  matrix products: 184 us -> 15 us
  blocking collectives: 143 us -> 0 us
  local copies, waits for them, and re-layouts: 204 us -> 70.7 us
  other arithmetic: 189 us -> 80.8 us
    pallas_call x5 -> x67, Pallas kernels: 77.9 us -> 471 us  [the longest x25 181 us: stage(): pl.pallas_call(kernel, grid=(count, 4), in_specs=[pl.BlockSpec(memory_spa...]
    dot_general x22 -> x3, matrix products: 183 us -> 13.4 us  [the longest x2 13.3 us: weight_grad(): lax.dot_general(left, right, (((0,), (0,)), ((), ())), preferred_element_...]
    ppermute x74 -> x25, starting transfers between devices: 202 us -> 34.7 us  [the longest x22 25.4 us: cross(): return lax.ppermute(value, 'z', [(k, k ^ offset) for k in range(LINE)])]
    all_gather x1 -> x0, blocking collectives: 84.6 us -> none  [per_device(): numbers = lax.all_gather(numbers, ('g',) + GROUP, axis=0)]
    ppermute x54 -> x55, waiting for transfers between devices: 123 us -> 178 us  [swap(): return lax.ppermute(value, axis, SWAP)]
    reshape x6 -> x11, local copies, waits for them, and re-layouts: 49.5 us -> 5.91 us  [the longest x2 1.99 us: to_weight_owners(): value = exchange(value.astype(BF16).reshape(4, weight_rows, -1), ('y', 'c'))]
    psum x1 -> x0, blocking collectives: 42.5 us -> none  [per_device(): lax.psum((grad_gain_moe, grad_router, grad_gate_vec, jnp.stack([jnp.sum(v...]
    convert_element_type x48 -> x6, other arithmetic: 42.3 us -> 7.32 us  [the longest x1 2.74 us: from_slots(): arrived = cross(far.astype(BF16), 1)]
  transfers between devices with their start and end apart: 138 -> 86, of which waited for: 48 -> 45; matrix products, arithmetic and copies ran while one was open for 28% -> 12% of each run, Pallas kernels for 4% -> 32%
where the time goes in v2:
time: 1150 us; the launch traced here: 1140 us
  Pallas kernels  471 us (41%)
  waiting for transfers between devices  392 us (34%)
  starting transfers between devices  101 us (9%)
  other arithmetic  80.8 us (7%)
  local copies, waits for them, and re-layouts  70.7 us (6%)
  matrix products  15 us (1%)
    ppermute x22, waiting for transfers between devices, cross(): return lax.ppermute(value, 'z', [(k, k ^ offset) for k in range(LINE)])  210 us
    pallas_call x25, Pallas kernels, stage(): pl.pallas_call(kernel, grid=(count, 4), in_specs=[pl.BlockSpec(memory_spa...  181 us
    ppermute x55, waiting for transfers between devices, swap(): return lax.ppermute(value, axis, SWAP)  178 us
    pallas_call x4, Pallas kernels, weight_sum(): pl.pallas_call(sum_kernel, grid=(parts, steps, steps_of_tiles), in_specs=...  53.6 us
    pallas_call x6, Pallas kernels, combine(): pl.pallas_call(functools.partial(combine_kernel, capacity), grid=(taken,)...  53.4 us
    pallas_call x2, Pallas kernels, run_expert(): pl.pallas_call(functools.partial(expert_kernel, steps), grid=(2 * steps,)...  46.9 us
    ppermute x55, starting transfers between devices, swap(): return lax.ppermute(value, axis, SWAP)  44.4 us
    pallas_call x2, Pallas kernels, moe_in(): pl.pallas_call(functools.partial(moe_in_kernel, (experts, own, held, capa...  33.7 us
  transfers between devices with their start and end apart: 86, of which 45 were waited for; matrix products, arithmetic and copies ran while one was open for 12% of the time, Pallas kernels for 32%

profile of v2, /device:TPU:0, one launch (start us, length us, event | category | flops | bytes accessed | tf_op | source)
XLA Modules:
  0.0 1139.7 jit_solution(17937791591798596493)
XLA Ops:
  31.8 10.8 collective-permute-done.2.second_y
  61.5 22.6 %collective-permute-done.3 = bf16[128,2048]{1,0:T(8,128)(2,1)} collective-permute-done((bf16[128,2048]{1,0:T(8,128)(2,1)S(1)}, bf16[128,2048]{1,0:T(8,128)(2,1)}, u32[]{:S(2)}, u32[]{:S(2)}) %collective-permute-start.3) | collective-permute-done | bytes 524320 | tf_op jit(solution)/shard_map/ppermute | solution.py:35
  86.2 23.1 %collective-permute-done.13 = bf16[512,768]{0,1:T(8,128)(2,1)} collective-permute-done((bf16[512,768]{0,1:T(8,128)(2,1)}, bf16[512,768]{0,1:T(8,128)(2,1)}, u32[]{:S(2)}, u32[]{:S(2)}) %collective-permute-start.13) | collective-permute-done | bytes 786464 | tf_op jit(solution)/shard_map/ppermute | solution.py:35
  125.5 18.7 %collective-permute-done.7.second_y = bf16[4,64,2048]{2,1,0:T(8,128)(2,1)S(1)} collective-permute-done((bf16[4,64,2048]{2,1,0:T(8,128)(2,1)S(1)}, bf16[4,64,2048]{2,1,0:T(8,128)(2,1)S(1)}, u32[]{:S(2)}, u32[]{:S(2)}) %collective-permute-start.7) | collective-permute-done | bytes 1048608 | tf_op jit(solution)/shard_map/ppermute | solution.py:31
  206.4 11.8 %plane.5.marker_ref = bf16[4,512,2048]{2,1,0:T(8,128)(2,1)} custom-call(s32[1]{0:T(128)} %constant.178.clone.1.after_ref, bf16[4,128,2048]{2,1,0:T(8,128)(2,1)} %get-tuple-element.96.first.marker_ref, bf16[4,128,2048]{2,1,0:T(8,128)(2,1)} %collective-permute-done.8.first_y, bf16[4,128,2048]{2,1,0:T(8,128)(2,1)} %get-tuple-element.97.second, ...), custom_call_target="tpu_custom_call" | custom-call | tf_op jit(solution)/shard_map/plane/pallas_call | solution.py:53
  220.7 14.3 %project.2 = (bf16[2048,2048]{1,0:T(8,128)(2,1)}, bf16[2048,768]{1,0:T(8,128)(2,1)}) custom-call(s32[9]{0:T(128)} %concatenate.81.order_ref, bf16[1024,2048]{1,0:T(8,128)(2,1)} %bitcast.405, bf16[1024,2048]{1,0:T(8,128)(2,1)} %bitcast.15.other_ref.rows_ref, bf16[2048,768]{1,0:T(8,128)(2,1)} %copy.136.weight_ref.marker_ref, f32[1,768]{1,0:T(1,128)} %bitcast.482, ...), custom_call_target="tpu_custom_call" | custom-call | flops 6442450944 | bytes 23068672 | tf_op jit(solution)/shard_map/project/pallas_call | solution.py:314
  235.0 11.1 attend.1.act_ref.marker_ref
  262.2 12.1 %collective-permute-done.21.first_y = bf16[1,128,2048]{2,1,0:T(8,128)(2,1)S(1)} collective-permute-done((bf16[1,128,2048]{2,1,0:T(8,128)(2,1)}, bf16[1,128,2048]{2,1,0:T(8,128)(2,1)S(1)}, u32[]{:S(2)}, u32[]{:S(2)}) %collective-permute-start.21) | collective-permute-done | bytes 524320 | tf_op jit(solution)/shard_map/ppermute | solution.py:31
  297.3 20.9 %collective-permute-done.25 = bf16[128,2048]{1,0:T(8,128)(2,1)S(1)} collective-permute-done((bf16[128,2048]{1,0:T(8,128)(2,1)S(1)}, bf16[128,2048]{1,0:T(8,128)(2,1)S(1)}, u32[]{:S(2)}, u32[]{:S(2)}) %collective-permute-start.25) | collective-permute-done | bytes 524320 | tf_op jit(solution)/shard_map/ppermute | solution.py:35
  320.9 10.2 collective-permute-done.27.second_y
  348.9 26.7 %collective-permute-done.28.first_y = bf16[2,128,2048]{2,1,0:T(8,128)(2,1)} collective-permute-done((bf16[2,128,2048]{2,1,0:T(8,128)(2,1)}, bf16[2,128,2048]{2,1,0:T(8,128)(2,1)}, u32[]{:S(2)}, u32[]{:S(2)}) %collective-permute-start.28) | collective-permute-done | bytes 1048608 | tf_op jit(solution)/shard_map/ppermute | solution.py:31
  385.4 29.7 %collective-permute-done.30 = bf16[2,128,2048]{2,1,0:T(8,128)(2,1)} collective-permute-done((bf16[2,128,2048]{2,1,0:T(8,128)(2,1)}, bf16[2,128,2048]{2,1,0:T(8,128)(2,1)}, u32[]{:S(2)}, u32[]{:S(2)}) %collective-permute-start.30) | collective-permute-done | bytes 1048608 | tf_op jit(solution)/shard_map/ppermute | solution.py:35
  449.9 14.6 %collective-permute-done.39.second_x = bf16[2,128,2048]{2,1,0:T(8,128)(2,1)} collective-permute-done((bf16[2,128,2048]{2,1,0:T(8,128)(2,1)}, bf16[2,128,2048]{2,1,0:T(8,128)(2,1)}, u32[]{:S(2)}, u32[]{:S(2)}) %collective-permute-start.39) | collective-permute-done | bytes 1048608 | tf_op jit(solution)/shard_map/ppermute | solution.py:31
  473.0 16.8 %moe_in.2 = (bf16[2048,512]{1,0:T(8,128)(2,1)}, bf16[2048,256]{1,0:T(8,128)(2,1)}, f32[2048,1]{1,0:T(8,128)}, bf16[768,2048]{1,0:T(8,128)(2,1)}, bf16[768,2048]{1,0:T(8,128)(2,1)}, /*index=5*/f32[768,128]{1,0:T(8,128)}) custom-call(s32[1]{0:T(128)S(6)} %add.260.expert_ref, bf16[1024,2048]{1,0:T(8,128)(2,1)} %bitcast.382, ...), custom_call_target="tpu_custom_call" | custom-call | flops 8053063680 | bytes 25165824 | tf_op jit(solution)/shard_map/moe_in/pallas_call | solution.py:596
  489.9 23.5 %run_expert.2 = (bf16[768,2048]{1,0:T(8,128)(2,1)}, bf16[768,2048]{1,0:T(8,128)(2,1)}, bf16[2,768,704]{2,1,0:T(8,128)(2,1)}, bf16[768,704]{1,0:T(8,128)(2,1)}, f32[768,1]{1,0:T(8,128)}) custom-call(s32[1]{0:T(128)} %constant.178.clone.1.after_ref, bf16[768,2048]{1,0:T(8,128)(2,1)} %get-tuple-element.112.rows_ref.refs_2_, ...), custom_call_target="tpu_custom_call" | custom-call | flops 13287555072 | bytes 29884416 | tf_op jit(solution)/shard_map/run_expert/pallas_call | solution.py:682
  541.8 16.9 %moe_in.3 = (bf16[2048,512]{1,0:T(8,128)(2,1)}, bf16[2048,256]{1,0:T(8,128)(2,1)}, f32[2048,1]{1,0:T(8,128)}, bf16[768,2048]{1,0:T(8,128)(2,1)}, bf16[768,2048]{1,0:T(8,128)(2,1)}, /*index=5*/f32[768,128]{1,0:T(8,128)}) custom-call(s32[1]{0:T(128)S(6)} %add.261.expert_ref, bf16[1024,2048]{1,0:T(8,128)(2,1)} %bitcast.89.rows_ref.refs_6_, ...), custom_call_target="tpu_custom_call" | custom-call | flops 8053063680 | bytes 25165824 | tf_op jit(solution)/shard_map/moe_in/pallas_call | solution.py:596
  558.7 23.4 %run_expert.3 = (bf16[768,2048]{1,0:T(8,128)(2,1)}, bf16[768,2048]{1,0:T(8,128)(2,1)}, bf16[2,768,704]{2,1,0:T(8,128)(2,1)}, bf16[768,704]{1,0:T(8,128)(2,1)}, f32[768,1]{1,0:T(8,128)}) custom-call(s32[1]{0:T(128)} %constant.178.clone.1.after_ref, bf16[768,2048]{1,0:T(8,128)(2,1)} %get-tuple-element.119.rows_ref.refs_3_, ...), custom_call_target="tpu_custom_call" | custom-call | flops 13287555072 | bytes 29884416 | tf_op jit(solution)/shard_map/run_expert/pallas_call | solution.py:682
  622.7 11.2 combine.11
  652.5 16.9 %collective-permute-done.45.marker_ref.first_y = bf16[2,128,2048]{2,1,0:T(8,128)(2,1)S(1)} collective-permute-done((bf16[2,128,2048]{2,1,0:T(8,128)(2,1)}, bf16[2,128,2048]{2,1,0:T(8,128)(2,1)S(1)}, u32[]{:S(2)}, u32[]{:S(2)}) %collective-permute-start.45) | collective-permute-done | bytes 1048608 | tf_op jit(solution)/shard_map/ppermute | solution.py:31
  703.4 14.7 %weight_sum.4 = bf16[1,512,2048]{2,1,0:T(8,128)(2,1)} custom-call(s32[1]{0:T(128)} %bitcast.117.after_ref, bf16[1,2048,512]{2,1,0:T(8,128)(2,1)} %bitcast.394, bf16[1,2048,512]{2,1,0:T(8,128)(2,1)} %bitcast.395, bf16[1,2048,512]{2,1,0:T(8,128)(2,1)} %bitcast.396, bf16[1,2048,512]{2,1,0:T(8,128)(2,1)} %bitcast.397, bf16[1024,2048]{1,0:T(8,128)(2,1)} %bitcast.383, ...), custom_call_target="tpu_custom_call" | custom-call | flops 8589934592 | bytes 25165824 | tf_op jit(solution)/shard_map/weight_sum/pallas_call | solution.py:754
  730.3 10.9 weight_sum.5
  758.6 15.3 %collective-permute-done.61.second_y = bf16[1,64,2048]{2,1,0:T(8,128)(2,1)S(1)} collective-permute-done((bf16[1,64,2048]{2,1,0:T(8,128)(2,1)S(1)}, bf16[1,64,2048]{2,1,0:T(8,128)(2,1)S(1)}, u32[]{:S(2)}, u32[]{:S(2)}) %collective-permute-start.61) | collective-permute-done | bytes 262176 | tf_op jit(solution)/shard_map/ppermute | solution.py:31
  779.6 18.6 %collective-permute-done.62.first_y = bf16[1,128,2048]{2,1,0:T(8,128)(2,1)S(1)} collective-permute-done((bf16[1,128,2048]{2,1,0:T(8,128)(2,1)}, bf16[1,128,2048]{2,1,0:T(8,128)(2,1)S(1)}, u32[]{:S(2)}, u32[]{:S(2)}) %collective-permute-start.62) | collective-permute-done | bytes 524320 | tf_op jit(solution)/shard_map/ppermute | solution.py:31
  805.1 11.2 combine.10
  816.3 15.8 %core_sum.8 = (f32[4,128,2048]{2,1,0:T(8,128)}, bf16[4,128,2048]{2,1,0:T(8,128)(2,1)}, f32[4,128,2048]{2,1,0:T(8,128)}, bf16[4,128,2048]{2,1,0:T(8,128)(2,1)}) custom-call(s32[1]{0:T(128)} %constant.178.clone.1.after_ref, bf16[4,512,2048]{2,1,0:T(8,128)(2,1)} %bitcast.377, bf16[4,512,2048]{2,1,0:T(8,128)(2,1)} %collective-permute-done.46.arrived), custom_call_target="tpu_custom_call" | custom-call | tf_op jit(solution)/shard_map/core_sum/pallas_call | solution.py:53
  844.1 18.2 %attend_back.1.act_ref = bf16[2048,768]{1,0:T(8,128)(2,1)} custom-call(bf16[2048,768]{1,0:T(8,128)(2,1)} %get-tuple-element.99.q_ref.k_ref.v_ref, bf16[2048,768]{1,0:T(8,128)(2,1)} %get-tuple-element.99.q_ref.k_ref.v_ref, bf16[2048,768]{1,0:T(8,128)(2,1)} %get-tuple-element.99.q_ref.k_ref.v_ref, bf16[1024,256]{1,0:T(8,128)(2,1)} %get-tuple-element.156.g_ref, ...), custom_call_target="tpu_custom_call" | custom-call | flops 3355443200 | bytes 6291456 | tf_op jit(solution)/shard_map/attend_back/pallas_call | solution.py:509
  880.5 12.1 %pair_sum.7 = (f32[4,64,2048]{2,1,0:T(8,128)}, bf16[4,64,2048]{2,1,0:T(8,128)(2,1)}, f32[4,64,2048]{2,1,0:T(8,128)}, bf16[4,64,2048]{2,1,0:T(8,128)(2,1)}) custom-call(s32[1]{0:T(128)} %constant.178.clone.1.after_ref, f32[4,128,2048]{2,1,0:T(8,128)} %get-tuple-element.132.first.marker_ref, bf16[4,128,2048]{2,1,0:T(8,128)(2,1)} %collective-permute-done.47.first_y, ...), custom_call_target="tpu_custom_call" | custom-call | tf_op jit(solution)/shard_map/pair_sum/pallas_call | solution.py:53
  896.5 11.9 %convolution_convert_fusion = bf16[2048,768]{1,0:T(8,128)(2,1)} fusion(bf16[2048,2048]{1,0:T(8,128)(2,1)} %get-tuple-element.169, bf16[2048,768]{1,0:T(8,128)(2,1)} %attend_back.1.act_ref), kind=kOutput, calls=%fused_computation.5 | convolution fusion | flops 6444023808 | bytes 14680064 | tf_op jit(solution)/shard_map/dot_general | solution.py:1126
  919.6 10.7 last_sum.6
  955.7 28.4 %collective-permute-done.79 = bf16[512,256]{1,0:T(8,128)(2,1)S(1)} collective-permute-done((bf16[512,256]{1,0:T(8,128)(2,1)S(1)}, bf16[512,256]{1,0:T(8,128)(2,1)S(1)}, u32[]{:S(2)}, u32[]{:S(2)}) %collective-permute-start.79) | collective-permute-done | bytes 262176 | tf_op jit(solution)/shard_map/ppermute | solution.py:35
  1032.6 30.9 %collective-permute-done.77 = bf16[512,768]{1,0:T(8,128)(2,1)S(1)} collective-permute-done((bf16[512,768]{1,0:T(8,128)(2,1)}, bf16[512,768]{1,0:T(8,128)(2,1)S(1)}, u32[]{:S(2)}, u32[]{:S(2)}) %collective-permute-start.77) | collective-permute-done | bytes 786464 | tf_op jit(solution)/shard_map/ppermute | solution.py:35
  1099.0 18.0 %weight_sum.6 = f32[2,704,2048]{2,1,0:T(8,128)} custom-call(s32[1]{0:T(128)} %bitcast.166.after_ref, bf16[2,768,704]{2,1,0:T(8,128)(2,1)} %get-tuple-element.171.refs_0_, bf16[2,768,704]{2,1,0:T(8,128)(2,1)} %get-tuple-element.172.refs_1_, bf16[768,2048]{1,0:T(8,128)(2,1)} %get-tuple-element.112.rows_ref.refs_2_, ...), custom_call_target="tpu_custom_call" | custom-call | flops 8858370048 | bytes 22151168 | tf_op jit(solution)/shard_map/weight_sum/pallas_call | solution.py:754
  (586 shorter events, 578.8 us)
Async XLA Ops:
  28.8 55.2 %collective-permute-start.3 = (bf16[128,2048]{1,0:T(8,128)(2,1)S(1)}, bf16[128,2048]{1,0:T(8,128)(2,1)}, u32[]{:S(2)}, u32[]{:S(2)}) collective-permute-start(bf16[128,2048]{1,0:T(8,128)(2,1)S(1)} %copy-done.22), channel_id=1, source_target_pairs={{0,16},{8,24},{16,0},{24,8},{1,17},{9,25},{17,1},{25,9},{2,18},{10... | collective-permute-start | bytes 1572872 | tf_op jit(solution)/shard_map/ppermute | solution.py:35
  31.4 53.1 %collective-permute-start.5 = (bf16[128,2048]{1,0:T(8,128)(2,1)S(1)}, bf16[128,2048]{1,0:T(8,128)(2,1)}, u32[]{:S(2)}, u32[]{:S(2)}) collective-permute-start(bf16[128,2048]{1,0:T(8,128)(2,1)S(1)} %copy-done.22), channel_id=1, source_target_pairs={{0,24},{8,16},{16,8},{24,0},{1,25},{9,17},{17,9},{25,1},{2,26},{10... | collective-permute-start | bytes 1572872 | tf_op jit(solution)/shard_map/ppermute | solution.py:35
  48.1 63.6 %collective-permute-start.11 = (bf16[2,128,2048]{2,1,0:T(8,128)(2,1)}, bf16[2,128,2048]{2,1,0:T(8,128)(2,1)}, u32[]{:S(2)}, u32[]{:S(2)}) collective-permute-start(bf16[2,128,2048]{2,1,0:T(8,128)(2,1)} %get-tuple-element.98.second), channel_id=1, source_target_pairs={{0,1},{1,0},{2,3},{3,2},{4,5},{5,4},{6,7},{7,6},{8,9},{9,8},{10,11... | collective-permute-start | bytes 3145736 | tf_op jit(solution)/shard_map/ppermute | solution.py:31
  49.6 62.1 %collective-permute-start.10 = (bf16[2,128,2048]{2,1,0:T(8,128)(2,1)}, bf16[2,128,2048]{2,1,0:T(8,128)(2,1)}, u32[]{:S(2)}, u32[]{:S(2)}) collective-permute-start(bf16[2,128,2048]{2,1,0:T(8,128)(2,1)} %get-tuple-element.95.marker_ref.first), channel_id=1, source_target_pairs={{0,4},{4,0},{1,5},{5,1},{2,6},{6,2},{3,7},{7,3},{8,12},{12,8},{9,1... | collective-permute-start | bytes 3145736 | tf_op jit(solution)/shard_map/ppermute | solution.py:31
  51.0 58.3 %collective-permute-start.13 = (bf16[512,768]{0,1:T(8,128)(2,1)}, bf16[512,768]{0,1:T(8,128)(2,1)}, u32[]{:S(2)}, u32[]{:S(2)}) collective-permute-start(bf16[512,768]{0,1:T(8,128)(2,1)} %get-tuple-element.273), channel_id=1, source_target_pairs={{0,16},{8,24},{16,0},{24,8},{1,17},{9,25},{17,1},{25,9},{2,18},{10... | collective-permute-start | bytes 2359304 | tf_op jit(solution)/shard_map/ppermute | solution.py:35
  84.0 35.7 %collective-permute-start.15 = (s32[10,256]{1,0:T(8,128)S(1)}, s32[10,256]{1,0:T(8,128)S(1)}, u32[]{:S(2)}, u32[]{:S(2)}) collective-permute-start(s32[10,256]{1,0:T(8,128)S(1)} %add_add_fusion.1), channel_id=1, source_target_pairs={{0,4},{4,0},{1,5},{5,1},{2,6},{6,2},{3,7},{7,3},{8,12},{12,8},{9,1... | collective-permute-start | bytes 30728 | tf_op jit(solution)/shard_map/ppermute | solution.py:31
  111.7 48.1 %collective-permute-start.14 = (bf16[2,512,768]{1,2,0:T(8,128)(2,1)}, bf16[2,512,768]{1,2,0:T(8,128)(2,1)}, u32[]{:S(2)}, u32[]{:S(2)}) collective-permute-start(bf16[2,512,768]{1,2,0:T(8,128)(2,1)} %pad_maximum_fusion.2), channel_id=1, source_target_pairs={{0,8},{8,0},{16,24},{24,16},{1,9},{9,1},{17,25},{25,17},{2,10},{10... | collective-permute-start | bytes 4718600 | tf_op jit(solution)/shard_map/ppermute | solution.py:35
  118.3 102.4 %collective-permute-start.12 = (bf16[2,512,2048]{2,1,0:T(8,128)(2,1)}, bf16[2,512,2048]{2,1,0:T(8,128)(2,1)}, u32[]{:S(2)}, u32[]{:S(2)}) collective-permute-start(bf16[2,512,2048]{2,1,0:T(8,128)(2,1)} %plane.6), channel_id=1, source_target_pairs={{0,2},{2,0},{1,3},{3,1},{4,6},{6,4},{5,7},{7,5},{8,10},{10,8},{9,1... | collective-permute-start | bytes 12582920 | tf_op jit(solution)/shard_map/ppermute | solution.py:31
  157.7 48.7 %collective-permute-start.8 = (bf16[4,128,2048]{2,1,0:T(8,128)(2,1)}, bf16[4,128,2048]{2,1,0:T(8,128)(2,1)}, u32[]{:S(2)}, u32[]{:S(2)}) collective-permute-start(bf16[4,128,2048]{2,1,0:T(8,128)(2,1)} %get-tuple-element.96.first.marker_ref), channel_id=1, source_target_pairs={{0,4},{4,0},{1,5},{5,1},{2,6},{6,2},{3,7},{7,3},{8,12},{12,8},{9,1... | collective-permute-start | bytes 6291464 | tf_op jit(solution)/shard_map/ppermute | solution.py:31
  159.2 47.2 %collective-permute-start.9 = (bf16[4,128,2048]{2,1,0:T(8,128)(2,1)}, bf16[4,128,2048]{2,1,0:T(8,128)(2,1)}, u32[]{:S(2)}, u32[]{:S(2)}) collective-permute-start(bf16[4,128,2048]{2,1,0:T(8,128)(2,1)} %get-tuple-element.97.second), channel_id=1, source_target_pairs={{0,1},{1,0},{2,3},{3,2},{4,5},{5,4},{6,7},{7,6},{8,9},{9,8},{10,11... | collective-permute-start | bytes 6291464 | tf_op jit(solution)/shard_map/ppermute | solution.py:31
  283.9 189.2 %collective-permute-start.34 = (bf16[4,512,2048]{2,1,0:T(8,128)(2,1)}, bf16[4,512,2048]{2,1,0:T(8,128)(2,1)}, u32[]{:S(2)}, u32[]{:S(2)}) collective-permute-start(bf16[4,512,2048]{2,1,0:T(8,128)(2,1)} %plane.5.marker_ref), channel_id=1, source_target_pairs={{0,2},{2,0},{1,3},{3,1},{4,6},{6,4},{5,7},{7,5},{8,10},{10,8},{9,1... | collective-permute-start | bytes 25165832 | tf_op jit(solution)/shard_map/ppermute | solution.py:31
  338.4 37.2 %collective-permute-start.28 = (bf16[2,128,2048]{2,1,0:T(8,128)(2,1)}, bf16[2,128,2048]{2,1,0:T(8,128)(2,1)}, u32[]{:S(2)}, u32[]{:S(2)}) collective-permute-start(bf16[2,128,2048]{2,1,0:T(8,128)(2,1)} %get-tuple-element.108.first), channel_id=1, source_target_pairs={{0,4},{4,0},{1,5},{5,1},{2,6},{6,2},{3,7},{7,3},{8,12},{12,8},{9,1... | collective-permute-start | bytes 3145736 | tf_op jit(solution)/shard_map/ppermute | solution.py:31
  339.5 36.1 %collective-permute-start.29 = (bf16[2,128,2048]{2,1,0:T(8,128)(2,1)}, bf16[2,128,2048]{2,1,0:T(8,128)(2,1)}, u32[]{:S(2)}, u32[]{:S(2)}) collective-permute-start(bf16[2,128,2048]{2,1,0:T(8,128)(2,1)} %get-tuple-element.109.second), channel_id=1, source_target_pairs={{0,1},{1,0},{2,3},{3,2},{4,5},{5,4},{6,7},{7,6},{8,9},{9,8},{10,11... | collective-permute-start | bytes 3145736 | tf_op jit(solution)/shard_map/ppermute | solution.py:31
  344.6 99.8 %all-to-all-start.1 = ((bf16[16,528,128]{2,1,0:T(8,128)(2,1)}), bf16[16,528,128]{2,1,0:T(8,128)(2,1)S(1)}, u32[]{:S(2)}, u32[]{:S(2)}) async-start(bf16[16,528,128]{2,1,0:T(8,128)(2,1)} %maximum_select_fusion.1), calls=%async_computation.1 | async-start | bytes 4325376 | tf_op jit(solution)/shard_map/all_to_all | solution.py:233
  382.3 90.7 %collective-permute-start.33 = (bf16[2,512,2048]{2,1,0:T(8,128)(2,1)}, bf16[2,512,2048]{2,1,0:T(8,128)(2,1)}, u32[]{:S(2)}, u32[]{:S(2)}) collective-permute-start(bf16[2,512,2048]{2,1,0:T(8,128)(2,1)} %plane.7.marker_ref), channel_id=1, source_target_pairs={{0,2},{2,0},{1,3},{3,1},{4,6},{6,4},{5,7},{7,5},{8,10},{10,8},{9,1... | collective-permute-start | bytes 12582920 | tf_op jit(solution)/shard_map/ppermute | solution.py:31
  540.2 41.8 %collective-permute-start.42 = (bf16[2,128,2048]{2,1,0:T(8,128)(2,1)}, bf16[2,128,2048]{2,1,0:T(8,128)(2,1)S(1)}, u32[]{:S(2)}, u32[]{:S(2)}) collective-permute-start(bf16[2,128,2048]{2,1,0:T(8,128)(2,1)} %get-tuple-element.123), channel_id=1, source_target_pairs={{0,4},{4,0},{1,5},{5,1},{2,6},{6,2},{3,7},{7,3},{8,12},{12,8},{9,1... | collective-permute-start | bytes 3145736 | tf_op jit(solution)/shard_map/ppermute | solution.py:31
  540.7 41.4 %collective-permute-start.43 = (bf16[2,128,2048]{2,1,0:T(8,128)(2,1)}, bf16[2,128,2048]{2,1,0:T(8,128)(2,1)S(1)}, u32[]{:S(2)}, u32[]{:S(2)}) collective-permute-start(bf16[2,128,2048]{2,1,0:T(8,128)(2,1)} %get-tuple-element.125), channel_id=1, source_target_pairs={{0,1},{1,0},{2,3},{3,2},{4,5},{5,4},{6,7},{7,6},{8,9},{9,8},{10,11... | collective-permute-start | bytes 3145736 | tf_op jit(solution)/shard_map/ppermute | solution.py:31
  599.7 34.8 %collective-permute-start.44 = (bf16[2,512,2048]{2,1,0:T(8,128)(2,1)}, bf16[2,512,2048]{2,1,0:T(8,128)(2,1)}, u32[]{:S(2)}, u32[]{:S(2)}) collective-permute-start(bf16[2,512,2048]{2,1,0:T(8,128)(2,1)} %bitcast.403), channel_id=1, source_target_pairs={{0,2},{2,0},{1,3},{3,1},{4,6},{6,4},{5,7},{7,5},{8,10},{10,8},{9,1... | collective-permute-start | bytes 12582920 | tf_op jit(solution)/shard_map/ppermute | solution.py:31
  633.9 182.4 %collective-permute-start.46 = (bf16[4,512,2048]{2,1,0:T(8,128)(2,1)}, bf16[4,512,2048]{2,1,0:T(8,128)(2,1)}, u32[]{:S(2)}, u32[]{:S(2)}) collective-permute-start(bf16[4,512,2048]{2,1,0:T(8,128)(2,1)} %bitcast.398), channel_id=1, source_target_pairs={{0,2},{2,0},{1,3},{3,1},{4,6},{6,4},{5,7},{7,5},{8,10},{10,8},{9,1... | collective-permute-start | bytes 25165832 | tf_op jit(solution)/shard_map/ppermute | solution.py:31
  744.3 118.0 %all-to-all-start.3 = ((bf16[16,528,128]{2,1,0:T(8,128)(2,1)}), bf16[16,528,128]{2,1,0:T(8,128)(2,1)S(1)}, u32[]{:S(2)}, u32[]{:S(2)}) async-start(bf16[16,528,128]{2,1,0:T(8,128)(2,1)} %maximum_bitcast_fusion), calls=%async_computation.3 | async-start | bytes 4325376 | tf_op jit(solution)/shard_map/all_to_all | solution.py:233
  832.0 48.4 %collective-permute-start.47 = (bf16[4,128,2048]{2,1,0:T(8,128)(2,1)}, bf16[4,128,2048]{2,1,0:T(8,128)(2,1)}, u32[]{:S(2)}, u32[]{:S(2)}) collective-permute-start(bf16[4,128,2048]{2,1,0:T(8,128)(2,1)} %get-tuple-element.133), channel_id=1, source_target_pairs={{0,4},{4,0},{1,5},{5,1},{2,6},{6,2},{3,7},{7,3},{8,12},{12,8},{9,1... | collective-permute-start | bytes 6291464 | tf_op jit(solution)/shard_map/ppermute | solution.py:31
  832.0 48.4 %collective-permute-start.48 = (bf16[4,128,2048]{2,1,0:T(8,128)(2,1)}, bf16[4,128,2048]{2,1,0:T(8,128)(2,1)}, u32[]{:S(2)}, u32[]{:S(2)}) collective-permute-start(bf16[4,128,2048]{2,1,0:T(8,128)(2,1)} %get-tuple-element.135), channel_id=1, source_target_pairs={{0,1},{1,0},{2,3},{3,2},{4,5},{5,4},{6,7},{7,6},{8,9},{9,8},{10,11... | collective-permute-start | bytes 6291464 | tf_op jit(solution)/shard_map/ppermute | solution.py:31
  875.2 69.1 %collective-permute-start.65 = (bf16[2,512,2048]{2,1,0:T(8,128)(2,1)}, bf16[2,512,2048]{2,1,0:T(8,128)(2,1)}, u32[]{:S(2)}, u32[]{:S(2)}) collective-permute-start(bf16[2,512,2048]{2,1,0:T(8,128)(2,1)} %bitcast.485), channel_id=1, source_target_pairs={{0,2},{2,0},{1,3},{3,1},{4,6},{6,4},{5,7},{7,5},{8,10},{10,8},{9,1... | collective-permute-start | bytes 12582920 | tf_op jit(solution)/shard_map/ppermute | solution.py:31
  914.7 90.7 %collective-permute-start.76 = (bf16[2,512,768]{2,1,0:T(8,128)(2,1)}, bf16[2,512,768]{2,1,0:T(8,128)(2,1)S(1)}, u32[]{:S(2)}, u32[]{:S(2)}) collective-permute-start(bf16[2,512,768]{2,1,0:T(8,128)(2,1)} %dynamic-slice_bitcast_fusion), channel_id=1, source_target_pairs={{0,8},{8,0},{16,24},{24,16},{1,9},{9,1},{17,25},{25,17},{2,10},{10... | collective-permute-start | bytes 4718600 | tf_op jit(solution)/shard_map/ppermute | solution.py:35
  933.2 55.2 %collective-permute-start.51 = (bf16[2,128,2048]{2,1,0:T(8,128)(2,1)}, bf16[2,128,2048]{2,1,0:T(8,128)(2,1)}, u32[]{:S(2)}, u32[]{:S(2)}) collective-permute-start(bf16[2,128,2048]{2,1,0:T(8,128)(2,1)} %slice.460), channel_id=1, source_target_pairs={{0,8},{8,0},{16,24},{24,16},{1,9},{9,1},{17,25},{25,17},{2,10},{10... | collective-permute-start | bytes 3145736 | tf_op jit(solution)/shard_map/ppermute | solution.py:35
  933.3 50.7 %collective-permute-start.79 = (bf16[512,256]{1,0:T(8,128)(2,1)S(1)}, bf16[512,256]{1,0:T(8,128)(2,1)S(1)}, u32[]{:S(2)}, u32[]{:S(2)}) collective-permute-start(bf16[512,256]{1,0:T(8,128)(2,1)S(1)} %fusion.35), channel_id=1, source_target_pairs={{0,16},{8,24},{16,0},{24,8},{1,17},{9,25},{17,1},{25,9},{2,18},{10... | collective-permute-start | bytes 786440 | tf_op jit(solution)/shard_map/ppermute | solution.py:35
  953.1 37.5 %collective-permute-start.66 = (bf16[2,128,2048]{2,1,0:T(8,128)(2,1)}, bf16[2,128,2048]{2,1,0:T(8,128)(2,1)}, u32[]{:S(2)}, u32[]{:S(2)}) collective-permute-start(bf16[2,128,2048]{2,1,0:T(8,128)(2,1)} %get-tuple-element.160), channel_id=1, source_target_pairs={{0,4},{4,0},{1,5},{5,1},{2,6},{6,2},{3,7},{7,3},{8,12},{12,8},{9,1... | collective-permute-start | bytes 3145736 | tf_op jit(solution)/shard_map/ppermute | solution.py:31
  953.8 36.8 %collective-permute-start.67 = (bf16[2,128,2048]{2,1,0:T(8,128)(2,1)}, bf16[2,128,2048]{2,1,0:T(8,128)(2,1)}, u32[]{:S(2)}, u32[]{:S(2)}) collective-permute-start(bf16[2,128,2048]{2,1,0:T(8,128)(2,1)} %get-tuple-element.162), channel_id=1, source_target_pairs={{0,1},{1,0},{2,3},{3,2},{4,5},{5,4},{6,7},{7,6},{8,9},{9,8},{10,11... | collective-permute-start | bytes 3145736 | tf_op jit(solution)/shard_map/ppermute | solution.py:31
  985.0 45.5 %all-to-all-start.5 = ((bf16[4,128,256]{1,2,0:T(8,128)(2,1)}), bf16[4,128,256]{1,2,0:T(8,128)(2,1)S(1)}, u32[]{:S(2)}, u32[]{:S(2)}) async-start(bf16[4,128,256]{1,2,0:T(8,128)(2,1)} %copy.162), calls=%async_computation.5 | async-start | bytes 524288 | tf_op jit(solution)/shard_map/all_to_all | solution.py:233
  1002.1 67.8 %collective-permute-start.52 = (bf16[128,2048]{1,0:T(8,128)(2,1)}, bf16[128,2048]{1,0:T(8,128)(2,1)}, u32[]{:S(2)}, u32[]{:S(2)}) collective-permute-start(bf16[128,2048]{1,0:T(8,128)(2,1)} %fusion.28), channel_id=1, source_target_pairs={{0,16},{8,24},{16,0},{24,8},{1,17},{9,25},{17,1},{25,9},{2,18},{10... | collective-permute-start | bytes 1572872 | tf_op jit(solution)/shard_map/ppermute | solution.py:35
  1008.9 54.6 %collective-permute-start.77 = (bf16[512,768]{1,0:T(8,128)(2,1)}, bf16[512,768]{1,0:T(8,128)(2,1)S(1)}, u32[]{:S(2)}, u32[]{:S(2)}) collective-permute-start(bf16[512,768]{1,0:T(8,128)(2,1)} %fusion.26), channel_id=1, source_target_pairs={{0,16},{8,24},{16,0},{24,8},{1,17},{9,25},{17,1},{25,9},{2,18},{10... | collective-permute-start | bytes 2359304 | tf_op jit(solution)/shard_map/ppermute | solution.py:35
  1022.5 47.4 %collective-permute-start.70 = (bf16[128,2048]{1,0:T(8,128)(2,1)}, bf16[128,2048]{1,0:T(8,128)(2,1)}, u32[]{:S(2)}, u32[]{:S(2)}) collective-permute-start(bf16[128,2048]{1,0:T(8,128)(2,1)} %fusion.30), channel_id=1, source_target_pairs={{8,0},{16,8},{24,16},{9,1},{17,9},{25,17},{10,2},{18,10},{26,18},{... | collective-permute-start | bytes 1572872 | tf_op jit(solution)/shard_map/ppermute | solution.py:1120
  (154 other events, 2052.8 us)

commit v3 on v2

--- a/solution.py
+++ b/solution.py
@@ -17,7 +17,6 @@
 MASKED = -1e30
 
 LINE = 4
-OFFSETS = (0, 2, 1, 3)
 GROUP = ("z", "y", "c")
 EVERY = ("g", "z", "y", "c", "x")
 SWAP = [(0, 1), (1, 0)]
@@ -43,25 +42,38 @@
     return take(value, index, dim), take(value, 1 - index, dim)
 
 
+ANYWHERE = pl.BlockSpec(memory_space=pl.ANY)
+
+
+def without(count, kernel, first=0):
+    def run(*refs):
+        kernel(*refs[:first], *refs[first + count :])
+
+    return run
+
+
 def stage(kernel, after, inputs, outputs, name):
     count, _, width = inputs[0].shape
-    part = width // 4
+    parts = max(1, 4 // count)
 
     def spec(rows):
-        return pl.BlockSpec((1, rows, part), lambda i, j: (i, 0, j))
+        return pl.BlockSpec((1, rows, width // parts), lambda i, j: (i, 0, j))
 
     return pl.pallas_call(
-        kernel,
-        grid=(count, 4),
-        in_specs=[pl.BlockSpec(memory_space=pltpu.SMEM)] + [spec(v.shape[1]) for v in inputs],
+        without(len(after), kernel),
+        grid=(count, parts),
+        in_specs=[ANYWHERE] * len(after) + [spec(v.shape[1]) for v in inputs],
         out_specs=[spec(rows) for rows, _ in outputs],
         out_shape=[jax.ShapeDtypeStruct((count, rows, width), kind) for rows, kind in outputs],
         compiler_params=pltpu.CompilerParams(vmem_limit_bytes=VMEM_LIMIT),
+        cost_estimate=pl.CostEstimate(
+            flops=0, bytes_accessed=8 * count * width * sum(rows for rows, _ in outputs), transcendentals=0
+        ),
         name=name,
-    )(after.reshape(1), *inputs)
-
-
-def pair_kernel(after_ref, first, first_x, second, second_y, out_first, out_second):
+    )(*after, *inputs)
+
+
+def pair_kernel(first, first_x, second, second_y, out_first, out_second):
     half = first.shape[1]
     out_first[0, :half] = first[0]
     out_first[0, half:] = first_x[0]
@@ -69,7 +81,7 @@
     out_second[0, half:] = second_y[0]
 
 
-def plane_kernel(after_ref, first, first_y, second, second_x, out):
+def plane_kernel(first, first_y, second, second_x, out):
     rows = first.shape[1]
     half = rows // 2
     for y, source in enumerate((first, first_y)):
@@ -80,28 +92,39 @@
             out[0, start : start + half] = source[0, y * half : (y + 1) * half]
 
 
-def slot_gather(shards, after_pair, after_plane):
+def slot_pair(shards, after):
     rows = shards.shape[1]
     half = rows // 2
     first, second = shards[:, :half], shards[:, half:]
-    first, second = stage(
+    pairs = stage(
         pair_kernel,
-        after_pair,
+        after,
         [first, swap(first, "x"), second, swap(second, "y")],
         [(rows, BF16)] * 2,
         "pair",
     )
-    (own,) = stage(
-        plane_kernel,
-        after_plane,
-        [first, swap(first, "y"), second, swap(second, "x")],
-        [(4 * rows, BF16)],
-        "plane",
-    )
-    return (own, swap(own, "c")), (first, own)
-
-
-def core_sum_kernel(after_ref, keep, arrived, first, first_send, second, second_send):
+    arrived = swap(pairs[0], "y"), swap(pairs[1], "x")
+
+    def plane(after):
+        (own,) = stage(
+            plane_kernel,
+            after,
+            [pairs[0], arrived[0], pairs[1], arrived[1]],
+            [(4 * rows, BF16)],
+            "plane",
+        )
+        return own, swap(own, "c")
+
+    return pairs, plane, arrived
+
+
+def slot_gather(shards, after_pair, after_plane):
+    pairs, plane, _ = slot_pair(shards, after_pair)
+    halves = plane(after_plane)
+    return halves, (pairs[0], halves[0])
+
+
+def core_sum_kernel(keep, arrived, first, first_send, second, second_send):
     rows = first.shape[1]
     half = rows // 2
 
@@ -117,7 +140,7 @@
         second_send[0, y * half : (y + 1) * half] = total(start + half, half).astype(BF16)
 
 
-def pair_sum_kernel(after_ref, first, first_y, second, second_x, first_keep, first_send, second_keep, second_send):
+def pair_sum_kernel(first, first_y, second, second_x, first_keep, first_send, second_keep, second_send):
     half = first_keep.shape[1]
     for value, arrived, keep, send in (
         (first, first_y, first_keep, first_send),
@@ -127,38 +150,47 @@
         send[0] = (value[0, half:] + arrived[0, half:].astype(F32)).astype(BF16)
 
 
-def last_sum_kernel(after_ref, first, first_x, second, second_y, out):
+def last_sum_kernel(first, first_x, second, second_y, out):
     half = first.shape[1]
     out[0, :half] = first[0] + first_x[0].astype(F32)
     out[0, half:] = second[0] + second_y[0].astype(F32)
 
 
-def slot_scatter(keep, send, after_core, after_pair, after_last):
+def scatter_core(keep, send, after):
     rows = keep.shape[1] // 4
     first, first_send, second, second_send = stage(
         core_sum_kernel,
-        after_core,
+        after,
         [keep, swap(send, "c")],
         [(rows, F32), (rows, BF16)] * 2,
         "core_sum",
     )
-    first_y, second_x = swap(first_send, "y"), swap(second_send, "x")
-    first_keep, first_send, second_keep, second_send = stage(
+    return first, swap(first_send, "y"), second, swap(second_send, "x")
+
+
+def scatter_pair(steps, after):
+    half = steps[0].shape[1] // 2
+    first, first_send, second, second_send = stage(
         pair_sum_kernel,
-        after_pair,
-        [first, first_y, second, second_x],
-        [(rows // 2, F32), (rows // 2, BF16)] * 2,
+        after,
+        list(steps),
+        [(half, F32), (half, BF16)] * 2,
         "pair_sum",
     )
-    first_x, second_y = swap(first_send, "x"), swap(second_send, "y")
+    return first, swap(first_send, "x"), second, swap(second_send, "y")
+
+
+def scatter_last(steps, after):
     (whole,) = stage(
-        last_sum_kernel,
-        after_last,
-        [first_keep, first_x, second_keep, second_y],
-        [(rows, F32)],
-        "last_sum",
-    )
-    return whole, (first, first_y, first_keep, first_x)
+        last_sum_kernel, after, list(steps), [(2 * steps[0].shape[1], F32)], "last_sum"
+    )
+    return whole
+
+
+def slot_scatter(keep, send, after_core, after_pair, after_last):
+    core = scatter_core(keep, send, after_core)
+    pair = scatter_pair(core, after_pair)
+    return scatter_last(pair, after_last), (core[0], core[1], pair[0], pair[1])
 
 
 def tick_kernel(marker_ref, out_ref):
@@ -196,19 +228,8 @@
     return jnp.where(index == 0, value, jnp.flip(value, dim))
 
 
-def slot_shards(shard):
-    return jnp.stack([shard] + [cross(shard, offset) for offset in OFFSETS[1:]])
-
-
-def from_slots(near, far):
-    arrived = cross(far.astype(BF16), 1)
-    pair = near + arrived.astype(F32)
-    return pair[0] + cross(pair[1].astype(BF16), 2).astype(F32), arrived
-
-
-def gather_line(value, flag):
+def gather_line(value, across):
     z = lax.axis_index("z")
-    across = cross(value, 2)
     others = cross(jnp.stack([value, across]), 1)
     held = [[value, others[0]], [across, others[1]]]
     placed = []
@@ -216,17 +237,18 @@
         for low in range(2):
             rows = [jnp.where(z % 2 == low, held[k][0], held[k][1]) for k in range(2)]
             placed.append(jnp.where(z // 2 == high, rows[0], rows[1]))
-    return hold(jnp.concatenate(placed, 0), flag)
+    return jnp.concatenate(placed, 0), others
 
 
 def scatter_line(value):
     z = lax.axis_index("z")
     parts = value.reshape(2, 2, -1, value.shape[-1])
     keep, send = split(parts, z % 2, 1)
-    arrived = cross(send, 1)
-    keep = keep.astype(F32) + arrived.astype(F32)
+    marks = [send, cross(send, 1)]
+    keep = keep.astype(F32) + marks[1].astype(F32)
     keep, send = split(keep, z // 2, 0)
-    return keep + cross(send.astype(BF16), 2).astype(F32), arrived
+    marks.append(cross(send.astype(BF16), 2))
+    return (keep + marks[2].astype(F32)).astype(BF16), marks
 
 
 def exchange(value, axes):
@@ -288,7 +310,7 @@
     ).astype(BF16)
 
 
-def project(order, halves, weight, bias=None, cosine=None, sine=None):
+def project(after, order, halves, weight, bias=None, cosine=None, sine=None):
     slots, half_rows, model = halves[0].shape
     halves = [half.reshape(slots * half_rows, model) for half in halves]
     count = 2 * slots * half_rows
@@ -312,11 +334,11 @@
         specs = arrived + [whole, row, placed(HEAD), placed(HEAD)]
         extra = (bias, cosine, sine)
     return pl.pallas_call(
-        kernel,
+        without(len(after), kernel, 1),
         grid_spec=pltpu.PrefetchScalarGridSpec(
             num_scalar_prefetch=1,
             grid=(2 * steps,),
-            in_specs=specs,
+            in_specs=[ANYWHERE] * len(after) + specs,
             out_specs=[placed(model), placed(width)],
         ),
         out_shape=[
@@ -325,12 +347,12 @@
         ],
         compiler_params=pltpu.CompilerParams(vmem_limit_bytes=VMEM_LIMIT),
         cost_estimate=pl.CostEstimate(
-            flops=2 * count * model * width,
+            flops=3 * (2 * count * model * width),
             bytes_accessed=2 * (2 * count * model + model * width + count * width),
             transcendentals=0,
         ),
         name="project",
-    )(order, *halves, weight, *extra)
+    )(order, *after, *halves, weight, *extra)
 
 
 def spread_kernel(order_ref, act_ref, weight_ref, rows_ref, out_ref, sum_ref, held_ref):
@@ -353,7 +375,7 @@
     out_ref[...] = jnp.dot(held_ref[...], weight_ref[...], preferred_element_type=F32).astype(BF16)
 
 
-def spread(order, act, weight, core, rows=None):
+def spread(after, order, act, weight, core, rows=None):
     count, inner = act.shape
     model = weight.shape[1]
     slots = order.shape[0] // 4
@@ -366,25 +388,25 @@
     ]
     out_specs = [pl.BlockSpec((step, model), lambda i, order: (i, 0))]
     out_shape = [jax.ShapeDtypeStruct((count // 2, model), BF16)]
-    operands = (order, act, weight)
+    operands = (order, *after, act, weight)
     if rows is not None:
         specs.append(pl.BlockSpec((step, model), lambda i, order: (i, 0)))
         out_specs.append(pl.BlockSpec((1, model), lambda i, order: (0, 0)))
         out_shape.append(jax.ShapeDtypeStruct((1, model), F32))
         operands = operands + (rows.reshape(count // 2, model),)
     results = pl.pallas_call(
-        spread_plain_kernel if rows is None else spread_kernel,
+        without(len(after), spread_plain_kernel if rows is None else spread_kernel, 1),
         grid_spec=pltpu.PrefetchScalarGridSpec(
             num_scalar_prefetch=1,
             grid=(2 * slots,),
-            in_specs=specs,
+            in_specs=[ANYWHERE] * len(after) + specs,
             out_specs=out_specs,
             scratch_shapes=[pltpu.VMEM((step, inner), BF16)],
         ),
         out_shape=out_shape,
         compiler_params=pltpu.CompilerParams(vmem_limit_bytes=VMEM_LIMIT),
         cost_estimate=pl.CostEstimate(
-            flops=count * model * inner,
+            flops=3 * (count * model * inner),
             bytes_accessed=2 * (count * model + model * inner),
             transcendentals=0,
         ),
@@ -433,16 +455,17 @@
     ]
 
 
-def attend(projected, seg_q, seg_k, valid_k):
+def attend(after, projected, seg_q, seg_k, valid_k):
     held, width = projected.shape
     count, width = held // 2, width // 3
     step = count // 4
     heads = width // HEAD
     flops = 4 * count * (step + count) * width
     return pl.pallas_call(
-        functools.partial(attend_kernel, step, count),
+        without(len(after), functools.partial(attend_kernel, step, count)),
         grid=(heads, 4),
-        in_specs=head_specs(held, step, heads)
+        in_specs=[ANYWHERE] * len(after)
+        + head_specs(held, step, heads)
         + [
             pl.BlockSpec((step, 1), lambda h, i: (i, 0)),
             pl.BlockSpec((1, held), lambda h, i: (0, 0)),
@@ -452,10 +475,10 @@
         out_shape=jax.ShapeDtypeStruct((count, width), BF16),
         compiler_params=pltpu.CompilerParams(vmem_limit_bytes=VMEM_LIMIT),
         cost_estimate=pl.CostEstimate(
-            flops=flops, bytes_accessed=8 * held * width, transcendentals=flops // (4 * HEAD)
+            flops=9 * (flops), bytes_accessed=8 * held * width, transcendentals=flops // (4 * HEAD)
         ),
         name="attend",
-    )(projected, projected, projected, seg_q, seg_k, valid_k)
+    )(*after, projected, projected, projected, seg_q, seg_k, valid_k)
 
 
 def attend_back_kernel(
@@ -500,16 +523,17 @@
         out_ref[:, columns[2]] = dv_ref[...].astype(BF16)
 
 
-def attend_back(projected, grad, seg_q, seg_k, valid_k, cosine, sine):
+def attend_back(after, projected, grad, seg_q, seg_k, valid_k, cosine, sine):
     held, width = projected.shape
     count, width = held // 2, width // 3
     step = count // 4
     heads = width // HEAD
     flops = 10 * count * (step + count) * width
     return pl.pallas_call(
-        functools.partial(attend_back_kernel, step, count, heads),
+        without(len(after), functools.partial(attend_back_kernel, step, count, heads)),
         grid=(heads, 4),
-        in_specs=head_specs(held, step, heads)
+        in_specs=[ANYWHERE] * len(after)
+        + head_specs(held, step, heads)
         + [
             pl.BlockSpec((step, HEAD), lambda h, i: (i, h)),
             pl.BlockSpec((step, 1), lambda h, i: (i, 0)),
@@ -523,10 +547,10 @@
         scratch_shapes=[pltpu.VMEM((held, HEAD), F32)] * 2,
         compiler_params=pltpu.CompilerParams(vmem_limit_bytes=VMEM_LIMIT),
         cost_estimate=pl.CostEstimate(
-            flops=flops, bytes_accessed=12 * held * width, transcendentals=flops // (10 * HEAD)
+            flops=6 * (flops), bytes_accessed=12 * held * width, transcendentals=flops // (10 * HEAD)
         ),
         name="attend_back",
-    )(projected, projected, projected, grad, seg_q, seg_k, valid_k, cosine, sine)
+    )(*after, projected, projected, projected, grad, seg_q, seg_k, valid_k, cosine, sine)
 
 
 def one_hot(slot_row, capacity):
@@ -573,7 +597,7 @@
     )
 
 
-def moe_in(expert, rows, grads, chunk, w_in, w_dn, slot_rows, experts, own, capacity):
+def moe_in(after, expert, rows, grads, chunk, w_in, w_dn, slot_rows, experts, own, capacity):
     blocks, _, step = slot_rows.shape
     model = rows[0].shape[1]
     held = w_dn.shape[0]
@@ -594,9 +618,10 @@
         return pl.BlockSpec((step, model), lambda i: (block(i), 0))
 
     return pl.pallas_call(
-        functools.partial(moe_in_kernel, (experts, own, held, capacity)),
+        without(len(after), functools.partial(moe_in_kernel, (experts, own, held, capacity))),
         grid=(blocks,),
-        in_specs=[
+        in_specs=[ANYWHERE] * len(after)
+        + [
             pl.BlockSpec(memory_space=pltpu.SMEM),
             row_spec(0),
             row_spec(1),
@@ -624,12 +649,12 @@
         ],
         compiler_params=pltpu.CompilerParams(vmem_limit_bytes=VMEM_LIMIT),
         cost_estimate=pl.CostEstimate(
-            flops=2 * count * model * (3 * held + 2 * capacity),
+            flops=2 * (2 * count * model * (3 * held + 2 * capacity)),
             bytes_accessed=6 * count * model,
             transcendentals=2 * count * held,
         ),
         name="moe_in",
-    )(expert, *rows, *grads, w_in, w_dn, slot_rows)
+    )(*after, expert, *rows, *grads, w_in, w_dn, slot_rows)
 
 
 def dot_nt(left, right):
@@ -637,7 +662,7 @@
 
 
 def expert_kernel(
-    steps, after_ref, rows_ref, grad_ref, gate_ref, wgu_ref, wd_ref,
+    steps, rows_ref, grad_ref, gate_ref, wgu_ref, wd_ref,
     back_ref, out_ref, dgu_ref, hid_ref, ggate_ref, acc_g, acc_u, acc_r,
 ):
     step = pl.program_id(0)
@@ -680,10 +705,10 @@
     steps = 4
     chunk = model // steps
     return pl.pallas_call(
-        functools.partial(expert_kernel, steps),
+        without(len(after), functools.partial(expert_kernel, steps)),
         grid=(2 * steps,),
-        in_specs=[
-            pl.BlockSpec(memory_space=pltpu.SMEM),
+        in_specs=[ANYWHERE] * len(after)
+        + [
             pl.BlockSpec((count, chunk), lambda i: (0, jnp.minimum(i, steps - 1))),
             pl.BlockSpec((count, chunk), lambda i: (0, jnp.minimum(i, steps - 1))),
             pl.BlockSpec((count, HEAD), lambda i: (0, 0)),
@@ -707,15 +732,15 @@
         scratch_shapes=[pltpu.VMEM((count, cols), F32)] * 3,
         compiler_params=pltpu.CompilerParams(vmem_limit_bytes=VMEM_LIMIT),
         cost_estimate=pl.CostEstimate(
-            flops=12 * count * model * cols,
+            flops=2 * (12 * count * model * cols),
             bytes_accessed=8 * count * model + 12 * model * cols,
             transcendentals=count * cols,
         ),
         name="run_expert",
-    )(after.reshape(1), rows, grad, gates, w_gu, w_down)
-
-
-def sum_kernel(after_ref, *refs):
+    )(*after, rows, grad, gates, w_gu, w_down)
+
+
+def sum_kernel(*refs):
     lefts, rights = refs[: len(refs) // 2 - 1], refs[len(refs) // 2 - 1 : -2]
     out_ref, acc_ref = refs[-2:]
     tile = pl.program_id(2)
@@ -752,9 +777,9 @@
         return pl.BlockSpec((tile, width), lambda j, d, t: (t * stride + first, d))
 
     return pl.pallas_call(
-        sum_kernel,
+        without(len(after), sum_kernel),
         grid=(parts, steps, steps_of_tiles),
-        in_specs=[pl.BlockSpec(memory_space=pltpu.SMEM)]
+        in_specs=[ANYWHERE] * len(after)
         + [left_spec(term[1]) for term in terms]
         + [right_spec(*term[3:]) for term in terms],
         out_specs=pl.BlockSpec((1, inner, width), lambda j, d, t: (j, 0, d)),
@@ -762,53 +787,90 @@
         scratch_shapes=[pltpu.VMEM((inner, width), F32)],
         compiler_params=pltpu.CompilerParams(vmem_limit_bytes=VMEM_LIMIT),
         cost_estimate=pl.CostEstimate(
-            flops=2 * len(terms) * parts * steps_of_tiles * tile * inner * model,
+            flops=2 * (2 * len(terms) * parts * steps_of_tiles * tile * inner * model),
             bytes_accessed=len(terms) * 2 * steps_of_tiles * tile * (parts * inner + model)
             + 4 * parts * inner * model,
             transcendentals=0,
         ),
         name="weight_sum",
-    )(after.reshape(1), *[term[0] for term in terms], *[term[2] for term in terms])
-
-
-def combine_kernel(capacity, after_ref, act_ref, weight_ref, slot_ref, rows_ref, out_ref):
-    place = jnp.where(one_hot(slot_ref[0], capacity), 1.0, 0.0).astype(BF16)
-    routed = lax.dot_general(
-        place, rows_ref[...], (((0,), (0,)), ((), ())), preferred_element_type=F32
-    )
-    own = jnp.dot(act_ref[...], weight_ref[...], preferred_element_type=F32)
-    out_ref[...] = (own + routed).astype(BF16)
-
-
-def combine(after, act, weight, slot_rows, rows, core):
-    inner, model = weight.shape
-    blocks, _, step = slot_rows.shape
-    capacity = rows.shape[0] // blocks
+    )(*after, *[term[0] for term in terms], *[term[2] for term in terms])
+
+
+def combine_kernel(capacity, taken, *refs):
+    out_ref = refs[-1]
+
+    def write(act_ref, weight_ref, slot_ref, rows_ref):
+        place = jnp.where(one_hot(slot_ref[0], capacity), 1.0, 0.0).astype(BF16)
+        routed = lax.dot_general(
+            place, rows_ref[...], (((0,), (0,)), ((), ())), preferred_element_type=F32
+        )
+        own = jnp.dot(act_ref[...], weight_ref[...], preferred_element_type=F32)
+        out_ref[...] = (own + routed).astype(BF16)
+
+    for term in range(len(refs) // 4):
+        pl.when(pl.program_id(0) // taken == term)(
+            functools.partial(write, *refs[4 * term : 4 * term + 4])
+        )
+
+
+def combine(after, terms, core):
+    blocks, _, step = terms[0][2].shape
+    model = terms[0][1].shape[1]
+    capacity = terms[0][3].shape[0] // blocks
     taken = blocks // 2
-
-    def block(i):
-        return core * taken + i
-
+    specs, operands, flops = [], [], 0
+    for term, (act, weight, slot_rows, rows) in enumerate(terms):
+        inner = weight.shape[0]
+
+        def block(i, term=term):
+            return core * taken + jnp.clip(i - term * taken, 0, taken - 1)
+
+        specs += [
+            pl.BlockSpec((step, inner), lambda i, block=block: (block(i), 0)),
+            pl.BlockSpec((inner, model), lambda i: (0, 0)),
+            pl.BlockSpec((1, 1, step), lambda i, block=block: (block(i), 0, 0)),
+            pl.BlockSpec((capacity, model), lambda i, block=block: (block(i), 0)),
+        ]
+        operands += [act, weight, slot_rows, rows]
+        flops += 2 * taken * step * model * (inner + capacity)
+    count = len(terms) * taken * step
     return pl.pallas_call(
-        functools.partial(combine_kernel, capacity),
-        grid=(taken,),
-        in_specs=[
-            pl.BlockSpec(memory_space=pltpu.SMEM),
-            pl.BlockSpec((step, inner), lambda i: (block(i), 0)),
-            pl.BlockSpec((inner, model), lambda i: (0, 0)),
-            pl.BlockSpec((1, 1, step), lambda i: (block(i), 0, 0)),
-            pl.BlockSpec((capacity, model), lambda i: (block(i), 0)),
-        ],
+        without(len(after), functools.partial(combine_kernel, capacity, taken)),
+        grid=(len(terms) * taken,),
+        in_specs=[ANYWHERE] * len(after) + specs,
         out_specs=pl.BlockSpec((step, model), lambda i: (i, 0)),
-        out_shape=jax.ShapeDtypeStruct((taken * step, model), BF16),
+        out_shape=jax.ShapeDtypeStruct((count, model), BF16),
         compiler_params=pltpu.CompilerParams(vmem_limit_bytes=VMEM_LIMIT),
         cost_estimate=pl.CostEstimate(
-            flops=2 * taken * step * model * (inner + capacity),
-            bytes_accessed=2 * taken * (step * (model + inner) + capacity * model),
+            flops=3 * (flops),
+            bytes_accessed=2 * count * model * (step + capacity) // step,
             transcendentals=0,
         ),
         name="combine",
-    )(after.reshape(1), act, weight, slot_rows, rows)
+    )(*after, *operands)
+
+
+def finish_kernel(hidden_ref, attn_ref, valid_ref, first, second, third, fourth, out_ref, sum_ref):
+    residual, attn, valid = hidden_ref[...].astype(F32), attn_ref[...], valid_ref[...]
+    moe = first[...] + second[...].astype(F32) + third[...].astype(F32) + fourth[...].astype(F32)
+    out_ref[...] = (residual + attn + moe).astype(BF16)
+    for place, value in enumerate((residual, attn, moe)):
+        sum_ref[0, place] = jnp.sum(valid * value * value)
+    sum_ref[0, 3] = jnp.sum(valid)
+
+
+def finish(after, hidden_in, attn_rows, valid_rows, moe_parts):
+    return pl.pallas_call(
+        without(len(after), finish_kernel),
+        in_specs=[ANYWHERE] * len(after) + [pl.BlockSpec(memory_space=pltpu.VMEM)] * 7,
+        out_specs=[pl.BlockSpec(memory_space=pltpu.VMEM), pl.BlockSpec(memory_space=pltpu.SMEM)],
+        out_shape=[
+            jax.ShapeDtypeStruct(hidden_in.shape, BF16),
+            jax.ShapeDtypeStruct((1, 4), F32),
+        ],
+        compiler_params=pltpu.CompilerParams(vmem_limit_bytes=VMEM_LIMIT),
+        name="finish",
+    )(*after, hidden_in, attn_rows, valid_rows, *moe_parts)
 
 
 def norm_scale(rows_in):
@@ -885,13 +947,15 @@
     gain_attn, gain_moe = norm_gains[0], norm_gains[1]
     scale_attn = norm_scale(residual)
     own_attn = (residual * scale_attn * gain_attn).astype(BF16)
+    numbers = jnp.concatenate([segments[None], valid_mask[None], routes.T, slots.T], 0)
+    numbers = jnp.stack([numbers, swap(numbers, "y")])
+    numbers = jnp.stack([numbers, swap(numbers, "c")])
+    numbers_here = flip(flip(numbers[:, :, :2], c, 0), y, 1).transpose(2, 1, 0, 3)
+    numbers_here = numbers_here.reshape(2, plane_rows)
+    numbers_before = jnp.where(z == 0, -1, lax.ppermute(numbers_here, "z", ahead))
+
     before = lax.ppermute(own_attn, "z", ahead)
-    grad_shards = slot_shards(cotangent)
-    now = jnp.zeros((), jnp.int32)
-    rows_attn, attn_marks = slot_gather(jnp.stack([before, own_attn]), now, now)
-    flag = tick(attn_marks[0])
-    slot_grads, grad_marks = slot_gather(hold(grad_shards, flag), now, now)
-    slot_grads = [half.reshape(-1, model) for half in slot_grads]
+    crossed = [cross(cotangent, offset) for offset in range(1, LINE)]
 
     def cut_heads(value):
         return value.reshape(weight_rows, -1, 4, cols).transpose(2, 0, 1, 3)
@@ -900,26 +964,17 @@
     out_cut = cut_heads(out_weight.T).reshape(4, weight_rows, cols)
     w_heads = exchange(jnp.concatenate([qkv_cut, out_cut], 2), ("y", "c"))
     w_heads = w_heads.reshape(4 * weight_rows, 4 * cols)
-    w_qkv = gather_line(w_heads[:, : 3 * cols], tick(grad_marks[0]))
+    qkv_rows = w_heads[:, : 3 * cols]
+    qkv_across = cross(qkv_rows, 2)
+    later = tick(w_heads)
+    attn_pairs, attn_plane, _ = slot_pair(jnp.stack([before, own_attn]), (w_heads, numbers_before))
+    rows_attn = attn_plane(tuple(crossed) + (qkv_across,))
+    grad_pairs, grad_plane, grad_arrived = slot_pair(
+        hold(jnp.stack([cotangent] + crossed), tick(attn_pairs[0])), ()
+    )
+    w_qkv, qkv_others = gather_line(qkv_rows, qkv_across)
     if groups > 1:
         w_qkv = lax.all_gather(w_qkv, "g", axis=0, tiled=True)
-    later = tick(w_heads)
-
-    numbers = jnp.concatenate([segments[None], valid_mask[None], routes.T, slots.T], 0) + later
-    numbers = jnp.stack([numbers, swap(numbers, "y")])
-    numbers = jnp.stack([numbers, swap(numbers, "c")])
-    plane_numbers = flip(flip(numbers[:, :, :2], c, 0), y, 1).transpose(1, 0, 2, 3)
-    plane_numbers = plane_numbers.reshape(4, 2, blocks).transpose(1, 0, 2).reshape(2, plane_rows)
-    numbers = slot_shards(numbers)
-    numbers = numbers.reshape(LINE, 1, 4, 2 + 2 * top, blocks)
-    if groups > 1:
-        numbers = lax.all_gather(numbers, "g", axis=1, tiled=True)
-    slot_here = jnp.max(
-        jnp.where(numbers[:, :, :, 2 : 2 + top] == expert, numbers[:, :, :, 2 + top :], -1), 3
-    )
-    slot_here = slot_here.reshape(LINE, groups, 4, 2, 2, rows_here // 2)
-    slot_here = flip(slot_here, x, 3).transpose(0, 1, 2, 4, 3, 5)
-    slot_here = slot_here.reshape(2, 2, groups, 2, 2, blocks)
 
     late_gu, late_dn = hold(shared_gate_up, later), hold(shared_down, later)
     shared_cut = jnp.concatenate(
@@ -938,25 +993,47 @@
     order = order.astype(jnp.int32)
     order_one = jnp.concatenate([x[None], order])
     order_two = jnp.concatenate([x[None], order[:2], order[:2] + 4, order[2:], order[2:] + 4])
-    own_rows, projected = project(order_two, rows_attn, w_qkv, bias, cosine, sine)
-    w_out = gather_line(hold(w_heads[:, 3 * cols :], tick(w_qkv)), now)
+    own_rows, projected = project((), order_two, rows_attn, w_qkv, bias, cosine, sine)
+    w_out_rows = hold(w_heads[:, 3 * cols :], tick(qkv_others))
+    w_out, _ = gather_line(w_out_rows, hold(cross(w_out_rows, 2), tick(projected)))
     if groups > 1:
         w_out = lax.all_gather(w_out, "g", axis=0, tiled=True)
-    numbers_before = jnp.where(z == 0, -1, lax.ppermute(plane_numbers, "z", ahead))
-    near = jnp.concatenate([numbers_before, plane_numbers], 1)
+    numbers = hold(numbers, tick(projected))
+    numbers = jnp.stack([numbers] + [cross(numbers, offset) for offset in range(1, LINE)])
+    numbers = numbers.reshape(LINE, 1, 4, 2 + 2 * top, blocks)
+    if groups > 1:
+        numbers = lax.all_gather(numbers, "g", axis=1, tiled=True)
+    slot_here = jnp.max(
+        jnp.where(numbers[:, :, :, 2 : 2 + top] == expert, numbers[:, :, :, 2 + top :], -1), 3
+    )
+    slot_here = slot_here.reshape(LINE * groups * 4, 2, 2, rows_here // 2)
+    slot_here = flip(slot_here, x, 1).transpose(0, 2, 1, 3).reshape(2, 2, groups, 2, 2, blocks)
+    near = jnp.concatenate([numbers_before, numbers_here], 1)
     seg_k, valid_k = near[:1], near[1:]
-    seg_q = plane_numbers[0].reshape(plane_rows, 1)
-    attended = attend(projected, seg_q, seg_k, valid_k)
+    seg_q = numbers_here[0].reshape(plane_rows, 1)
+    attended = attend(grad_arrived, projected, seg_q, seg_k, valid_k)
     w_out_t = w_out.T
-    order_late = order_one + tick(grad_marks[1])
-    (send,) = spread(order_late, attended, w_out_t, 1)
-    (keep,) = spread(order_late, attended, w_out_t, 0)
-    attn_rows = slot_scatter(keep, send, now, now, now)[0][0]
+    (send,) = spread((), order_one, attended, w_out_t, 1)
+    (keep,) = spread((send,), order_one, attended, w_out_t, 0)
+    attn_rows = slot_scatter(keep, send, (slot_here.reshape(-1, blocks),), (), ())[0][0]
     middle = residual + attn_rows
     scale_moe = norm_scale(middle)
     own_moe = (middle * scale_moe * gain_moe).astype(BF16)
-
-    w_shared = exchange(hold(shared_cut, tick(attended)), everywhere)
+    all_grads = [half.reshape(-1, model) for half in grad_plane((own_moe,))]
+    crossed = [cross(own_moe, offset) for offset in range(1, LINE)]
+    near_pairs, near_plane, _ = slot_pair(jnp.stack([own_moe, crossed[0]]), tuple(crossed[1:]))
+    w_shared = exchange(hold(shared_cut, tick(near_pairs[0])), everywhere)
+    near_rows = near_plane(())
+    far_pairs, far_plane, _ = slot_pair(hold(jnp.stack(crossed[1:]), tick(near_rows[0])), ())
+    def whole_slots(halves):
+        halves = [half.reshape(-1, model) for half in halves]
+        if groups > 1:
+            halves = [lax.all_gather(half, "g", axis=0, tiled=True) for half in halves]
+        return halves
+
+    all_grads = whole_slots(all_grads)
+    chunk_rows = [whole_slots(near_rows)]
+
     w_shared = w_shared.transpose(1, 0, 2).reshape(3 * own, model)
 
     def padded(*values):
@@ -972,94 +1049,85 @@
     )
     shared_dn = padded(w_shared[2 * own :])
 
-    near_shards = jnp.stack([own_moe, cross(own_moe, 2)])
-    far_shards = cross(near_shards, 1)
-    near_rows, near_marks = slot_gather(near_shards, now, now)
-    far_rows, far_marks = slot_gather(hold(far_shards, tick(near_marks[1])), now, now)
-    chunk_rows = [[half.reshape(-1, model) for half in rows] for rows in (near_rows, far_rows)]
-    if groups > 1:
-        chunk_rows = [
-            [lax.all_gather(half, "g", axis=0, tiled=True) for half in rows] for rows in chunk_rows
-        ]
-        slot_grads = [lax.all_gather(half, "g", axis=0, tiled=True) for half in slot_grads]
-
     w_gu, w_down = expert_gate_up[0].transpose(0, 2, 1), expert_down[0]
     expert_id = expert.reshape(1).astype(jnp.int32)
 
     def slots_of(table):
         return table.transpose(3, 2, 0, 1, 4, 5).reshape(-1, 1, blocks)
 
-    def to_owners(act, weight, table, rows, after):
-        halves = []
-        for core in range(2):
-            half = combine(after[1 - core], act, weight, table, rows, core)
-            if groups > 1:
-                half = lax.psum_scatter(half, "g", scatter_dimension=0, tiled=True)
-            halves.append(half.reshape(-1, plane_rows // 2, model))
-        total, marks = slot_scatter(*halves, *after[2:])
-        return total, (halves[0],) + marks
-
+    def core_part(after, terms, core):
+        if groups == 1:
+            part = combine(after, terms, core)
+        else:
+            parts = [combine(after, [term], core) for term in terms]
+            parts = [lax.psum_scatter(v, "g", scatter_dimension=0, tiled=True) for v in parts]
+            part = jnp.concatenate(parts, 0)
+        return part.reshape(-1, plane_rows // 2, model)
+
+    tables = [slots_of(slot_here[chunk : chunk + 1]) for chunk in range(2)]
     acts, hiddens, signals, inputs, grads, results = [], [], [], [], [], []
-    gate_grads, totals = [], []
-    start, begin = tick(far_marks[0]), tick(far_marks[1])
-    for chunk, rows in enumerate(chunk_rows):
-        table = slots_of(slot_here[chunk : chunk + 1])
+    gate_grads, backs = [], []
+
+    def enter_chunk(chunk, after):
         act, hid, sig, erow, egrad, egate = moe_in(
-            expert_id + start,
-            rows, slot_grads, chunk, shared_in, shared_dn, table, experts, own, capacity,
+            after, expert_id,
+            chunk_rows[chunk], all_grads, chunk, shared_in, shared_dn, tables[chunk],
+            experts, own, capacity,
         )
-        back, out, dgu, ehid, ggate = run_expert(now, erow, egrad, egate, w_gu, w_down)
-        chosen = table == jnp.arange(capacity, dtype=jnp.int32)[None, :, None]
+        signals.append(sig.reshape(-1, blocks))
+        acts.append(act)
+        hiddens.append(hid)
+        return erow, egrad, egate
+
+    def run_chunk(chunk, after, erow, egrad, egate):
+        back, out, dgu, ehid, ggate = run_expert(after, erow, egrad, egate, w_gu, w_down)
+        chosen = tables[chunk] == jnp.arange(capacity, dtype=jnp.int32)[None, :, None]
         ggate = ggate.reshape(-1, capacity, 1)
         gate_grads.append(jnp.sum(jnp.where(chosen, ggate, 0.0), axis=1))
-        signals.append(sig.reshape(-1, blocks))
-        total, marks = to_owners(act, shared_in, table, back, (begin, now, now, now, now))
-        start, begin = tick(marks[1]), tick(marks[3])
-        totals.append(total)
-        acts.append(act)
-        hiddens.append(hid)
         inputs.append((dgu, erow))
         grads.append((ehid, egrad))
         results.append(out)
-    grad_normed, last_mark = from_slots(totals[0], totals[1])
-
+        backs.append(back)
+
+    def grad_term(chunk):
+        return [(acts[chunk], shared_in, tables[chunk], backs[chunk])]
+
+    def moe_term(chunk):
+        return [(hiddens[chunk], shared_dn, tables[chunk], results[chunk])]
+
+    entered = enter_chunk(0, (far_pairs[0],))
+    far_rows = far_plane((acts[0],))
+    chunk_rows.append(whole_slots(far_rows))
+    run_chunk(0, (), *entered)
+    send = core_part((far_rows[0],), grad_term(0), 1)
+    keep = core_part((send,), grad_term(0), 0)
+    near_steps = scatter_core(keep, send, ())
+    run_chunk(1, (), *enter_chunk(1, (near_steps[0],)))
+    near_steps = scatter_pair(near_steps, ())
+    send = core_part((near_steps[0],), grad_term(1), 1)
+    keep = core_part((send,), grad_term(1), 0)
+    near_total = scatter_last(near_steps, ())
+    near_cross = cross(near_total[1].astype(BF16), 1)
+
+    far_steps = scatter_core(keep, send, (near_total,))
+    moe_terms = moe_term(0) + moe_term(1)
+    moe_send = core_part((far_steps[0],), moe_terms, 1)
+    moe_keep = core_part((moe_send,), moe_terms, 0)
     signals = jnp.stack([jnp.stack(gate_grads), jnp.stack(signals)])
     signals = signals.reshape(2, 2, 2, groups, 2, 2, 2, 2, rows_here // 2)
-    for dim, index in ((1, z % 2), (2, c), (4, z // 2), (5, y), (7, x)):
+    for dim, index in ((1, z // 2), (2, c), (4, z % 2), (5, y), (7, x)):
         signals = flip(signals, index, dim)
-    signals = signals.transpose(3, 4, 1, 5, 2, 7, 0, 6, 8).reshape(2 * shares, 2, rows_here)
-    signals = exchange(signals, EVERY).reshape(experts, 2, 2, rows_here)
-    grad_router_probs = jnp.sum(signals[:, :, 0], axis=1).T
-    gate_signal = jnp.sum(signals[:, :, 1], axis=(0, 1))
-
-    def over_chunks(parts):
-        width = parts[0].shape[-1]
-        parts = [part.reshape(2, groups, -1, width) for part in parts]
-        return jnp.concatenate(parts, 2).reshape(-1, width)
-
-    if groups == 1:
-        moe_parts, moe_marks = to_owners(
-            over_chunks(hiddens),
-            shared_dn,
-            slots_of(slot_here),
-            over_chunks(results),
-            (tick(marks[0]), tick(marks[2]), now, now, now),
-        )
-        moe_parts = [moe_parts[:2], moe_parts[2:]]
-    else:
-        moe_parts = []
-        for chunk in range(2):
-            table = slots_of(slot_here[chunk : chunk + 1])
-            after = tick(moe_parts[-1] if moe_parts else last_mark)
-            part, moe_marks = to_owners(
-                hiddens[chunk], shared_dn, table, results[chunk], (after, after, now, now, now)
-            )
-            moe_parts.append(part)
-    moe_rows, _ = from_slots(*moe_parts)
-    output = (middle + moe_rows).astype(BF16)
+    signals = signals.transpose(3, 1, 4, 5, 2, 7, 0, 6, 8).reshape(2 * shares, 2, rows_here)
+    far_steps = scatter_pair(far_steps, (moe_keep,))
+    moe_steps = scatter_core(moe_keep, moe_send, (far_steps[0],))
+    far_total = scatter_last(far_steps, (moe_steps[0],))
+    far_cross = [cross(far_total[k].astype(BF16), 2 + k) for k in range(2)]
+    moe_steps = scatter_pair(moe_steps, (far_total,))
+
     tiles = range(2)
+    shared_time = (far_total,)
     grad_sgu = weight_sum(
-        tick(marks[4]),
+        shared_time,
         [
             (acts[chunk][None], core * groups, chunk_rows[chunk][core], 1, 0)
             for chunk in tiles
@@ -1070,9 +1138,9 @@
         BF16,
     )[0]
     grad_sdn = weight_sum(
-        tick(last_mark),
+        shared_time,
         [
-            (hiddens[chunk][None], core * groups, slot_grads[core], 2, chunk)
+            (hiddens[chunk][None], core * groups, all_grads[core], 2, chunk)
             for chunk in tiles
             for core in tiles
         ],
@@ -1080,14 +1148,23 @@
         groups,
         BF16,
     )[0]
+    grad_normed = near_total[0] + near_cross.astype(F32)
+    grad_normed = grad_normed + far_cross[0].astype(F32) + far_cross[1].astype(F32)
+    grad_normed = hold(grad_normed, tick(grad_sgu) + tick(grad_sdn) + tick(moe_steps[0]))
     shared_grad = jnp.concatenate(
         [grad_sgu[:own], grad_sgu[held : held + own], grad_sdn[:own]], 0
     )
     shared_grad = shared_grad.reshape(3 * own, shares, weight_rows).transpose(1, 0, 2)
     shared_grad = exchange(shared_grad, everywhere)
-    shared_mark = tick(shared_grad)
+    shared_grad_sent = shared_grad
     shared_grad = shared_grad.reshape(shares, 3, own, weight_rows).transpose(1, 0, 2, 3)
     shared_grad = shared_grad.reshape(3, shared_cols, weight_rows).astype(F32)
+    grad_sgu = shared_grad[:2].transpose(0, 2, 1)
+
+    signals = exchange(hold(signals, tick(far_total)), EVERY)
+    signals = signals.reshape(experts, 2, 2, rows_here)
+    grad_router_probs = jnp.sum(signals[:, :, 0], axis=1).T
+    gate_signal = jnp.sum(signals[:, :, 1], axis=(0, 1))
 
     own_logits = jnp.dot(own_moe, router_weight, preferred_element_type=F32)
     router_probs = jax.nn.softmax(own_logits, axis=-1)
@@ -1106,21 +1183,10 @@
     grad_middle = cotangent.astype(F32) + norm_back(middle, scale_moe, gain_moe, grad_normed)
     grad_attn = grad_middle.astype(BF16)
 
-    plane_grad, _ = slot_gather(grad_attn[None], now, now)
-    plane_grad, grad_attended = project(order_one + tick(moe_marks[1]), plane_grad, w_out)
-    grad_projected = attend_back(
-        projected, grad_attended, seg_q, seg_k, valid_k, cosine, sine
-    )
-    w_qkv_t = w_qkv.T
-    order_late = order_two + shared_mark
-    send, sum_send = spread(order_late, grad_projected, w_qkv_t, 1, rows_attn[1])
-    keep, sum_keep = spread(order_late, grad_projected, w_qkv_t, 0, rows_attn[0])
-    gain_sum = (sum_send + sum_keep)[0] / gain_attn
-    back_both, back_marks = slot_scatter(keep, send, tick(moe_marks[3]), now, now)
-    back_own = back_both[1] + lax.ppermute(back_both[0].astype(BF16), "z", behind).astype(F32)
-    input_grad = grad_middle + norm_back(residual, scale_attn, gain_attn, back_own)
-    bias_sum = jnp.sum(grad_projected.astype(F32), axis=0).reshape(3, cols)
-    grad_bias = lax.dynamic_update_slice_in_dim(jnp.zeros((3, model), F32), bias_sum, here, 1)
+    _, plane, _ = slot_pair(grad_attn[None], (moe_steps[1], moe_steps[3]))
+    moe_parts = scatter_last(moe_steps, (grad_attn,))
+    moe_cross = [cross(moe_parts[k].astype(BF16), k) for k in range(1, LINE)]
+    plane_grad, grad_attended = project((), order_one, plane((moe_parts,)), w_out)
 
     def weight_grad(left, right):
         return lax.dot_general(left, right, (((0,), (0,)), ((), ())), preferred_element_type=F32)
@@ -1129,30 +1195,40 @@
         if groups > 1:
             value = lax.psum_scatter(value, "g", scatter_dimension=0, tiled=True)
         value, mark = scatter_line(value)
-        value = exchange(value.astype(BF16).reshape(4, weight_rows, -1), ("y", "c"))
-        return value.astype(F32), mark
-
-    grad_out, _ = to_weight_owners(weight_grad(plane_grad, attended).astype(BF16))
+        return exchange(value.reshape(4, weight_rows, -1), ("y", "c")).astype(F32), mark
+
+    grad_out = weight_grad(plane_grad, attended).astype(BF16)
+    grad_projected = attend_back(
+        (grad_out, shared_grad_sent, moe_cross[0]),
+        projected, grad_attended, seg_q, seg_k, valid_k, cosine, sine,
+    )
+    grad_qkv = weight_grad(own_rows, grad_projected).astype(BF16)
+    grad_out, out_marks = to_weight_owners(grad_out)
     grad_out = grad_out.transpose(1, 0, 2).reshape(weight_rows, local_cols).T
-    grad_qkv, qkv_mark = to_weight_owners(weight_grad(own_rows, grad_projected).astype(BF16))
+    tile = inputs[0][1].shape[0]
+    grad_egu = weight_sum(
+        (grad_projected,), [(left, 0, right, 1, 0) for left, right in inputs], tile, 1, F32
+    )
+    grad_qkv, qkv_marks = to_weight_owners(grad_qkv)
+    grad_edown = weight_sum(
+        (grad_egu,), [(left[None], 0, right, 1, 0) for left, right in grads], tile, 1, F32
+    )
     grad_qkv = grad_qkv.reshape(4, weight_rows, 3, cols).transpose(2, 1, 0, 3)
     grad_qkv = grad_qkv.reshape(3, weight_rows, local_cols)
-
-    tile = inputs[0][1].shape[0]
-    grad_egu = weight_sum(
-        tick(back_marks[1]), [(left, 0, right, 1, 0) for left, right in inputs], tile, 1, F32
-    )
-    grad_egu = grad_egu.transpose(0, 2, 1)[None]
-    grad_edown = weight_sum(
-        tick(qkv_mark), [(left[None], 0, right, 1, 0) for left, right in grads], tile, 1, F32
-    )
+    w_qkv_t = w_qkv.T
+    send, sum_send = spread(
+        (qkv_marks[0], out_marks[1], moe_cross[1]),
+        order_two, grad_projected, w_qkv_t, 1, rows_attn[1],
+    )
+    keep, sum_keep = spread((send, moe_cross[2], grad_egu), order_two, grad_projected, w_qkv_t, 0, rows_attn[0])
+    gain_sum = (sum_send + sum_keep)[0] / gain_attn
+    bias_sum = jnp.sum(grad_projected.astype(F32), axis=0).reshape(3, cols)
+    grad_bias = lax.dynamic_update_slice_in_dim(jnp.zeros((3, model), F32), bias_sum, here, 1)
 
     valid_rows = lax.dynamic_slice_in_dim(valid_mask, x * rows_here, rows_here, 0).astype(F32)
-    valid_rows = valid_rows[:, None]
-
-    def in_lanes(values):
-        flat = jnp.stack(values)
-        return jnp.pad(flat, (0, model - len(values)))[None]
+    output, squares = finish(
+        (grad_projected,), hidden_in, attn_rows, valid_rows[:, None], [moe_parts[0]] + moe_cross
+    )
 
     sums_of_all = all_sum(
         jnp.concatenate(
@@ -1160,20 +1236,18 @@
                 grad_router,
                 grad_gate_vec[None],
                 grad_gain_moe[None],
-                gain_sum[None],
+                hold(gain_sum[None], tick(grad_edown) + tick(grad_sgu)),
                 grad_bias,
-                in_lanes(
-                    [
-                        jnp.sum(valid_rows * residual * residual),
-                        jnp.sum(valid_rows * attn_rows * attn_rows),
-                        jnp.sum(valid_rows * moe_rows * moe_rows),
-                        jnp.sum(valid_rows),
-                    ]
-                ),
+                jnp.pad(squares, ((0, 0), (0, model - 4))),
             ],
             0,
         )
     )
+    back_both, _ = slot_scatter(
+        keep, send, (qkv_marks[1], out_marks[2]), (qkv_marks[2], grad_edown), ()
+    )
+    back_own = back_both[1] + lax.ppermute(back_both[0].astype(BF16), "z", behind).astype(F32)
+    input_grad = grad_middle + norm_back(residual, scale_attn, gain_attn, back_own)
     others = sums_of_all[experts:]
     root_means = jnp.sqrt(others[6, :3] / (jnp.maximum(others[6, 3], 1.0) * model))
     return (
@@ -1185,9 +1259,9 @@
         grad_out,
         sums_of_all[:experts].T,
         others[0],
-        shared_grad[:2].transpose(0, 2, 1),
+        grad_sgu,
         shared_grad[2],
-        grad_egu,
+        grad_egu.transpose(0, 2, 1)[None],
         grad_edown,
         root_means[0],
         root_means[1],

time: 1150 us -> 1040 us (0.904)
  waiting for transfers between devices: 392 us -> 320 us
  Pallas kernels: 471 us -> 405 us
  starting transfers between devices: 101 us -> 141 us
  other arithmetic: 80.8 us -> 55.4 us
  local copies, waits for them, and re-layouts: 70.7 us -> 82.4 us
    ppermute x22 -> x25, waiting for transfers between devices: 210 us -> 124 us  [cross(): return lax.ppermute(value, 'z', [(k, k ^ offset) for k in range(LINE)])]
    pallas_call x47 -> x48, Pallas kernels: 445 us -> 388 us  [the longest x25 125 us: stage(): pl.pallas_call(without(len(after), kernel), grid=(count, parts), in_specs...]
    ppermute x22 -> x25, starting transfers between devices: 25.4 us -> 63.2 us  [cross(): return lax.ppermute(value, 'z', [(k, k ^ offset) for k in range(LINE)])]
    ppermute x1, waiting for transfers between devices: 0.01 us -> 12.5 us  [per_device(): lax.ppermute(numbers_here, 'z', ahead)]
    pallas_call x20 -> x12, Pallas kernels: 26.5 us -> 16.4 us  [tick(): pl.pallas_call(tick_kernel, grid=(1,), in_specs=[pl.BlockSpec(block, lamb...]
    unnamed x210 -> x195, local copies, waits for them, and re-layouts: 29.8 us -> 30.1 us
  transfers between devices with their start and end apart: 86 -> 89, of which waited for: 45 -> 37; matrix products, arithmetic and copies ran while one was open for 12% -> 12% of each run, Pallas kernels for 32% -> 32%
where the time goes in v3:
time: 1040 us; the launch traced here: 1030 us
  Pallas kernels  405 us (39%)
  waiting for transfers between devices  320 us (31%)
  starting transfers between devices  141 us (14%)
  local copies, waits for them, and re-layouts  82.4 us (8%)
  other arithmetic  55.4 us (5%)
  matrix products  14.7 us (1%)
  between operations  11.7 us (1%)
    ppermute x55, waiting for transfers between devices, swap(): return lax.ppermute(value, axis, SWAP)  166 us
    pallas_call x25, Pallas kernels, stage(): pl.pallas_call(without(len(after), kernel), grid=(count, parts), in_specs...  125 us
    ppermute x25, waiting for transfers between devices, cross(): return lax.ppermute(value, 'z', [(k, k ^ offset) for k in range(LINE)])  124 us
    ppermute x25, starting transfers between devices, cross(): return lax.ppermute(value, 'z', [(k, k ^ offset) for k in range(LINE)])  63.2 us
    pallas_call x6, Pallas kernels, combine(): pl.pallas_call(without(len(after), functools.partial(combine_kernel, capa...  52.3 us
    pallas_call x4, Pallas kernels, weight_sum(): pl.pallas_call(without(len(after), sum_kernel), grid=(parts, steps, steps...  50.5 us
    ppermute x55, starting transfers between devices, swap(): return lax.ppermute(value, axis, SWAP)  47.9 us
    pallas_call x2, Pallas kernels, run_expert(): pl.pallas_call(without(len(after), functools.partial(expert_kernel, steps...  46.6 us
  transfers between devices with their start and end apart: 89, of which 37 were waited for; matrix products, arithmetic and copies ran while one was open for 12% of the time, Pallas kernels for 32%

profile of v3, /device:TPU:0, one launch (start us, length us, event | category | flops | bytes accessed | tf_op | source)
XLA Modules:
  0.0 1030.9 jit_solution(16695611254573095192)
XLA Ops:
  17.2 10.4 %collective-permute-done.7 = bf16[128,2048]{1,0:T(8,128)(2,1)S(1)} collective-permute-done((bf16[128,2048]{1,0:T(8,128)(2,1)S(1)}, bf16[128,2048]{1,0:T(8,128)(2,1)S(1)}, u32[]{:S(2)}, u32[]{:S(2)}) %collective-permute-start.7) | collective-permute-done | bytes 524320 | tf_op jit(solution)/shard_map/ppermute | solution.py:957
  42.1 12.5 %collective-permute-done.6 = s32[2,1024]{1,0:T(2,128)S(1)} collective-permute-done((s32[2,1024]{1,0:T(2,128)S(1)}, s32[2,1024]{1,0:T(2,128)S(1)}, u32[]{:S(2)}, u32[]{:S(2)}) %collective-permute-start.6) | collective-permute-done | bytes 8224 | tf_op jit(solution)/shard_map/ppermute | solution.py:955
  61.5 18.3 %collective-permute-start = (bf16[128,2048]{1,0:T(8,128)(2,1)S(1)}, bf16[128,2048]{1,0:T(8,128)(2,1)S(1)}, u32[]{:S(2)}, u32[]{:S(2)}) collective-permute-start(bf16[128,2048]{1,0:T(8,128)(2,1)S(1)} %copy-done.14), channel_id=1, source_target_pairs={{0,8},{8,0},{16,24},{24,16},{1,9},{9,1},{17,25},{25,17},{2,10},{10... | collective-permute-start | bytes 1572872 | tf_op jit(solution)/shard_map/ppermute | solution.py:34
  84.3 17.6 %collective-permute-done.refs_0_ = bf16[128,2048]{1,0:T(8,128)(2,1)S(1)} collective-permute-done((bf16[128,2048]{1,0:T(8,128)(2,1)S(1)}, bf16[128,2048]{1,0:T(8,128)(2,1)S(1)}, u32[]{:S(2)}, u32[]{:S(2)}) %collective-permute-start) | collective-permute-done | bytes 524320 | tf_op jit(solution)/shard_map/ppermute | solution.py:34
  101.9 16.2 %collective-permute-done.1.refs_1_ = bf16[128,2048]{1,0:T(8,128)(2,1)} collective-permute-done((bf16[128,2048]{1,0:T(8,128)(2,1)S(1)}, bf16[128,2048]{1,0:T(8,128)(2,1)}, u32[]{:S(2)}, u32[]{:S(2)}) %collective-permute-start.1) | collective-permute-done | bytes 524320 | tf_op jit(solution)/shard_map/ppermute | solution.py:34
  131.7 10.0 collective-permute-start.13
  153.8 14.5 %collective-permute-done.17.refs_1_ = bf16[4,64,2048]{2,1,0:T(8,128)(2,1)} collective-permute-done((bf16[4,64,2048]{2,1,0:T(8,128)(2,1)}, bf16[4,64,2048]{2,1,0:T(8,128)(2,1)}, u32[]{:S(2)}, u32[]{:S(2)}) %collective-permute-start.17) | collective-permute-done | bytes 1048608 | tf_op jit(solution)/shard_map/ppermute | solution.py:30
  194.5 14.4 %project.2 = (bf16[2048,2048]{1,0:T(8,128)(2,1)}, bf16[2048,768]{1,0:T(8,128)(2,1)}) custom-call(s32[9]{0:T(128)} %concatenate.59.refs_0_, bf16[1024,2048]{1,0:T(8,128)(2,1)} %bitcast.386, bf16[1024,2048]{1,0:T(8,128)(2,1)} %bitcast.25.refs_2_.refs_6_, bf16[2048,768]{1,0:T(8,128)(2,1)} %copy.160.refs_3_, f32[1,768]{1,0:T(1,128)} %bitcast.454, ...), custom_call_target="tpu_custom_call" | custom-call | flops 19327352832 | bytes 23068672 | tf_op jit(solution)/shard_map/project/pallas_call | solution.py:336
  211.3 9.7 collective-permute-done.19.refs_0_.refs_2_
  222.0 11.1 %attend.1.refs_1_.refs_2_ = bf16[1024,256]{1,0:T(8,128)(2,1)} custom-call(bf16[4,128,2048]{2,1,0:T(8,128)(2,1)} %collective-permute-done.19.refs_0_.refs_2_, bf16[4,128,2048]{2,1,0:T(8,128)(2,1)} %collective-permute-done.20.refs_1_.refs_4_, bf16[2048,768]{1,0:T(8,128)(2,1)} %get-tuple-element.99.marker_ref.refs_2_.refs_3_.refs_4_.refs_5_, ...), custom_call_target="tpu_custom_call" | custom-call | flops 12079595520 | bytes 4194304 | tf_op jit(solution)/shard_map/attend/pallas_call | solution.py:464
  260.4 12.6 %collective-permute-done.24.refs_1_ = bf16[1,128,2048]{2,1,0:T(8,128)(2,1)S(1)} collective-permute-done((bf16[1,128,2048]{2,1,0:T(8,128)(2,1)}, bf16[1,128,2048]{2,1,0:T(8,128)(2,1)S(1)}, u32[]{:S(2)}, u32[]{:S(2)}) %collective-permute-start.24) | collective-permute-done | bytes 524320 | tf_op jit(solution)/shard_map/ppermute | solution.py:30
  305.4 10.8 %collective-permute-done.30 = bf16[128,2048]{1,0:T(8,128)(2,1)S(1)} collective-permute-done((bf16[128,2048]{1,0:T(8,128)(2,1)S(1)}, bf16[128,2048]{1,0:T(8,128)(2,1)S(1)}, u32[]{:S(2)}, u32[]{:S(2)}) %collective-permute-start.30) | collective-permute-done | bytes 524320 | tf_op jit(solution)/shard_map/ppermute | solution.py:34
  327.7 23.5 %collective-permute-done.28.refs_0_ = bf16[128,2048]{1,0:T(8,128)(2,1)S(1)} collective-permute-done((bf16[128,2048]{1,0:T(8,128)(2,1)S(1)}, bf16[128,2048]{1,0:T(8,128)(2,1)S(1)}, u32[]{:S(2)}, u32[]{:S(2)}) %collective-permute-start.28) | collective-permute-done | bytes 524320 | tf_op jit(solution)/shard_map/ppermute | solution.py:34
  366.7 28.0 %collective-permute-done.33.refs_1_ = bf16[2,128,2048]{2,1,0:T(8,128)(2,1)} collective-permute-done((bf16[2,128,2048]{2,1,0:T(8,128)(2,1)}, bf16[2,128,2048]{2,1,0:T(8,128)(2,1)}, u32[]{:S(2)}, u32[]{:S(2)}) %collective-permute-start.33) | collective-permute-done | bytes 1048608 | tf_op jit(solution)/shard_map/ppermute | solution.py:30
  403.9 12.4 %collective-permute-done.35.refs_1_ = bf16[2,64,2048]{2,1,0:T(8,128)(2,1)} collective-permute-done((bf16[2,64,2048]{2,1,0:T(8,128)(2,1)S(1)}, bf16[2,64,2048]{2,1,0:T(8,128)(2,1)}, u32[]{:S(2)}, u32[]{:S(2)}) %collective-permute-start.35) | collective-permute-done | bytes 524320 | tf_op jit(solution)/shard_map/ppermute | solution.py:30
  429.1 16.7 %moe_in.2 = (bf16[2048,512]{1,0:T(8,128)(2,1)}, bf16[2048,256]{1,0:T(8,128)(2,1)}, f32[2048,1]{1,0:T(8,128)}, bf16[768,2048]{1,0:T(8,128)(2,1)}, bf16[768,2048]{1,0:T(8,128)(2,1)}, /*index=5*/f32[768,128]{1,0:T(8,128)}) custom-call(bf16[2,128,2048]{2,1,0:T(8,128)(2,1)} %get-tuple-element.112.refs_0_.refs_1_, s32[1]{0:T(128)} %bitcast.59.refs_1_, ...), custom_call_target="tpu_custom_call" | custom-call | flops 16106127360 | bytes 25165824 | tf_op jit(solution)/shard_map/moe_in/pallas_call | solution.py:620
  445.8 23.3 %run_expert.2 = (bf16[768,2048]{1,0:T(8,128)(2,1)}, bf16[768,2048]{1,0:T(8,128)(2,1)}, bf16[2,768,704]{2,1,0:T(8,128)(2,1)}, bf16[768,704]{1,0:T(8,128)(2,1)}, f32[768,1]{1,0:T(8,128)}) custom-call(bf16[768,2048]{1,0:T(8,128)(2,1)} %get-tuple-element.115.refs_0_.refs_3_, bf16[768,2048]{1,0:T(8,128)(2,1)} %get-tuple-element.116.refs_1_.refs_3_, ...), custom_call_target="tpu_custom_call" | custom-call | flops 26575110144 | bytes 29884416 | tf_op jit(solution)/shard_map/run_expert/pallas_call | solution.py:707
  500.4 16.9 %moe_in.3 = (bf16[2048,512]{1,0:T(8,128)(2,1)}, bf16[2048,256]{1,0:T(8,128)(2,1)}, f32[2048,1]{1,0:T(8,128)}, bf16[768,2048]{1,0:T(8,128)(2,1)}, bf16[768,2048]{1,0:T(8,128)(2,1)}, /*index=5*/f32[768,128]{1,0:T(8,128)}) custom-call(f32[2,128,2048]{2,1,0:T(8,128)} %get-tuple-element.119.refs_0_, s32[1]{0:T(128)} %bitcast.59.refs_1_, ...), custom_call_target="tpu_custom_call" | custom-call | flops 16106127360 | bytes 25165824 | tf_op jit(solution)/shard_map/moe_in/pallas_call | solution.py:620
  517.3 23.3 %run_expert.3 = (bf16[768,2048]{1,0:T(8,128)(2,1)}, bf16[768,2048]{1,0:T(8,128)(2,1)}, bf16[2,768,704]{2,1,0:T(8,128)(2,1)}, bf16[768,704]{1,0:T(8,128)(2,1)}, f32[768,1]{1,0:T(8,128)}) custom-call(bf16[768,2048]{1,0:T(8,128)(2,1)} %get-tuple-element.128.refs_0_.refs_4_, bf16[768,2048]{1,0:T(8,128)(2,1)} %get-tuple-element.129.refs_1_.refs_4_, ...), custom_call_target="tpu_custom_call" | custom-call | flops 26575110144 | bytes 29884416 | tf_op jit(solution)/shard_map/run_expert/pallas_call | solution.py:707
  582.5 11.2 %combine.10 = bf16[2048,2048]{1,0:T(8,128)(2,1)} custom-call(f32[2,128,2048]{2,1,0:T(8,128)} %get-tuple-element.132.refs_0_.refs_1_, bf16[2048,256]{1,0:T(8,128)(2,1)} %get-tuple-element.133.refs_1_, bf16[256,2048]{1,0:T(8,128)(2,1)} %pad.17.refs_7_.refs_2_.refs_6_, s32[8,1,256]{2,1,0:T(1,128)} %bitcast.444, bf16[768,2048]{1,0:T(8,128)(2,1)} %get-tuple-element.134.refs_4_, ...), custom_call_target="tpu_custom_call" | custom-call | flops 8858370048 | bytes 11534336 | tf_op jit(solution)/shard_map/combine/pallas_call | solution.py:837
  598.8 11.4 %combine.11 = bf16[2048,2048]{1,0:T(8,128)(2,1)} custom-call(bf16[4,512,2048]{2,1,0:T(8,128)(2,1)} %bitcast.458, bf16[2048,256]{1,0:T(8,128)(2,1)} %get-tuple-element.133.refs_1_, bf16[256,2048]{1,0:T(8,128)(2,1)} %pad.17.refs_7_.refs_2_.refs_6_, s32[8,1,256]{2,1,0:T(1,128)} %bitcast.445, bf16[768,2048]{1,0:T(8,128)(2,1)} %get-tuple-element.134.refs_4_, ...), custom_call_target="tpu_custom_call" | custom-call | flops 8858370048 | bytes 11534336 | tf_op jit(solution)/shard_map/combine/pallas_call | solution.py:837
  610.1 12.9 %collective-permute-done.48.refs_2_ = bf16[2,128,2048]{2,1,0:T(8,128)(2,1)S(1)} collective-permute-done((bf16[2,128,2048]{2,1,0:T(8,128)(2,1)}, bf16[2,128,2048]{2,1,0:T(8,128)(2,1)S(1)}, u32[]{:S(2)}, u32[]{:S(2)}) %collective-permute-start.48) | collective-permute-done | bytes 1048608 | tf_op jit(solution)/shard_map/ppermute | solution.py:30
  634.1 10.3 core_sum.8
  665.3 10.3 weight_sum.5
  677.1 14.1 %weight_sum.4 = bf16[1,512,2048]{2,1,0:T(8,128)(2,1)} custom-call(f32[2,128,2048]{2,1,0:T(8,128)} %last_sum.7.refs_0_.marker_ref, bf16[1,2048,512]{2,1,0:T(8,128)(2,1)} %bitcast.402, bf16[1,2048,512]{2,1,0:T(8,128)(2,1)} %bitcast.403, bf16[1,2048,512]{2,1,0:T(8,128)(2,1)} %bitcast.472, bf16[1,2048,512]{2,1,0:T(8,128)(2,1)} %bitcast.473, ...), custom_call_target="tpu_custom_call" | custom-call | flops 17179869184 | bytes 25165824 | tf_op jit(solution)/shard_map/weight_sum/pallas_call | solution.py:779
  730.8 19.5 %collective-permute-done.60.refs_3_ = bf16[1,64,2048]{2,1,0:T(8,128)(2,1)S(1)} collective-permute-done((bf16[1,64,2048]{2,1,0:T(8,128)(2,1)S(1)}, bf16[1,64,2048]{2,1,0:T(8,128)(2,1)S(1)}, u32[]{:S(2)}, u32[]{:S(2)}) %collective-permute-start.60) | collective-permute-done | bytes 262176 | tf_op jit(solution)/shard_map/ppermute | solution.py:30
  750.3 12.6 %collective-permute-done.61.refs_5_ = bf16[1,64,2048]{2,1,0:T(8,128)(2,1)S(1)} collective-permute-done((bf16[1,64,2048]{2,1,0:T(8,128)(2,1)S(1)}, bf16[1,64,2048]{2,1,0:T(8,128)(2,1)S(1)}, u32[]{:S(2)}, u32[]{:S(2)}) %collective-permute-start.61) | collective-permute-done | bytes 262176 | tf_op jit(solution)/shard_map/ppermute | solution.py:30
  819.5 18.1 %attend_back.1.refs_0_.refs_4_ = bf16[2048,768]{1,0:T(8,128)(2,1)} custom-call(bf16[2048,256]{1,0:T(8,128)(2,1)} %copy-done.41, bf16[16,528,128]{2,1,0:T(8,128)(2,1)} %all-to-all-done.3.refs_1_, bf16[128,2048]{1,0:T(8,128)(2,1)} %copy-done.52, bf16[2048,768]{1,0:T(8,128)(2,1)} %get-tuple-element.99.marker_ref.refs_2_.refs_3_.refs_4_.refs_5_, ...), custom_call_target="tpu_custom_call" | custom-call | flops 20132659200 | bytes 6291456 | tf_op jit(solution)/shard_map/attend_back/pallas_call | solution.py:532
  837.7 10.4 %convolution_convert_fusion = bf16[2048,768]{1,0:T(8,128)(2,1)S(1)} fusion(bf16[2048,2048]{1,0:T(8,128)(2,1)} %get-tuple-element.161, bf16[2048,768]{1,0:T(8,128)(2,1)} %attend_back.1.refs_0_.refs_4_), kind=kOutput, calls=%fused_computation.4 | convolution fusion | flops 6444023808 | bytes 14680064 | tf_op jit(solution)/shard_map/dot_general | solution.py:1192
  861.7 16.9 %weight_sum.6.refs_0_.refs_3_ = f32[2,704,2048]{2,1,0:T(8,128)} custom-call(bf16[2048,768]{1,0:T(8,128)(2,1)} %attend_back.1.refs_0_.refs_4_, bf16[2,768,704]{2,1,0:T(8,128)(2,1)} %get-tuple-element.162.refs_1_, bf16[2,768,704]{2,1,0:T(8,128)(2,1)} %get-tuple-element.163.refs_2_, bf16[768,2048]{1,0:T(8,128)(2,1)} %get-tuple-element.115.refs_0_.refs_3_, ...), custom_call_target="tpu_custom_call" | custom-call | flops 17716740096 | bytes 22151168 | tf_op jit(solution)/shard_map/weight_sum/pallas_call | solution.py:779
  878.6 9.2 weight_sum.7.refs_1_.marker_ref
  947.7 36.5 %collective-permute-done.82 = f32[23,2048]{1,0:T(8,128)} collective-permute-done((f32[23,2048]{1,0:T(8,128)}, f32[23,2048]{1,0:T(8,128)}, u32[]{:S(2)}, u32[]{:S(2)}) %collective-permute-start.82) | collective-permute-done | bytes 188448 | tf_op jit(solution)/shard_map/ppermute | solution.py:34
  (569 shorter events, 523.7 us)
Async XLA Ops:
  34.9 46.8 %collective-permute-start.3 = (bf16[512,768]{0,1:T(8,128)(2,1)}, bf16[512,768]{0,1:T(8,128)(2,1)S(1)}, u32[]{:S(2)}, u32[]{:S(2)}) collective-permute-start(bf16[512,768]{0,1:T(8,128)(2,1)} %get-tuple-element.260), channel_id=1, source_target_pairs={{0,16},{8,24},{16,0},{24,8},{1,17},{9,25},{17,1},{25,9},{2,18},{10... | collective-permute-start | bytes 2359304 | tf_op jit(solution)/shard_map/ppermute | solution.py:34
  60.3 57.9 %collective-permute-start.10 = (bf16[2,128,2048]{2,1,0:T(8,128)(2,1)}, bf16[2,128,2048]{2,1,0:T(8,128)(2,1)}, u32[]{:S(2)}, u32[]{:S(2)}) collective-permute-start(bf16[2,128,2048]{2,1,0:T(8,128)(2,1)} %get-tuple-element.97.refs_4_.marker_ref), channel_id=1, source_target_pairs={{0,4},{4,0},{1,5},{5,1},{2,6},{6,2},{3,7},{7,3},{8,12},{12,8},{9,1... | collective-permute-start | bytes 3145736 | tf_op jit(solution)/shard_map/ppermute | solution.py:30
  61.0 57.2 %collective-permute-start.11 = (bf16[2,128,2048]{2,1,0:T(8,128)(2,1)}, bf16[2,128,2048]{2,1,0:T(8,128)(2,1)}, u32[]{:S(2)}, u32[]{:S(2)}) collective-permute-start(bf16[2,128,2048]{2,1,0:T(8,128)(2,1)} %get-tuple-element.98.refs_6_), channel_id=1, source_target_pairs={{0,1},{1,0},{2,3},{3,2},{4,5},{5,4},{6,7},{7,6},{8,9},{9,8},{10,11... | collective-permute-start | bytes 3145736 | tf_op jit(solution)/shard_map/ppermute | solution.py:30
  61.5 40.4 %collective-permute-start = (bf16[128,2048]{1,0:T(8,128)(2,1)S(1)}, bf16[128,2048]{1,0:T(8,128)(2,1)S(1)}, u32[]{:S(2)}, u32[]{:S(2)}) collective-permute-start(bf16[128,2048]{1,0:T(8,128)(2,1)S(1)} %copy-done.14), channel_id=1, source_target_pairs={{0,8},{8,0},{16,24},{24,16},{1,9},{9,1},{17,25},{25,17},{2,10},{10... | collective-permute-start | bytes 1572872 | tf_op jit(solution)/shard_map/ppermute | solution.py:34
  122.9 71.6 %collective-permute-start.12 = (bf16[2,512,2048]{2,1,0:T(8,128)(2,1)}, bf16[2,512,2048]{2,1,0:T(8,128)(2,1)}, u32[]{:S(2)}, u32[]{:S(2)}) collective-permute-start(bf16[2,512,2048]{2,1,0:T(8,128)(2,1)} %plane.5), channel_id=1, source_target_pairs={{0,2},{2,0},{1,3},{3,1},{4,6},{6,4},{5,7},{7,5},{8,10},{10,8},{9,1... | collective-permute-start | bytes 12582920 | tf_op jit(solution)/shard_map/ppermute | solution.py:30
  131.7 45.3 %collective-permute-start.13 = (bf16[2,512,768]{1,2,0:T(8,128)(2,1)}, bf16[2,512,768]{1,2,0:T(8,128)(2,1)}, u32[]{:S(2)}, u32[]{:S(2)}) collective-permute-start(bf16[2,512,768]{1,2,0:T(8,128)(2,1)} %pad_maximum_fusion.1), channel_id=1, source_target_pairs={{0,8},{8,0},{16,24},{24,16},{1,9},{9,1},{17,25},{25,17},{2,10},{10... | collective-permute-start | bytes 4718600 | tf_op jit(solution)/shard_map/ppermute | solution.py:34
  174.0 46.9 %collective-permute-start.19 = (bf16[4,128,2048]{2,1,0:T(8,128)(2,1)}, bf16[4,128,2048]{2,1,0:T(8,128)(2,1)}, u32[]{:S(2)}, u32[]{:S(2)}) collective-permute-start(bf16[4,128,2048]{2,1,0:T(8,128)(2,1)} %get-tuple-element.100.refs_1_), channel_id=1, source_target_pairs={{0,4},{4,0},{1,5},{5,1},{2,6},{6,2},{3,7},{7,3},{8,12},{12,8},{9,1... | collective-permute-start | bytes 6291464 | tf_op jit(solution)/shard_map/ppermute | solution.py:30
  175.3 46.7 %collective-permute-start.20 = (bf16[4,128,2048]{2,1,0:T(8,128)(2,1)}, bf16[4,128,2048]{2,1,0:T(8,128)(2,1)}, u32[]{:S(2)}, u32[]{:S(2)}) collective-permute-start(bf16[4,128,2048]{2,1,0:T(8,128)(2,1)} %get-tuple-element.101.refs_3_), channel_id=1, source_target_pairs={{0,1},{1,0},{2,3},{3,2},{4,5},{5,4},{6,7},{7,6},{8,9},{9,8},{10,11... | collective-permute-start | bytes 6291464 | tf_op jit(solution)/shard_map/ppermute | solution.py:30
  300.1 129.0 %collective-permute-start.38 = (bf16[4,512,2048]{2,1,0:T(8,128)(2,1)}, bf16[4,512,2048]{2,1,0:T(8,128)(2,1)}, u32[]{:S(2)}, u32[]{:S(2)}) collective-permute-start(bf16[4,512,2048]{2,1,0:T(8,128)(2,1)} %plane.7), channel_id=1, source_target_pairs={{0,2},{2,0},{1,3},{3,1},{4,6},{6,4},{5,7},{7,5},{8,10},{10,8},{9,1... | collective-permute-start | bytes 25165832 | tf_op jit(solution)/shard_map/ppermute | solution.py:30
  303.7 47.4 %collective-permute-start.28 = (bf16[128,2048]{1,0:T(8,128)(2,1)S(1)}, bf16[128,2048]{1,0:T(8,128)(2,1)S(1)}, u32[]{:S(2)}, u32[]{:S(2)}) collective-permute-start(bf16[128,2048]{1,0:T(8,128)(2,1)S(1)} %copy-done.7), channel_id=1, source_target_pairs={{0,16},{8,24},{16,0},{24,8},{1,17},{9,25},{17,1},{25,9},{2,18},{10... | collective-permute-start | bytes 1572872 | tf_op jit(solution)/shard_map/ppermute | solution.py:34
  363.0 62.6 %all-to-all-start.1 = ((bf16[16,528,128]{2,1,0:T(8,128)(2,1)}), bf16[16,528,128]{2,1,0:T(8,128)(2,1)S(1)}, u32[]{:S(2)}, u32[]{:S(2)}) async-start(bf16[16,528,128]{2,1,0:T(8,128)(2,1)} %maximum_select_fusion), calls=%async_computation.1 | async-start | bytes 4325376 | tf_op jit(solution)/shard_map/all_to_all | solution.py:255
  424.7 44.4 %collective-permute-start.39 = (bf16[2,128,2048]{2,1,0:T(8,128)(2,1)}, bf16[2,128,2048]{2,1,0:T(8,128)(2,1)S(1)}, u32[]{:S(2)}, u32[]{:S(2)}) collective-permute-start(bf16[2,128,2048]{2,1,0:T(8,128)(2,1)} %get-tuple-element.112.refs_0_.refs_1_), channel_id=1, source_target_pairs={{0,4},{4,0},{1,5},{5,1},{2,6},{6,2},{3,7},{7,3},{8,12},{12,8},{9,1... | collective-permute-start | bytes 3145736 | tf_op jit(solution)/shard_map/ppermute | solution.py:30
  424.7 44.4 %collective-permute-start.40 = (bf16[2,128,2048]{2,1,0:T(8,128)(2,1)}, bf16[2,128,2048]{2,1,0:T(8,128)(2,1)}, u32[]{:S(2)}, u32[]{:S(2)}) collective-permute-start(bf16[2,128,2048]{2,1,0:T(8,128)(2,1)} %get-tuple-element.114.refs_3_), channel_id=1, source_target_pairs={{0,1},{1,0},{2,3},{3,2},{4,5},{5,4},{6,7},{7,6},{8,9},{9,8},{10,11... | collective-permute-start | bytes 3145736 | tf_op jit(solution)/shard_map/ppermute | solution.py:30
  497.2 43.4 %collective-permute-start.42 = (bf16[2,128,2048]{2,1,0:T(8,128)(2,1)}, bf16[2,128,2048]{2,1,0:T(8,128)(2,1)S(1)}, u32[]{:S(2)}, u32[]{:S(2)}) collective-permute-start(bf16[2,128,2048]{2,1,0:T(8,128)(2,1)} %get-tuple-element.120), channel_id=1, source_target_pairs={{0,4},{4,0},{1,5},{5,1},{2,6},{6,2},{3,7},{7,3},{8,12},{12,8},{9,1... | collective-permute-start | bytes 3145736 | tf_op jit(solution)/shard_map/ppermute | solution.py:30
  499.2 41.5 %collective-permute-start.43 = (bf16[2,128,2048]{2,1,0:T(8,128)(2,1)}, bf16[2,128,2048]{2,1,0:T(8,128)(2,1)S(1)}, u32[]{:S(2)}, u32[]{:S(2)}) collective-permute-start(bf16[2,128,2048]{2,1,0:T(8,128)(2,1)} %get-tuple-element.122), channel_id=1, source_target_pairs={{0,1},{1,0},{2,3},{3,2},{4,5},{5,4},{6,7},{7,6},{8,9},{9,8},{10,11... | collective-permute-start | bytes 3145736 | tf_op jit(solution)/shard_map/ppermute | solution.py:30
  593.7 40.3 %collective-permute-start.50 = (bf16[4,512,2048]{2,1,0:T(8,128)(2,1)}, bf16[4,512,2048]{2,1,0:T(8,128)(2,1)}, u32[]{:S(2)}, u32[]{:S(2)}) collective-permute-start(bf16[4,512,2048]{2,1,0:T(8,128)(2,1)} %bitcast.457), channel_id=1, source_target_pairs={{0,2},{2,0},{1,3},{3,1},{4,6},{6,4},{5,7},{7,5},{8,10},{10,8},{9,1... | collective-permute-start | bytes 25165832 | tf_op jit(solution)/shard_map/ppermute | solution.py:30
  634.1 92.3 %collective-permute-start.55 = (bf16[128,2048]{1,0:T(8,128)(2,1)}, bf16[128,2048]{1,0:T(8,128)(2,1)}, u32[]{:S(2)}, u32[]{:S(2)}) collective-permute-start(bf16[128,2048]{1,0:T(8,128)(2,1)} %fusion.28), channel_id=1, source_target_pairs={{0,8},{8,0},{16,24},{24,16},{1,9},{9,1},{17,25},{25,17},{2,10},{10... | collective-permute-start | bytes 1572872 | tf_op jit(solution)/shard_map/ppermute | solution.py:34
  653.5 45.4 %all-to-all-start.2 = ((f32[32,2,128]{2,1,0:T(2,128)}), f32[32,2,128]{2,1,0:T(2,128)S(1)}, u32[]{:S(2)}, u32[]{:S(2)}) async-start(f32[32,2,128]{2,1,0:T(2,128)} %reshape.398), calls=%async_computation.2 | async-start | bytes 65536 | tf_op jit(solution)/shard_map/all_to_all | solution.py:255
  658.7 67.7 %collective-permute-start.57 = (bf16[128,2048]{1,0:T(8,128)(2,1)}, bf16[128,2048]{1,0:T(8,128)(2,1)}, u32[]{:S(2)}, u32[]{:S(2)}) collective-permute-start(bf16[128,2048]{1,0:T(8,128)(2,1)} %get-tuple-element.250), channel_id=1, source_target_pairs={{0,24},{8,16},{16,8},{24,0},{1,25},{9,17},{17,9},{25,1},{2,26},{10... | collective-permute-start | bytes 1572872 | tf_op jit(solution)/shard_map/ppermute | solution.py:34
  662.3 64.1 %collective-permute-start.56 = (bf16[128,2048]{1,0:T(8,128)(2,1)}, bf16[128,2048]{1,0:T(8,128)(2,1)}, u32[]{:S(2)}, u32[]{:S(2)}) collective-permute-start(bf16[128,2048]{1,0:T(8,128)(2,1)} %get-tuple-element.249), channel_id=1, source_target_pairs={{0,16},{8,24},{16,0},{24,8},{1,17},{9,25},{17,1},{25,9},{2,18},{10... | collective-permute-start | bytes 1572872 | tf_op jit(solution)/shard_map/ppermute | solution.py:34
  662.3 49.7 %collective-permute-start.53 = (bf16[4,128,2048]{2,1,0:T(8,128)(2,1)}, bf16[4,128,2048]{2,1,0:T(8,128)(2,1)}, u32[]{:S(2)}, u32[]{:S(2)}) collective-permute-start(bf16[4,128,2048]{2,1,0:T(8,128)(2,1)} %get-tuple-element.145), channel_id=1, source_target_pairs={{0,4},{4,0},{1,5},{5,1},{2,6},{6,2},{3,7},{7,3},{8,12},{12,8},{9,1... | collective-permute-start | bytes 6291464 | tf_op jit(solution)/shard_map/ppermute | solution.py:30
  663.8 48.2 %collective-permute-start.54 = (bf16[4,128,2048]{2,1,0:T(8,128)(2,1)}, bf16[4,128,2048]{2,1,0:T(8,128)(2,1)}, u32[]{:S(2)}, u32[]{:S(2)}) collective-permute-start(bf16[4,128,2048]{2,1,0:T(8,128)(2,1)} %get-tuple-element.147), channel_id=1, source_target_pairs={{0,1},{1,0},{2,3},{3,2},{4,5},{5,4},{6,7},{7,6},{8,9},{9,8},{10,11... | collective-permute-start | bytes 6291464 | tf_op jit(solution)/shard_map/ppermute | solution.py:30
  698.9 101.0 %all-to-all-start.3 = ((bf16[16,528,128]{2,1,0:T(8,128)(2,1)}), bf16[16,528,128]{2,1,0:T(8,128)(2,1)}, u32[]{:S(2)}, u32[]{:S(2)}) async-start(bf16[16,528,128]{2,1,0:T(8,128)(2,1)} %maximum_bitcast_fusion), calls=%async_computation.3 | async-start | bytes 4325376 | tf_op jit(solution)/shard_map/all_to_all | solution.py:255
  721.4 41.4 %collective-permute-start.58 = (bf16[4,64,2048]{2,1,0:T(8,128)(2,1)}, bf16[4,64,2048]{2,1,0:T(8,128)(2,1)S(1)}, u32[]{:S(2)}, u32[]{:S(2)}) collective-permute-start(bf16[4,64,2048]{2,1,0:T(8,128)(2,1)} %get-tuple-element.153), channel_id=1, source_target_pairs={{0,1},{1,0},{2,3},{3,2},{4,5},{5,4},{6,7},{7,6},{8,9},{9,8},{10,11... | collective-permute-start | bytes 3145736 | tf_op jit(solution)/shard_map/ppermute | solution.py:30
  722.8 40.0 %collective-permute-start.59 = (bf16[4,64,2048]{2,1,0:T(8,128)(2,1)}, bf16[4,64,2048]{2,1,0:T(8,128)(2,1)S(1)}, u32[]{:S(2)}, u32[]{:S(2)}) collective-permute-start(bf16[4,64,2048]{2,1,0:T(8,128)(2,1)} %get-tuple-element.155), channel_id=1, source_target_pairs={{0,4},{4,0},{1,5},{5,1},{2,6},{6,2},{3,7},{7,3},{8,12},{12,8},{9,1... | collective-permute-start | bytes 3145736 | tf_op jit(solution)/shard_map/ppermute | solution.py:30
  795.1 56.8 %collective-permute-start.66 = (bf16[128,2048]{1,0:T(8,128)(2,1)}, bf16[128,2048]{1,0:T(8,128)(2,1)}, u32[]{:S(2)}, u32[]{:S(2)}) collective-permute-start(bf16[128,2048]{1,0:T(8,128)(2,1)} %get-tuple-element.239), channel_id=1, source_target_pairs={{0,16},{8,24},{16,0},{24,8},{1,17},{9,25},{17,1},{25,9},{2,18},{10... | collective-permute-start | bytes 1572872 | tf_op jit(solution)/shard_map/ppermute | solution.py:34
  796.1 95.0 %collective-permute-start.67 = (bf16[128,2048]{1,0:T(8,128)(2,1)}, bf16[128,2048]{1,0:T(8,128)(2,1)}, u32[]{:S(2)}, u32[]{:S(2)}) collective-permute-start(bf16[128,2048]{1,0:T(8,128)(2,1)} %get-tuple-element.238), channel_id=1, source_target_pairs={{0,24},{8,16},{16,8},{24,0},{1,25},{9,17},{17,9},{25,1},{2,26},{10... | collective-permute-start | bytes 1572872 | tf_op jit(solution)/shard_map/ppermute | solution.py:34
  851.0 74.6 %collective-permute-start.68 = (bf16[2,512,768]{2,1,0:T(8,128)(2,1)}, bf16[2,512,768]{2,1,0:T(8,128)(2,1)}, u32[]{:S(2)}, u32[]{:S(2)}) collective-permute-start(bf16[2,512,768]{2,1,0:T(8,128)(2,1)} %dynamic-slice_bitcast_fusion.refs_1_), channel_id=1, source_target_pairs={{0,8},{8,0},{16,24},{24,16},{1,9},{9,1},{17,25},{25,17},{2,10},{10... | collective-permute-start | bytes 4718600 | tf_op jit(solution)/shard_map/ppermute | solution.py:34
  861.7 64.0 %collective-permute-start.72 = (bf16[2,512,2048]{2,1,0:T(8,128)(2,1)}, bf16[2,512,2048]{2,1,0:T(8,128)(2,1)}, u32[]{:S(2)}, u32[]{:S(2)}) collective-permute-start(bf16[2,512,2048]{2,1,0:T(8,128)(2,1)} %bitcast.461), channel_id=1, source_target_pairs={{0,2},{2,0},{1,3},{3,1},{4,6},{6,4},{5,7},{7,5},{8,10},{10,8},{9,1... | collective-permute-start | bytes 12582920 | tf_op jit(solution)/shard_map/ppermute | solution.py:30
  932.3 53.6 %collective-permute-start.73 = (bf16[2,128,2048]{2,1,0:T(8,128)(2,1)}, bf16[2,128,2048]{2,1,0:T(8,128)(2,1)}, u32[]{:S(2)}, u32[]{:S(2)}) collective-permute-start(bf16[2,128,2048]{2,1,0:T(8,128)(2,1)} %get-tuple-element.169), channel_id=1, source_target_pairs={{0,4},{4,0},{1,5},{5,1},{2,6},{6,2},{3,7},{7,3},{8,12},{12,8},{9,1... | collective-permute-start | bytes 3145736 | tf_op jit(solution)/shard_map/ppermute | solution.py:30
  934.3 51.6 %collective-permute-start.74 = (bf16[2,128,2048]{2,1,0:T(8,128)(2,1)}, bf16[2,128,2048]{2,1,0:T(8,128)(2,1)}, u32[]{:S(2)}, u32[]{:S(2)}) collective-permute-start(bf16[2,128,2048]{2,1,0:T(8,128)(2,1)} %get-tuple-element.171), channel_id=1, source_target_pairs={{0,1},{1,0},{2,3},{3,2},{4,5},{5,4},{6,7},{7,6},{8,9},{9,8},{10,11... | collective-permute-start | bytes 3145736 | tf_op jit(solution)/shard_map/ppermute | solution.py:30
  938.2 47.7 %collective-permute-start.69 = (bf16[512,768]{1,0:T(8,128)(2,1)}, bf16[512,768]{1,0:T(8,128)(2,1)}, u32[]{:S(2)}, u32[]{:S(2)}) collective-permute-start(bf16[512,768]{1,0:T(8,128)(2,1)} %fusion.25), channel_id=1, source_target_pairs={{0,16},{8,24},{16,0},{24,8},{1,17},{9,25},{17,1},{25,9},{2,18},{10... | collective-permute-start | bytes 2359304 | tf_op jit(solution)/shard_map/ppermute | solution.py:34
  (150 other events, 2124.7 us)

commit v4 on v3

--- a/solution.py
+++ b/solution.py
@@ -247,7 +247,8 @@
     marks = [send, cross(send, 1)]
     keep = keep.astype(F32) + marks[1].astype(F32)
     keep, send = split(keep, z // 2, 0)
-    marks.append(cross(send.astype(BF16), 2))
+    send = send.astype(BF16)
+    marks += [cross(send, 2), send]
     return (keep + marks[2].astype(F32)).astype(BF16), marks
 
 
@@ -597,7 +598,7 @@
     )
 
 
-def moe_in(after, expert, rows, grads, chunk, w_in, w_dn, slot_rows, experts, own, capacity):
+def moe_in(after, expert, rows, grads, w_in, w_dn, slot_rows, experts, own, capacity):
     blocks, _, step = slot_rows.shape
     model = rows[0].shape[1]
     held = w_dn.shape[0]
@@ -607,13 +608,6 @@
     def row_spec(core):
         def block(i):
             return jnp.maximum(i - half, 0) if core else jnp.minimum(i, half - 1)
-
-        return pl.BlockSpec((step, model), lambda i: (block(i), 0))
-
-    def grad_spec(core):
-        def block(i):
-            i = jnp.maximum(i - half, 0) if core else jnp.minimum(i, half - 1)
-            return ((i // 4) * 2 + chunk) * 4 + i % 4
 
         return pl.BlockSpec((step, model), lambda i: (block(i), 0))
 
@@ -625,8 +619,8 @@
             pl.BlockSpec(memory_space=pltpu.SMEM),
             row_spec(0),
             row_spec(1),
-            grad_spec(0),
-            grad_spec(1),
+            row_spec(0),
+            row_spec(1),
             pl.BlockSpec((2 * held, model), lambda i: (0, 0)),
             pl.BlockSpec((held, model), lambda i: (0, 0)),
             pl.BlockSpec((1, 1, step), lambda i: (i, 0, 0)),
@@ -955,8 +949,6 @@
     numbers_before = jnp.where(z == 0, -1, lax.ppermute(numbers_here, "z", ahead))
 
     before = lax.ppermute(own_attn, "z", ahead)
-    crossed = [cross(cotangent, offset) for offset in range(1, LINE)]
-
     def cut_heads(value):
         return value.reshape(weight_rows, -1, 4, cols).transpose(2, 0, 1, 3)
 
@@ -968,10 +960,9 @@
     qkv_across = cross(qkv_rows, 2)
     later = tick(w_heads)
     attn_pairs, attn_plane, _ = slot_pair(jnp.stack([before, own_attn]), (w_heads, numbers_before))
-    rows_attn = attn_plane(tuple(crossed) + (qkv_across,))
-    grad_pairs, grad_plane, grad_arrived = slot_pair(
-        hold(jnp.stack([cotangent] + crossed), tick(attn_pairs[0])), ()
-    )
+    rows_attn = attn_plane((qkv_across,))
+    grad_late = hold(cotangent, tick(rows_attn[0]))
+    grad_crossed = [cross(grad_late, offset) for offset in range(1, LINE)]
     w_qkv, qkv_others = gather_line(qkv_rows, qkv_across)
     if groups > 1:
         w_qkv = lax.all_gather(w_qkv, "g", axis=0, tiled=True)
@@ -1011,19 +1002,26 @@
     near = jnp.concatenate([numbers_before, numbers_here], 1)
     seg_k, valid_k = near[:1], near[1:]
     seg_q = numbers_here[0].reshape(plane_rows, 1)
-    attended = attend(grad_arrived, projected, seg_q, seg_k, valid_k)
+    attended = attend((grad_crossed[1],), projected, seg_q, seg_k, valid_k)
     w_out_t = w_out.T
-    (send,) = spread((), order_one, attended, w_out_t, 1)
+    (send,) = spread((grad_crossed[0],), order_one, attended, w_out_t, 1)
     (keep,) = spread((send,), order_one, attended, w_out_t, 0)
-    attn_rows = slot_scatter(keep, send, (slot_here.reshape(-1, blocks),), (), ())[0][0]
+    attn_rows = slot_scatter(
+        keep, send, (slot_here.reshape(-1, blocks),), (), (grad_crossed[2],)
+    )[0][0]
     middle = residual + attn_rows
     scale_moe = norm_scale(middle)
     own_moe = (middle * scale_moe * gain_moe).astype(BF16)
-    all_grads = [half.reshape(-1, model) for half in grad_plane((own_moe,))]
+    grad_pairs, grad_plane, grad_arrived = slot_pair(
+        hold(jnp.stack([cotangent, grad_crossed[0]]), tick(own_moe)), ()
+    )
     crossed = [cross(own_moe, offset) for offset in range(1, LINE)]
-    near_pairs, near_plane, _ = slot_pair(jnp.stack([own_moe, crossed[0]]), tuple(crossed[1:]))
+    near_pairs, near_plane, _ = slot_pair(
+        jnp.stack([own_moe, crossed[0]]), tuple(crossed[1:]) + grad_arrived
+    )
     w_shared = exchange(hold(shared_cut, tick(near_pairs[0])), everywhere)
     near_rows = near_plane(())
+    near_grads = grad_plane((near_pairs[0],))
     far_pairs, far_plane, _ = slot_pair(hold(jnp.stack(crossed[1:]), tick(near_rows[0])), ())
     def whole_slots(halves):
         halves = [half.reshape(-1, model) for half in halves]
@@ -1031,8 +1029,7 @@
             halves = [lax.all_gather(half, "g", axis=0, tiled=True) for half in halves]
         return halves
 
-    all_grads = whole_slots(all_grads)
-    chunk_rows = [whole_slots(near_rows)]
+    chunk_rows, chunk_grads = [whole_slots(near_rows)], [whole_slots(near_grads)]
 
     w_shared = w_shared.transpose(1, 0, 2).reshape(3 * own, model)
 
@@ -1071,7 +1068,7 @@
     def enter_chunk(chunk, after):
         act, hid, sig, erow, egrad, egate = moe_in(
             after, expert_id,
-            chunk_rows[chunk], all_grads, chunk, shared_in, shared_dn, tables[chunk],
+            chunk_rows[chunk], chunk_grads[chunk], shared_in, shared_dn, tables[chunk],
             experts, own, capacity,
         )
         signals.append(sig.reshape(-1, blocks))
@@ -1095,12 +1092,17 @@
     def moe_term(chunk):
         return [(hiddens[chunk], shared_dn, tables[chunk], results[chunk])]
 
-    entered = enter_chunk(0, (far_pairs[0],))
+    grad_pairs, grad_plane, _ = slot_pair(
+        hold(jnp.stack(grad_crossed[1:]), tick(near_rows[0])), (far_pairs[0],)
+    )
+    entered = enter_chunk(0, (far_pairs[0], grad_pairs[0]))
     far_rows = far_plane((acts[0],))
     chunk_rows.append(whole_slots(far_rows))
     run_chunk(0, (), *entered)
+    far_grads = grad_plane((backs[0],))
+    chunk_grads.append(whole_slots(far_grads))
     send = core_part((far_rows[0],), grad_term(0), 1)
-    keep = core_part((send,), grad_term(0), 0)
+    keep = core_part((send, far_grads[0]), grad_term(0), 0)
     near_steps = scatter_core(keep, send, ())
     run_chunk(1, (), *enter_chunk(1, (near_steps[0],)))
     near_steps = scatter_pair(near_steps, ())
@@ -1140,7 +1142,7 @@
     grad_sdn = weight_sum(
         shared_time,
         [
-            (hiddens[chunk][None], core * groups, all_grads[core], 2, chunk)
+            (hiddens[chunk][None], core * groups, chunk_grads[chunk][core], 1, 0)
             for chunk in tiles
             for core in tiles
         ],
@@ -1220,7 +1222,7 @@
         (qkv_marks[0], out_marks[1], moe_cross[1]),
         order_two, grad_projected, w_qkv_t, 1, rows_attn[1],
     )
-    keep, sum_keep = spread((send, moe_cross[2], grad_egu), order_two, grad_projected, w_qkv_t, 0, rows_attn[0])
+    keep, sum_keep = spread((send, moe_cross[2], grad_egu, qkv_marks[3]), order_two, grad_projected, w_qkv_t, 0, rows_attn[0])
     gain_sum = (sum_send + sum_keep)[0] / gain_attn
     bias_sum = jnp.sum(grad_projected.astype(F32), axis=0).reshape(3, cols)
     grad_bias = lax.dynamic_update_slice_in_dim(jnp.zeros((3, model), F32), bias_sum, here, 1)
@@ -1244,7 +1246,7 @@
         )
     )
     back_both, _ = slot_scatter(
-        keep, send, (qkv_marks[1], out_marks[2]), (qkv_marks[2], grad_edown), ()
+        keep, send, (), (qkv_marks[2], out_marks[2], grad_edown), ()
     )
     back_own = back_both[1] + lax.ppermute(back_both[0].astype(BF16), "z", behind).astype(F32)
     input_grad = grad_middle + norm_back(residual, scale_attn, gain_attn, back_own)

time: 1040 us -> 1000 us (0.962)
  waiting for transfers between devices: 320 us -> 284 us
  starting transfers between devices: 141 us -> 117 us
    ppermute x25, starting transfers between devices: 63.2 us -> 35.7 us  [cross(): return lax.ppermute(value, 'z', [(k, k ^ offset) for k in range(LINE)])]
    ppermute x25, waiting for transfers between devices: 124 us -> 113 us  [cross(): return lax.ppermute(value, 'z', [(k, k ^ offset) for k in range(LINE)])]
    ppermute x1, waiting for transfers between devices: 12.5 us -> 1.34 us  [per_device(): lax.ppermute(numbers_here, 'z', ahead)]
    pallas_call x25 -> x27, Pallas kernels: 125 us -> 131 us  [stage(): pl.pallas_call(without(len(after), kernel), grid=(count, parts), in_specs...]
    ppermute x55 -> x60, waiting for transfers between devices: 166 us -> 161 us  [swap(): return lax.ppermute(value, axis, SWAP)]
    unnamed x195 -> x227, local copies, waits for them, and re-layouts: 30.1 us -> 34.6 us
    ppermute x55 -> x60, starting transfers between devices: 47.9 us -> 46.2 us  [swap(): return lax.ppermute(value, axis, SWAP)]
  transfers between devices with their start and end apart: 89 -> 94, of which waited for: 37 -> 40; matrix products, arithmetic and copies ran while one was open for 12% -> 13% of each run, Pallas kernels for 32% -> 36%
where the time goes in v4:
time: 1000 us; the launch traced here: 992 us
  Pallas kernels  411 us (41%)
  waiting for transfers between devices  284 us (28%)
  starting transfers between devices  117 us (12%)
  local copies, waits for them, and re-layouts  90.2 us (9%)
  other arithmetic  61.7 us (6%)
  matrix products  14.7 us (1%)
  between operations  12.6 us (1%)
    ppermute x60, waiting for transfers between devices, swap(): return lax.ppermute(value, axis, SWAP)  161 us
    pallas_call x27, Pallas kernels, stage(): pl.pallas_call(without(len(after), kernel), grid=(count, parts), in_specs...  131 us
    ppermute x25, waiting for transfers between devices, cross(): return lax.ppermute(value, 'z', [(k, k ^ offset) for k in range(LINE)])  113 us
    pallas_call x6, Pallas kernels, combine(): pl.pallas_call(without(len(after), functools.partial(combine_kernel, capa...  52.4 us
    pallas_call x4, Pallas kernels, weight_sum(): pl.pallas_call(without(len(after), sum_kernel), grid=(parts, steps, steps...  50.6 us
    pallas_call x2, Pallas kernels, run_expert(): pl.pallas_call(without(len(after), functools.partial(expert_kernel, steps...  46.6 us
    ppermute x60, starting transfers between devices, swap(): return lax.ppermute(value, axis, SWAP)  46.2 us
    ppermute x25, starting transfers between devices, cross(): return lax.ppermute(value, 'z', [(k, k ^ offset) for k in range(LINE)])  35.7 us
  transfers between devices with their start and end apart: 94, of which 40 were waited for; matrix products, arithmetic and copies ran while one was open for 13% of the time, Pallas kernels for 36%

profile of v4, /device:TPU:0, one launch (start us, length us, event | category | flops | bytes accessed | tf_op | source)
XLA Modules:
  0.0 991.6 jit_solution(11340047494644763700)
XLA Ops:
  15.7 8.0 collective-permute-done.1
  53.2 32.4 %collective-permute-done = bf16[512,768]{0,1:T(8,128)(2,1)S(1)} collective-permute-done((bf16[512,768]{0,1:T(8,128)(2,1)S(1)}, bf16[512,768]{0,1:T(8,128)(2,1)S(1)}, u32[]{:S(2)}, u32[]{:S(2)}) %collective-permute-start) | collective-permute-done | bytes 786464 | tf_op jit(solution)/shard_map/ppermute | solution.py:34
  113.0 33.5 %collective-permute-done.11 = bf16[2,512,768]{1,2,0:T(8,128)(2,1)} collective-permute-done((bf16[2,512,768]{1,2,0:T(8,128)(2,1)}, bf16[2,512,768]{1,2,0:T(8,128)(2,1)}, u32[]{:S(2)}, u32[]{:S(2)}) %collective-permute-start.11) | collective-permute-done | bytes 1572896 | tf_op jit(solution)/shard_map/ppermute | solution.py:34
  162.3 14.4 %project.2 = (bf16[2048,2048]{1,0:T(8,128)(2,1)}, bf16[2048,768]{1,0:T(8,128)(2,1)}) custom-call(s32[9]{0:T(128)} %concatenate.61.refs_0_, bf16[1024,2048]{1,0:T(8,128)(2,1)} %bitcast.366, bf16[1024,2048]{1,0:T(8,128)(2,1)} %bitcast.26.refs_2_.refs_6_, bf16[2048,768]{1,0:T(8,128)(2,1)} %copy.160.refs_3_, f32[1,768]{1,0:T(1,128)} %bitcast.455, ...), custom_call_target="tpu_custom_call" | custom-call | flops 19327352832 | bytes 23068672 | tf_op jit(solution)/shard_map/project/pallas_call | solution.py:337
  182.1 11.1 %attend.1.refs_2_ = bf16[1024,256]{1,0:T(8,128)(2,1)} custom-call(bf16[128,2048]{1,0:T(8,128)(2,1)} %copy-done.57, bf16[2048,768]{1,0:T(8,128)(2,1)} %get-tuple-element.101.marker_ref.refs_1_.refs_2_.refs_3_.refs_4_.refs_5_, bf16[2048,768]{1,0:T(8,128)(2,1)} %get-tuple-element.101.marker_ref.refs_1_.refs_2_.refs_3_.refs_4_.refs_5_, ...), custom_call_target="tpu_custom_call" | custom-call | flops 12079595520 | bytes 4194304 | tf_op jit(solution)/shard_map/attend/pallas_call | solution.py:465
  220.8 10.4 %collective-permute-done.20.refs_1_ = bf16[1,128,2048]{2,1,0:T(8,128)(2,1)S(1)} collective-permute-done((bf16[1,128,2048]{2,1,0:T(8,128)(2,1)}, bf16[1,128,2048]{2,1,0:T(8,128)(2,1)S(1)}, u32[]{:S(2)}, u32[]{:S(2)}) %collective-permute-start.20) | collective-permute-done | bytes 524320 | tf_op jit(solution)/shard_map/ppermute | solution.py:30
  275.4 10.1 %collective-permute-done.30 = bf16[128,2048]{1,0:T(8,128)(2,1)S(1)} collective-permute-done((bf16[128,2048]{1,0:T(8,128)(2,1)S(1)}, bf16[128,2048]{1,0:T(8,128)(2,1)S(1)}, u32[]{:S(2)}, u32[]{:S(2)}) %collective-permute-start.30) | collective-permute-done | bytes 524320 | tf_op jit(solution)/shard_map/ppermute | solution.py:34
  288.0 16.3 %collective-permute-done.24.refs_0_ = bf16[128,2048]{1,0:T(8,128)(2,1)S(1)} collective-permute-done((bf16[128,2048]{1,0:T(8,128)(2,1)S(1)}, bf16[128,2048]{1,0:T(8,128)(2,1)S(1)}, u32[]{:S(2)}, u32[]{:S(2)}) %collective-permute-start.24) | collective-permute-done | bytes 524320 | tf_op jit(solution)/shard_map/ppermute | solution.py:34
  326.9 20.9 %collective-permute-done.33.refs_1_ = bf16[2,128,2048]{2,1,0:T(8,128)(2,1)} collective-permute-done((bf16[2,128,2048]{2,1,0:T(8,128)(2,1)}, bf16[2,128,2048]{2,1,0:T(8,128)(2,1)}, u32[]{:S(2)}, u32[]{:S(2)}) %collective-permute-start.33) | collective-permute-done | bytes 1048608 | tf_op jit(solution)/shard_map/ppermute | solution.py:30
  358.1 12.4 %collective-permute-done.35.refs_1_ = bf16[2,64,2048]{2,1,0:T(8,128)(2,1)S(1)} collective-permute-done((bf16[2,64,2048]{2,1,0:T(8,128)(2,1)S(1)}, bf16[2,64,2048]{2,1,0:T(8,128)(2,1)S(1)}, u32[]{:S(2)}, u32[]{:S(2)}) %collective-permute-start.35) | collective-permute-done | bytes 524320 | tf_op jit(solution)/shard_map/ppermute | solution.py:30
  395.9 16.6 %moe_in.2 = (bf16[2048,512]{1,0:T(8,128)(2,1)}, bf16[2048,256]{1,0:T(8,128)(2,1)}, f32[2048,1]{1,0:T(8,128)}, bf16[768,2048]{1,0:T(8,128)(2,1)}, bf16[768,2048]{1,0:T(8,128)(2,1)}, /*index=5*/f32[768,128]{1,0:T(8,128)}) custom-call(bf16[2,128,2048]{2,1,0:T(8,128)(2,1)} %get-tuple-element.114.refs_0_.refs_1_, ...), custom_call_target="tpu_custom_call" | custom-call | flops 16106127360 | bytes 25165824 | tf_op jit(solution)/shard_map/moe_in/pallas_call | solution.py:614
  412.5 23.3 %run_expert.2 = (bf16[768,2048]{1,0:T(8,128)(2,1)}, bf16[768,2048]{1,0:T(8,128)(2,1)}, bf16[2,768,704]{2,1,0:T(8,128)(2,1)}, bf16[768,704]{1,0:T(8,128)(2,1)}, f32[768,1]{1,0:T(8,128)}) custom-call(bf16[768,2048]{1,0:T(8,128)(2,1)} %get-tuple-element.118.refs_0_.refs_3_, bf16[768,2048]{1,0:T(8,128)(2,1)} %get-tuple-element.119.refs_1_.refs_3_, ...), custom_call_target="tpu_custom_call" | custom-call | flops 26575110144 | bytes 29884416 | tf_op jit(solution)/shard_map/run_expert/pallas_call | solution.py:701
  472.8 16.6 %moe_in.3 = (bf16[2048,512]{1,0:T(8,128)(2,1)}, bf16[2048,256]{1,0:T(8,128)(2,1)}, f32[2048,1]{1,0:T(8,128)}, bf16[768,2048]{1,0:T(8,128)(2,1)}, bf16[768,2048]{1,0:T(8,128)(2,1)}, /*index=5*/f32[768,128]{1,0:T(8,128)}) custom-call(f32[2,128,2048]{2,1,0:T(8,128)} %get-tuple-element.123.refs_0_, s32[1]{0:T(128)} %bitcast.60.refs_2_.refs_1_, ...), custom_call_target="tpu_custom_call" | custom-call | flops 16106127360 | bytes 25165824 | tf_op jit(solution)/shard_map/moe_in/pallas_call | solution.py:614
  489.4 23.3 %run_expert.3 = (bf16[768,2048]{1,0:T(8,128)(2,1)}, bf16[768,2048]{1,0:T(8,128)(2,1)}, bf16[2,768,704]{2,1,0:T(8,128)(2,1)}, bf16[768,704]{1,0:T(8,128)(2,1)}, f32[768,1]{1,0:T(8,128)}) custom-call(bf16[768,2048]{1,0:T(8,128)(2,1)} %get-tuple-element.132.refs_0_.refs_4_, bf16[768,2048]{1,0:T(8,128)(2,1)} %get-tuple-element.133.refs_1_.refs_4_, ...), custom_call_target="tpu_custom_call" | custom-call | flops 26575110144 | bytes 29884416 | tf_op jit(solution)/shard_map/run_expert/pallas_call | solution.py:701
  518.9 7.5 combine.8
  555.0 11.4 %combine.10 = bf16[2048,2048]{1,0:T(8,128)(2,1)} custom-call(f32[2,128,2048]{2,1,0:T(8,128)} %get-tuple-element.136.refs_0_.refs_1_, bf16[2048,256]{1,0:T(8,128)(2,1)} %get-tuple-element.137.refs_1_, bf16[256,2048]{1,0:T(8,128)(2,1)} %pad.17.refs_8_.refs_7_.refs_2_.refs_6_, s32[8,1,256]{2,1,0:T(1,128)} %bitcast.445, ...), custom_call_target="tpu_custom_call" | custom-call | flops 8858370048 | bytes 11534336 | tf_op jit(solution)/shard_map/combine/pallas_call | solution.py:831
  571.1 11.2 %combine.11 = bf16[2048,2048]{1,0:T(8,128)(2,1)} custom-call(bf16[4,512,2048]{2,1,0:T(8,128)(2,1)} %bitcast.459, bf16[2048,256]{1,0:T(8,128)(2,1)} %get-tuple-element.137.refs_1_, bf16[256,2048]{1,0:T(8,128)(2,1)} %pad.17.refs_8_.refs_7_.refs_2_.refs_6_, s32[8,1,256]{2,1,0:T(1,128)} %bitcast.446, bf16[768,2048]{1,0:T(8,128)(2,1)} %get-tuple-element.138.refs_4_, ...), custom_call_target="tpu_custom_call" | custom-call | flops 8858370048 | bytes 11534336 | tf_op jit(solution)/shard_map/combine/pallas_call | solution.py:831
  582.3 13.5 %collective-permute-done.53.refs_2_ = bf16[2,128,2048]{2,1,0:T(8,128)(2,1)S(1)} collective-permute-done((bf16[2,128,2048]{2,1,0:T(8,128)(2,1)}, bf16[2,128,2048]{2,1,0:T(8,128)(2,1)S(1)}, u32[]{:S(2)}, u32[]{:S(2)}) %collective-permute-start.53) | collective-permute-done | bytes 1048608 | tf_op jit(solution)/shard_map/ppermute | solution.py:30
  606.5 10.3 %core_sum.8 = (f32[4,128,2048]{2,1,0:T(8,128)}, bf16[4,128,2048]{2,1,0:T(8,128)(2,1)}, f32[4,128,2048]{2,1,0:T(8,128)}, bf16[4,128,2048]{2,1,0:T(8,128)(2,1)}) custom-call(f32[2,64,2048]{2,1,0:T(8,128)} %get-tuple-element.144.refs_0_.refs_1_, bf16[4,512,2048]{2,1,0:T(8,128)(2,1)} %bitcast.364, bf16[4,512,2048]{2,1,0:T(8,128)(2,1)} %collective-permute-done.55.refs_2_), custom_call_target="tpu_custom_call" | custom-call | bytes 33554432 | tf_op jit(solution)/shard_map/core_sum/pallas_call | solution.py:62
  639.6 10.3 %weight_sum.5 = bf16[1,256,2048]{2,1,0:T(8,128)(2,1)} custom-call(f32[2,128,2048]{2,1,0:T(8,128)} %last_sum.7.refs_0_.marker_ref, bf16[1,2048,256]{2,1,0:T(8,128)(2,1)} %bitcast.477, bf16[1,2048,256]{2,1,0:T(8,128)(2,1)} %bitcast.478, bf16[1,2048,256]{2,1,0:T(8,128)(2,1)} %bitcast.479, bf16[1,2048,256]{2,1,0:T(8,128)(2,1)} %bitcast.480, ...), custom_call_target="tpu_custom_call" | custom-call | flops 8589934592 | bytes 20971520 | tf_op jit(solution)/shard_map/weight_sum/pallas_call | solution.py:773
  651.5 14.2 %weight_sum.4 = bf16[1,512,2048]{2,1,0:T(8,128)(2,1)} custom-call(f32[2,128,2048]{2,1,0:T(8,128)} %last_sum.7.refs_0_.marker_ref, bf16[1,2048,512]{2,1,0:T(8,128)(2,1)} %bitcast.401, bf16[1,2048,512]{2,1,0:T(8,128)(2,1)} %bitcast.402, bf16[1,2048,512]{2,1,0:T(8,128)(2,1)} %bitcast.473, bf16[1,2048,512]{2,1,0:T(8,128)(2,1)} %bitcast.474, ...), custom_call_target="tpu_custom_call" | custom-call | flops 17179869184 | bytes 25165824 | tf_op jit(solution)/shard_map/weight_sum/pallas_call | solution.py:773
  678.5 7.9 collective-permute-done.58.refs_2_
  705.0 19.6 %collective-permute-done.65.refs_3_ = bf16[1,64,2048]{2,1,0:T(8,128)(2,1)S(1)} collective-permute-done((bf16[1,64,2048]{2,1,0:T(8,128)(2,1)S(1)}, bf16[1,64,2048]{2,1,0:T(8,128)(2,1)S(1)}, u32[]{:S(2)}, u32[]{:S(2)}) %collective-permute-start.65) | collective-permute-done | bytes 262176 | tf_op jit(solution)/shard_map/ppermute | solution.py:30
  724.7 12.4 %collective-permute-done.66.refs_5_ = bf16[1,64,2048]{2,1,0:T(8,128)(2,1)S(1)} collective-permute-done((bf16[1,64,2048]{2,1,0:T(8,128)(2,1)S(1)}, bf16[1,64,2048]{2,1,0:T(8,128)(2,1)S(1)}, u32[]{:S(2)}, u32[]{:S(2)}) %collective-permute-start.66) | collective-permute-done | bytes 262176 | tf_op jit(solution)/shard_map/ppermute | solution.py:30
  793.6 18.2 %attend_back.1.refs_0_.refs_4_.refs_5_ = bf16[2048,768]{1,0:T(8,128)(2,1)} custom-call(bf16[2048,256]{1,0:T(8,128)(2,1)} %copy-done.42, bf16[16,528,128]{2,1,0:T(8,128)(2,1)} %all-to-all-done.3.refs_1_, bf16[128,2048]{1,0:T(8,128)(2,1)} %copy-done.56, bf16[2048,768]{1,0:T(8,128)(2,1)} %get-tuple-element.101.marker_ref.refs_1_.refs_2_.refs_3_.refs_4_.refs_5_, ...), custom_call_target="tpu_custom_call" | custom-call | flops 20132659200 | bytes 6291456 | tf_op jit(solution)/shard_map/attend_back/pallas_call | solution.py:533
  811.8 10.4 %convolution_convert_fusion = bf16[2048,768]{1,0:T(8,128)(2,1)S(1)} fusion(bf16[2048,2048]{1,0:T(8,128)(2,1)} %get-tuple-element.165, bf16[2048,768]{1,0:T(8,128)(2,1)} %attend_back.1.refs_0_.refs_4_.refs_5_), kind=kOutput, calls=%fused_computation.4 | convolution fusion | flops 6444023808 | bytes 14680064 | tf_op jit(solution)/shard_map/dot_general | solution.py:1194
  826.8 8.9 spread.6
  835.8 16.9 %weight_sum.6.refs_0_.refs_3_ = f32[2,704,2048]{2,1,0:T(8,128)} custom-call(bf16[2048,768]{1,0:T(8,128)(2,1)} %attend_back.1.refs_0_.refs_4_.refs_5_, bf16[2,768,704]{2,1,0:T(8,128)(2,1)} %get-tuple-element.166.refs_1_, bf16[2,768,704]{2,1,0:T(8,128)(2,1)} %get-tuple-element.167.refs_2_, bf16[768,2048]{1,0:T(8,128)(2,1)} %get-tuple-element.118.refs_0_.refs_3_, ...), custom_call_target="tpu_custom_call" | custom-call | flops 17716740096 | bytes 22151168 | tf_op jit(solution)/shard_map/weight_sum/pallas_call | solution.py:773
  852.7 9.2 weight_sum.7.refs_2_.marker_ref
  876.8 9.1 spread.7
  918.3 13.3 %collective-permute-done.86 = f32[23,2048]{1,0:T(8,128)} collective-permute-done((f32[23,2048]{1,0:T(8,128)}, f32[23,2048]{1,0:T(8,128)}, u32[]{:S(2)}, u32[]{:S(2)}) %collective-permute-start.86) | collective-permute-done | bytes 188448 | tf_op jit(solution)/shard_map/ppermute | solution.py:34
  952.9 11.6 %collective-permute-done.80.refs_1_ = bf16[2,64,2048]{2,1,0:T(8,128)(2,1)S(1)} collective-permute-done((bf16[2,64,2048]{2,1,0:T(8,128)(2,1)}, bf16[2,64,2048]{2,1,0:T(8,128)(2,1)S(1)}, u32[]{:S(2)}, u32[]{:S(2)}) %collective-permute-start.80) | collective-permute-done | bytes 524320 | tf_op jit(solution)/shard_map/ppermute | solution.py:30
  (617 shorter events, 513.8 us)
Async XLA Ops:
  47.5 39.2 %collective-permute-start.7 = (bf16[2,128,2048]{2,1,0:T(8,128)(2,1)}, bf16[2,128,2048]{2,1,0:T(8,128)(2,1)}, u32[]{:S(2)}, u32[]{:S(2)}) collective-permute-start(bf16[2,128,2048]{2,1,0:T(8,128)(2,1)} %get-tuple-element.99.refs_1_), channel_id=1, source_target_pairs={{0,4},{4,0},{1,5},{5,1},{2,6},{6,2},{3,7},{7,3},{8,12},{12,8},{9,1... | collective-permute-start | bytes 3145736 | tf_op jit(solution)/shard_map/ppermute | solution.py:30
  48.2 38.6 %collective-permute-start.8 = (bf16[2,128,2048]{2,1,0:T(8,128)(2,1)}, bf16[2,128,2048]{2,1,0:T(8,128)(2,1)}, u32[]{:S(2)}, u32[]{:S(2)}) collective-permute-start(bf16[2,128,2048]{2,1,0:T(8,128)(2,1)} %get-tuple-element.100.refs_3_), channel_id=1, source_target_pairs={{0,1},{1,0},{2,3},{3,2},{4,5},{5,4},{6,7},{7,6},{8,9},{9,8},{10,11... | collective-permute-start | bytes 3145736 | tf_op jit(solution)/shard_map/ppermute | solution.py:30
  91.5 70.8 %collective-permute-start.10 = (bf16[2,512,2048]{2,1,0:T(8,128)(2,1)}, bf16[2,512,2048]{2,1,0:T(8,128)(2,1)}, u32[]{:S(2)}, u32[]{:S(2)}) collective-permute-start(bf16[2,512,2048]{2,1,0:T(8,128)(2,1)} %plane.6.marker_ref), channel_id=1, source_target_pairs={{0,2},{2,0},{1,3},{3,1},{4,6},{6,4},{5,7},{7,5},{8,10},{10,8},{9,1... | collective-permute-start | bytes 12582920 | tf_op jit(solution)/shard_map/ppermute | solution.py:30
  97.8 48.7 %collective-permute-start.11 = (bf16[2,512,768]{1,2,0:T(8,128)(2,1)}, bf16[2,512,768]{1,2,0:T(8,128)(2,1)}, u32[]{:S(2)}, u32[]{:S(2)}) collective-permute-start(bf16[2,512,768]{1,2,0:T(8,128)(2,1)} %pad_maximum_fusion.1), channel_id=1, source_target_pairs={{0,8},{8,0},{16,24},{24,16},{1,9},{9,1},{17,25},{25,17},{2,10},{10... | collective-permute-start | bytes 4718600 | tf_op jit(solution)/shard_map/ppermute | solution.py:34
  109.7 85.2 %collective-permute-start.15 = (bf16[128,2048]{1,0:T(8,128)(2,1)}, bf16[128,2048]{1,0:T(8,128)(2,1)}, u32[]{:S(2)}, u32[]{:S(2)}) collective-permute-start(bf16[128,2048]{1,0:T(8,128)(2,1)} %broadcast_select_fusion.10), channel_id=1, source_target_pairs={{0,8},{8,0},{16,24},{24,16},{1,9},{9,1},{17,25},{25,17},{2,10},{10... | collective-permute-start | bytes 1572872 | tf_op jit(solution)/shard_map/ppermute | solution.py:34
  111.0 70.3 %collective-permute-start.16 = (bf16[128,2048]{1,0:T(8,128)(2,1)}, bf16[128,2048]{1,0:T(8,128)(2,1)S(1)}, u32[]{:S(2)}, u32[]{:S(2)}) collective-permute-start(bf16[128,2048]{1,0:T(8,128)(2,1)} %broadcast_select_fusion.10), channel_id=1, source_target_pairs={{0,16},{8,24},{16,0},{24,8},{1,17},{9,25},{17,1},{25,9},{2,18},{10... | collective-permute-start | bytes 1572872 | tf_op jit(solution)/shard_map/ppermute | solution.py:34
  317.7 73.4 %all-to-all-start.1 = ((bf16[16,528,128]{2,1,0:T(8,128)(2,1)}), bf16[16,528,128]{2,1,0:T(8,128)(2,1)S(1)}, u32[]{:S(2)}, u32[]{:S(2)}) async-start(bf16[16,528,128]{2,1,0:T(8,128)(2,1)} %maximum_select_fusion), calls=%async_computation.1 | async-start | bytes 4325376 | tf_op jit(solution)/shard_map/all_to_all | solution.py:256
  326.5 68.2 %collective-permute-start.40 = (bf16[2,512,2048]{2,1,0:T(8,128)(2,1)}, bf16[2,512,2048]{2,1,0:T(8,128)(2,1)}, u32[]{:S(2)}, u32[]{:S(2)}) collective-permute-start(bf16[2,512,2048]{2,1,0:T(8,128)(2,1)} %plane.8), channel_id=1, source_target_pairs={{0,2},{2,0},{1,3},{3,1},{4,6},{6,4},{5,7},{7,5},{8,10},{10,8},{9,1... | collective-permute-start | bytes 12582920 | tf_op jit(solution)/shard_map/ppermute | solution.py:30
  352.5 43.4 %collective-permute-start.39 = (bf16[2,512,2048]{2,1,0:T(8,128)(2,1)}, bf16[2,512,2048]{2,1,0:T(8,128)(2,1)}, u32[]{:S(2)}, u32[]{:S(2)}) collective-permute-start(bf16[2,512,2048]{2,1,0:T(8,128)(2,1)} %plane.7.marker_ref), channel_id=1, source_target_pairs={{0,2},{2,0},{1,3},{3,1},{4,6},{6,4},{5,7},{7,5},{8,10},{10,8},{9,1... | collective-permute-start | bytes 12582920 | tf_op jit(solution)/shard_map/ppermute | solution.py:30
  379.8 56.0 %collective-permute-start.41 = (bf16[2,128,2048]{2,1,0:T(8,128)(2,1)}, bf16[2,128,2048]{2,1,0:T(8,128)(2,1)}, u32[]{:S(2)}, u32[]{:S(2)}) collective-permute-start(bf16[2,128,2048]{2,1,0:T(8,128)(2,1)} %get-tuple-element.114.refs_0_.refs_1_), channel_id=1, source_target_pairs={{0,4},{4,0},{1,5},{5,1},{2,6},{6,2},{3,7},{7,3},{8,12},{12,8},{9,1... | collective-permute-start | bytes 3145736 | tf_op jit(solution)/shard_map/ppermute | solution.py:30
  381.4 54.5 %collective-permute-start.42 = (bf16[2,128,2048]{2,1,0:T(8,128)(2,1)}, bf16[2,128,2048]{2,1,0:T(8,128)(2,1)}, u32[]{:S(2)}, u32[]{:S(2)}) collective-permute-start(bf16[2,128,2048]{2,1,0:T(8,128)(2,1)} %get-tuple-element.117.refs_3_), channel_id=1, source_target_pairs={{0,1},{1,0},{2,3},{3,2},{4,5},{5,4},{6,7},{7,6},{8,9},{9,8},{10,11... | collective-permute-start | bytes 3145736 | tf_op jit(solution)/shard_map/ppermute | solution.py:30
  391.1 57.4 %collective-permute-start.43 = (bf16[2,128,2048]{2,1,0:T(8,128)(2,1)}, bf16[2,128,2048]{2,1,0:T(8,128)(2,1)S(1)}, u32[]{:S(2)}, u32[]{:S(2)}) collective-permute-start(bf16[2,128,2048]{2,1,0:T(8,128)(2,1)} %get-tuple-element.115.refs_1_), channel_id=1, source_target_pairs={{0,4},{4,0},{1,5},{5,1},{2,6},{6,2},{3,7},{7,3},{8,12},{12,8},{9,1... | collective-permute-start | bytes 3145736 | tf_op jit(solution)/shard_map/ppermute | solution.py:30
  394.6 53.9 %collective-permute-start.44 = (bf16[2,128,2048]{2,1,0:T(8,128)(2,1)S(1)}, bf16[2,128,2048]{2,1,0:T(8,128)(2,1)S(1)}, u32[]{:S(2)}, u32[]{:S(2)}) collective-permute-start(bf16[2,128,2048]{2,1,0:T(8,128)(2,1)S(1)} %copy-done.51), channel_id=1, source_target_pairs={{0,1},{1,0},{2,3},{3,2},{4,5},{5,4},{6,7},{7,6},{8,9},{9,8},{10,11... | collective-permute-start | bytes 3145736 | tf_op jit(solution)/shard_map/ppermute | solution.py:30
  469.9 42.7 %collective-permute-start.46 = (bf16[2,128,2048]{2,1,0:T(8,128)(2,1)}, bf16[2,128,2048]{2,1,0:T(8,128)(2,1)S(1)}, u32[]{:S(2)}, u32[]{:S(2)}) collective-permute-start(bf16[2,128,2048]{2,1,0:T(8,128)(2,1)} %get-tuple-element.124), channel_id=1, source_target_pairs={{0,4},{4,0},{1,5},{5,1},{2,6},{6,2},{3,7},{7,3},{8,12},{12,8},{9,1... | collective-permute-start | bytes 3145736 | tf_op jit(solution)/shard_map/ppermute | solution.py:30
  472.0 40.7 %collective-permute-start.47 = (bf16[2,128,2048]{2,1,0:T(8,128)(2,1)}, bf16[2,128,2048]{2,1,0:T(8,128)(2,1)S(1)}, u32[]{:S(2)}, u32[]{:S(2)}) collective-permute-start(bf16[2,128,2048]{2,1,0:T(8,128)(2,1)} %get-tuple-element.126), channel_id=1, source_target_pairs={{0,1},{1,0},{2,3},{3,2},{4,5},{5,4},{6,7},{7,6},{8,9},{9,8},{10,11... | collective-permute-start | bytes 3145736 | tf_op jit(solution)/shard_map/ppermute | solution.py:30
  566.5 40.0 %collective-permute-start.55 = (bf16[4,512,2048]{2,1,0:T(8,128)(2,1)}, bf16[4,512,2048]{2,1,0:T(8,128)(2,1)}, u32[]{:S(2)}, u32[]{:S(2)}) collective-permute-start(bf16[4,512,2048]{2,1,0:T(8,128)(2,1)} %bitcast.458), channel_id=1, source_target_pairs={{0,2},{2,0},{1,3},{3,1},{4,6},{6,4},{5,7},{7,5},{8,10},{10,8},{9,1... | collective-permute-start | bytes 25165832 | tf_op jit(solution)/shard_map/ppermute | solution.py:30
  606.5 94.2 %collective-permute-start.60 = (bf16[128,2048]{1,0:T(8,128)(2,1)}, bf16[128,2048]{1,0:T(8,128)(2,1)}, u32[]{:S(2)}, u32[]{:S(2)}) collective-permute-start(bf16[128,2048]{1,0:T(8,128)(2,1)} %fusion.28), channel_id=1, source_target_pairs={{0,8},{8,0},{16,24},{24,16},{1,9},{9,1},{17,25},{25,17},{2,10},{10... | collective-permute-start | bytes 1572872 | tf_op jit(solution)/shard_map/ppermute | solution.py:34
  626.0 47.3 %all-to-all-start.2 = ((f32[32,2,128]{2,1,0:T(2,128)}), f32[32,2,128]{2,1,0:T(2,128)S(1)}, u32[]{:S(2)}, u32[]{:S(2)}) async-start(f32[32,2,128]{2,1,0:T(2,128)} %reshape.408), calls=%async_computation.2 | async-start | bytes 65536 | tf_op jit(solution)/shard_map/all_to_all | solution.py:256
  633.0 67.6 %collective-permute-start.62 = (bf16[128,2048]{1,0:T(8,128)(2,1)}, bf16[128,2048]{1,0:T(8,128)(2,1)}, u32[]{:S(2)}, u32[]{:S(2)}) collective-permute-start(bf16[128,2048]{1,0:T(8,128)(2,1)} %get-tuple-element.252), channel_id=1, source_target_pairs={{0,24},{8,16},{16,8},{24,0},{1,25},{9,17},{17,9},{25,1},{2,26},{10... | collective-permute-start | bytes 1572872 | tf_op jit(solution)/shard_map/ppermute | solution.py:34
  636.7 64.0 %collective-permute-start.61 = (bf16[128,2048]{1,0:T(8,128)(2,1)}, bf16[128,2048]{1,0:T(8,128)(2,1)}, u32[]{:S(2)}, u32[]{:S(2)}) collective-permute-start(bf16[128,2048]{1,0:T(8,128)(2,1)} %get-tuple-element.251), channel_id=1, source_target_pairs={{0,16},{8,24},{16,0},{24,8},{1,17},{9,25},{17,1},{25,9},{2,18},{10... | collective-permute-start | bytes 1572872 | tf_op jit(solution)/shard_map/ppermute | solution.py:34
  636.7 49.8 %collective-permute-start.58 = (bf16[4,128,2048]{2,1,0:T(8,128)(2,1)}, bf16[4,128,2048]{2,1,0:T(8,128)(2,1)}, u32[]{:S(2)}, u32[]{:S(2)}) collective-permute-start(bf16[4,128,2048]{2,1,0:T(8,128)(2,1)} %get-tuple-element.149), channel_id=1, source_target_pairs={{0,4},{4,0},{1,5},{5,1},{2,6},{6,2},{3,7},{7,3},{8,12},{12,8},{9,1... | collective-permute-start | bytes 6291464 | tf_op jit(solution)/shard_map/ppermute | solution.py:30
  638.2 48.3 %collective-permute-start.59 = (bf16[4,128,2048]{2,1,0:T(8,128)(2,1)}, bf16[4,128,2048]{2,1,0:T(8,128)(2,1)}, u32[]{:S(2)}, u32[]{:S(2)}) collective-permute-start(bf16[4,128,2048]{2,1,0:T(8,128)(2,1)} %get-tuple-element.151), channel_id=1, source_target_pairs={{0,1},{1,0},{2,3},{3,2},{4,5},{5,4},{6,7},{7,6},{8,9},{9,8},{10,11... | collective-permute-start | bytes 6291464 | tf_op jit(solution)/shard_map/ppermute | solution.py:30
  673.3 100.6 %all-to-all-start.3 = ((bf16[16,528,128]{2,1,0:T(8,128)(2,1)}), bf16[16,528,128]{2,1,0:T(8,128)(2,1)}, u32[]{:S(2)}, u32[]{:S(2)}) async-start(bf16[16,528,128]{2,1,0:T(8,128)(2,1)} %maximum_bitcast_fusion), calls=%async_computation.3 | async-start | bytes 4325376 | tf_op jit(solution)/shard_map/all_to_all | solution.py:256
  695.8 41.3 %collective-permute-start.63 = (bf16[4,64,2048]{2,1,0:T(8,128)(2,1)}, bf16[4,64,2048]{2,1,0:T(8,128)(2,1)S(1)}, u32[]{:S(2)}, u32[]{:S(2)}) collective-permute-start(bf16[4,64,2048]{2,1,0:T(8,128)(2,1)} %get-tuple-element.157), channel_id=1, source_target_pairs={{0,1},{1,0},{2,3},{3,2},{4,5},{5,4},{6,7},{7,6},{8,9},{9,8},{10,11... | collective-permute-start | bytes 3145736 | tf_op jit(solution)/shard_map/ppermute | solution.py:30
  697.2 40.0 %collective-permute-start.64 = (bf16[4,64,2048]{2,1,0:T(8,128)(2,1)}, bf16[4,64,2048]{2,1,0:T(8,128)(2,1)S(1)}, u32[]{:S(2)}, u32[]{:S(2)}) collective-permute-start(bf16[4,64,2048]{2,1,0:T(8,128)(2,1)} %get-tuple-element.159), channel_id=1, source_target_pairs={{0,4},{4,0},{1,5},{5,1},{2,6},{6,2},{3,7},{7,3},{8,12},{12,8},{9,1... | collective-permute-start | bytes 3145736 | tf_op jit(solution)/shard_map/ppermute | solution.py:30
  769.2 56.8 %collective-permute-start.71 = (bf16[128,2048]{1,0:T(8,128)(2,1)}, bf16[128,2048]{1,0:T(8,128)(2,1)}, u32[]{:S(2)}, u32[]{:S(2)}) collective-permute-start(bf16[128,2048]{1,0:T(8,128)(2,1)} %get-tuple-element.243), channel_id=1, source_target_pairs={{0,16},{8,24},{16,0},{24,8},{1,17},{9,25},{17,1},{25,9},{2,18},{10... | collective-permute-start | bytes 1572872 | tf_op jit(solution)/shard_map/ppermute | solution.py:34
  770.3 94.9 %collective-permute-start.72 = (bf16[128,2048]{1,0:T(8,128)(2,1)}, bf16[128,2048]{1,0:T(8,128)(2,1)}, u32[]{:S(2)}, u32[]{:S(2)}) collective-permute-start(bf16[128,2048]{1,0:T(8,128)(2,1)} %get-tuple-element.242), channel_id=1, source_target_pairs={{0,24},{8,16},{16,8},{24,0},{1,25},{9,17},{17,9},{25,1},{2,26},{10... | collective-permute-start | bytes 1572872 | tf_op jit(solution)/shard_map/ppermute | solution.py:34
  825.1 48.9 %collective-permute-start.73 = (bf16[2,512,768]{2,1,0:T(8,128)(2,1)}, bf16[2,512,768]{2,1,0:T(8,128)(2,1)}, u32[]{:S(2)}, u32[]{:S(2)}) collective-permute-start(bf16[2,512,768]{2,1,0:T(8,128)(2,1)} %dynamic-slice_bitcast_fusion.refs_1_), channel_id=1, source_target_pairs={{0,8},{8,0},{16,24},{24,16},{1,9},{9,1},{17,25},{25,17},{2,10},{10... | collective-permute-start | bytes 4718600 | tf_op jit(solution)/shard_map/ppermute | solution.py:34
  835.8 66.4 %collective-permute-start.77 = (bf16[2,512,2048]{2,1,0:T(8,128)(2,1)}, bf16[2,512,2048]{2,1,0:T(8,128)(2,1)}, u32[]{:S(2)}, u32[]{:S(2)}) collective-permute-start(bf16[2,512,2048]{2,1,0:T(8,128)(2,1)} %bitcast.462), channel_id=1, source_target_pairs={{0,2},{2,0},{1,3},{3,1},{4,6},{6,4},{5,7},{7,5},{8,10},{10,8},{9,1... | collective-permute-start | bytes 12582920 | tf_op jit(solution)/shard_map/ppermute | solution.py:30
  889.6 43.2 %collective-permute-start.74 = (bf16[512,768]{1,0:T(8,128)(2,1)}, bf16[512,768]{1,0:T(8,128)(2,1)}, u32[]{:S(2)}, u32[]{:S(2)}) collective-permute-start(bf16[512,768]{1,0:T(8,128)(2,1)} %fusion.25.refs_4_), channel_id=1, source_target_pairs={{0,16},{8,24},{16,0},{24,8},{1,17},{9,25},{17,1},{25,9},{2,18},{10... | collective-permute-start | bytes 2359304 | tf_op jit(solution)/shard_map/ppermute | solution.py:34
  908.5 37.0 %collective-permute-start.78 = (bf16[2,128,2048]{2,1,0:T(8,128)(2,1)}, bf16[2,128,2048]{2,1,0:T(8,128)(2,1)}, u32[]{:S(2)}, u32[]{:S(2)}) collective-permute-start(bf16[2,128,2048]{2,1,0:T(8,128)(2,1)} %get-tuple-element.173), channel_id=1, source_target_pairs={{0,4},{4,0},{1,5},{5,1},{2,6},{6,2},{3,7},{7,3},{8,12},{12,8},{9,1... | collective-permute-start | bytes 3145736 | tf_op jit(solution)/shard_map/ppermute | solution.py:30
  937.2 37.7 %all-to-all-start.4 = ((bf16[4,128,768]{1,2,0:T(8,128)(2,1)}), bf16[4,128,768]{1,2,0:T(8,128)(2,1)S(1)}, u32[]{:S(2)}, u32[]{:S(2)}) async-start(bf16[4,128,768]{1,2,0:T(8,128)(2,1)} %copy.187), calls=%async_computation.4 | async-start | bytes 1572864 | tf_op jit(solution)/shard_map/all_to_all | solution.py:256
  (171 other events, 2162.3 us)

commit v5 on v4

--- a/solution.py
+++ b/solution.py
@@ -1124,7 +1124,6 @@
     moe_steps = scatter_core(moe_keep, moe_send, (far_steps[0],))
     far_total = scatter_last(far_steps, (moe_steps[0],))
     far_cross = [cross(far_total[k].astype(BF16), 2 + k) for k in range(2)]
-    moe_steps = scatter_pair(moe_steps, (far_total,))
 
     tiles = range(2)
     shared_time = (far_total,)
@@ -1152,7 +1151,7 @@
     )[0]
     grad_normed = near_total[0] + near_cross.astype(F32)
     grad_normed = grad_normed + far_cross[0].astype(F32) + far_cross[1].astype(F32)
-    grad_normed = hold(grad_normed, tick(grad_sgu) + tick(grad_sdn) + tick(moe_steps[0]))
+    grad_normed = hold(grad_normed, tick(grad_sgu) + tick(grad_sdn) + tick(moe_steps[1]))
     shared_grad = jnp.concatenate(
         [grad_sgu[:own], grad_sgu[held : held + own], grad_sdn[:own]], 0
     )
@@ -1185,10 +1184,11 @@
     grad_middle = cotangent.astype(F32) + norm_back(middle, scale_moe, gain_moe, grad_normed)
     grad_attn = grad_middle.astype(BF16)
 
-    _, plane, _ = slot_pair(grad_attn[None], (moe_steps[1], moe_steps[3]))
-    moe_parts = scatter_last(moe_steps, (grad_attn,))
+    pairs, plane, _ = slot_pair(grad_attn[None], ())
+    moe_steps = scatter_pair(moe_steps, (pairs[0],))
+    plane_grad, grad_attended = project((), order_one, plane((moe_steps[0],)), w_out)
+    moe_parts = scatter_last(moe_steps, (grad_attended,))
     moe_cross = [cross(moe_parts[k].astype(BF16), k) for k in range(1, LINE)]
-    plane_grad, grad_attended = project((), order_one, plane((moe_parts,)), w_out)
 
     def weight_grad(left, right):
         return lax.dot_general(left, right, (((0,), (0,)), ((), ())), preferred_element_type=F32)
@@ -1201,7 +1201,7 @@
 
     grad_out = weight_grad(plane_grad, attended).astype(BF16)
     grad_projected = attend_back(
-        (grad_out, shared_grad_sent, moe_cross[0]),
+        (grad_out, shared_grad_sent, moe_parts),
         projected, grad_attended, seg_q, seg_k, valid_k, cosine, sine,
     )
     grad_qkv = weight_grad(own_rows, grad_projected).astype(BF16)
@@ -1219,10 +1219,10 @@
     grad_qkv = grad_qkv.reshape(3, weight_rows, local_cols)
     w_qkv_t = w_qkv.T
     send, sum_send = spread(
-        (qkv_marks[0], out_marks[1], moe_cross[1]),
+        (qkv_marks[0], out_marks[1]),
         order_two, grad_projected, w_qkv_t, 1, rows_attn[1],
     )
-    keep, sum_keep = spread((send, moe_cross[2], grad_egu, qkv_marks[3]), order_two, grad_projected, w_qkv_t, 0, rows_attn[0])
+    keep, sum_keep = spread((send, grad_egu, qkv_marks[3]), order_two, grad_projected, w_qkv_t, 0, rows_attn[0])
     gain_sum = (sum_send + sum_keep)[0] / gain_attn
     bias_sum = jnp.sum(grad_projected.astype(F32), axis=0).reshape(3, cols)
     grad_bias = lax.dynamic_update_slice_in_dim(jnp.zeros((3, model), F32), bias_sum, here, 1)

time: 1000 us -> 995 us (level)
    ppermute x60, waiting for transfers between devices: 161 us -> 143 us  [swap(): return lax.ppermute(value, axis, SWAP)]
    unnamed x227 -> x219, local copies, waits for them, and re-layouts: 34.6 us -> 31.2 us
  transfers between devices with their start and end apart: 94 -> 94, of which waited for: 40 -> 42; matrix products, arithmetic and copies ran while one was open for 13% -> 13% of each run, Pallas kernels for 36% -> 35%
where the time goes in v5:
time: 995 us; the launch traced here: 987 us
  Pallas kernels  411 us (41%)
  waiting for transfers between devices  276 us (28%)
  starting transfers between devices  124 us (12%)
  local copies, waits for them, and re-layouts  86.7 us (9%)
  other arithmetic  61.8 us (6%)
  matrix products  14.7 us (1%)
  between operations  12.5 us (1%)
    ppermute x60, waiting for transfers between devices, swap(): return lax.ppermute(value, axis, SWAP)  143 us
    pallas_call x27, Pallas kernels, stage(): pl.pallas_call(without(len(after), kernel), grid=(count, parts), in_specs...  131 us
    ppermute x25, waiting for transfers between devices, cross(): return lax.ppermute(value, 'z', [(k, k ^ offset) for k in range(LINE)])  122 us
    pallas_call x6, Pallas kernels, combine(): pl.pallas_call(without(len(after), functools.partial(combine_kernel, capa...  52.4 us
    pallas_call x4, Pallas kernels, weight_sum(): pl.pallas_call(without(len(after), sum_kernel), grid=(parts, steps, steps...  50.7 us
    ppermute x60, starting transfers between devices, swap(): return lax.ppermute(value, axis, SWAP)  50.1 us
    pallas_call x2, Pallas kernels, run_expert(): pl.pallas_call(without(len(after), functools.partial(expert_kernel, steps...  46.5 us
    ppermute x25, starting transfers between devices, cross(): return lax.ppermute(value, 'z', [(k, k ^ offset) for k in range(LINE)])  38.9 us
  transfers between devices with their start and end apart: 94, of which 42 were waited for; matrix products, arithmetic and copies ran while one was open for 13% of the time, Pallas kernels for 35%

profile of v5, /device:TPU:0, one launch (start us, length us, event | category | flops | bytes accessed | tf_op | source)
XLA Modules:
  0.0 986.7 jit_solution(11153839793812800559)
XLA Ops:
  15.7 8.0 collective-permute-done.1
  53.2 32.4 %collective-permute-done = bf16[512,768]{0,1:T(8,128)(2,1)S(1)} collective-permute-done((bf16[512,768]{0,1:T(8,128)(2,1)S(1)}, bf16[512,768]{0,1:T(8,128)(2,1)S(1)}, u32[]{:S(2)}, u32[]{:S(2)}) %collective-permute-start) | collective-permute-done | bytes 786464 | tf_op jit(solution)/shard_map/ppermute | solution.py:34
  112.9 33.5 %collective-permute-done.11 = bf16[2,512,768]{1,2,0:T(8,128)(2,1)} collective-permute-done((bf16[2,512,768]{1,2,0:T(8,128)(2,1)}, bf16[2,512,768]{1,2,0:T(8,128)(2,1)}, u32[]{:S(2)}, u32[]{:S(2)}) %collective-permute-start.11) | collective-permute-done | bytes 1572896 | tf_op jit(solution)/shard_map/ppermute | solution.py:34
  162.2 14.3 %project.2 = (bf16[2048,2048]{1,0:T(8,128)(2,1)}, bf16[2048,768]{1,0:T(8,128)(2,1)}) custom-call(s32[9]{0:T(128)} %concatenate.61.refs_0_, bf16[1024,2048]{1,0:T(8,128)(2,1)} %bitcast.367, bf16[1024,2048]{1,0:T(8,128)(2,1)} %bitcast.26.refs_2_.refs_5_, bf16[2048,768]{1,0:T(8,128)(2,1)} %copy.160.refs_3_, f32[1,768]{1,0:T(1,128)} %bitcast.455, ...), custom_call_target="tpu_custom_call" | custom-call | flops 19327352832 | bytes 23068672 | tf_op jit(solution)/shard_map/project/pallas_call | solution.py:337
  181.9 11.1 %attend.1.refs_2_ = bf16[1024,256]{1,0:T(8,128)(2,1)} custom-call(bf16[128,2048]{1,0:T(8,128)(2,1)} %copy-done.53, bf16[2048,768]{1,0:T(8,128)(2,1)} %get-tuple-element.101.marker_ref.refs_1_.refs_2_.refs_3_.refs_4_.refs_5_, bf16[2048,768]{1,0:T(8,128)(2,1)} %get-tuple-element.101.marker_ref.refs_1_.refs_2_.refs_3_.refs_4_.refs_5_, ...), custom_call_target="tpu_custom_call" | custom-call | flops 12079595520 | bytes 4194304 | tf_op jit(solution)/shard_map/attend/pallas_call | solution.py:465
  220.7 10.3 %collective-permute-done.20.refs_1_ = bf16[1,128,2048]{2,1,0:T(8,128)(2,1)S(1)} collective-permute-done((bf16[1,128,2048]{2,1,0:T(8,128)(2,1)}, bf16[1,128,2048]{2,1,0:T(8,128)(2,1)S(1)}, u32[]{:S(2)}, u32[]{:S(2)}) %collective-permute-start.20) | collective-permute-done | bytes 524320 | tf_op jit(solution)/shard_map/ppermute | solution.py:30
  275.2 10.1 %collective-permute-done.30 = bf16[128,2048]{1,0:T(8,128)(2,1)S(1)} collective-permute-done((bf16[128,2048]{1,0:T(8,128)(2,1)S(1)}, bf16[128,2048]{1,0:T(8,128)(2,1)S(1)}, u32[]{:S(2)}, u32[]{:S(2)}) %collective-permute-start.30) | collective-permute-done | bytes 524320 | tf_op jit(solution)/shard_map/ppermute | solution.py:34
  287.9 16.2 %collective-permute-done.24.refs_0_ = bf16[128,2048]{1,0:T(8,128)(2,1)S(1)} collective-permute-done((bf16[128,2048]{1,0:T(8,128)(2,1)S(1)}, bf16[128,2048]{1,0:T(8,128)(2,1)S(1)}, u32[]{:S(2)}, u32[]{:S(2)}) %collective-permute-start.24) | collective-permute-done | bytes 524320 | tf_op jit(solution)/shard_map/ppermute | solution.py:34
  326.7 20.9 %collective-permute-done.33.refs_1_ = bf16[2,128,2048]{2,1,0:T(8,128)(2,1)} collective-permute-done((bf16[2,128,2048]{2,1,0:T(8,128)(2,1)}, bf16[2,128,2048]{2,1,0:T(8,128)(2,1)}, u32[]{:S(2)}, u32[]{:S(2)}) %collective-permute-start.33) | collective-permute-done | bytes 1048608 | tf_op jit(solution)/shard_map/ppermute | solution.py:30
  357.9 12.4 %collective-permute-done.35.refs_1_ = bf16[2,64,2048]{2,1,0:T(8,128)(2,1)S(1)} collective-permute-done((bf16[2,64,2048]{2,1,0:T(8,128)(2,1)S(1)}, bf16[2,64,2048]{2,1,0:T(8,128)(2,1)S(1)}, u32[]{:S(2)}, u32[]{:S(2)}) %collective-permute-start.35) | collective-permute-done | bytes 524320 | tf_op jit(solution)/shard_map/ppermute | solution.py:30
  395.7 16.6 %moe_in.2 = (bf16[2048,512]{1,0:T(8,128)(2,1)}, bf16[2048,256]{1,0:T(8,128)(2,1)}, f32[2048,1]{1,0:T(8,128)}, bf16[768,2048]{1,0:T(8,128)(2,1)}, bf16[768,2048]{1,0:T(8,128)(2,1)}, /*index=5*/f32[768,128]{1,0:T(8,128)}) custom-call(bf16[2,128,2048]{2,1,0:T(8,128)(2,1)} %get-tuple-element.114.refs_0_.refs_1_, ...), custom_call_target="tpu_custom_call" | custom-call | flops 16106127360 | bytes 25165824 | tf_op jit(solution)/shard_map/moe_in/pallas_call | solution.py:614
  412.3 23.3 %run_expert.2 = (bf16[768,2048]{1,0:T(8,128)(2,1)}, bf16[768,2048]{1,0:T(8,128)(2,1)}, bf16[2,768,704]{2,1,0:T(8,128)(2,1)}, bf16[768,704]{1,0:T(8,128)(2,1)}, f32[768,1]{1,0:T(8,128)}) custom-call(bf16[768,2048]{1,0:T(8,128)(2,1)} %get-tuple-element.118.refs_0_.refs_3_, bf16[768,2048]{1,0:T(8,128)(2,1)} %get-tuple-element.119.refs_1_.refs_3_, ...), custom_call_target="tpu_custom_call" | custom-call | flops 26575110144 | bytes 29884416 | tf_op jit(solution)/shard_map/run_expert/pallas_call | solution.py:701
  472.6 16.6 %moe_in.3 = (bf16[2048,512]{1,0:T(8,128)(2,1)}, bf16[2048,256]{1,0:T(8,128)(2,1)}, f32[2048,1]{1,0:T(8,128)}, bf16[768,2048]{1,0:T(8,128)(2,1)}, bf16[768,2048]{1,0:T(8,128)(2,1)}, /*index=5*/f32[768,128]{1,0:T(8,128)}) custom-call(f32[2,128,2048]{2,1,0:T(8,128)} %get-tuple-element.123.refs_0_, s32[1]{0:T(128)} %bitcast.60.refs_2_.refs_1_, ...), custom_call_target="tpu_custom_call" | custom-call | flops 16106127360 | bytes 25165824 | tf_op jit(solution)/shard_map/moe_in/pallas_call | solution.py:614
  489.2 23.2 %run_expert.3 = (bf16[768,2048]{1,0:T(8,128)(2,1)}, bf16[768,2048]{1,0:T(8,128)(2,1)}, bf16[2,768,704]{2,1,0:T(8,128)(2,1)}, bf16[768,704]{1,0:T(8,128)(2,1)}, f32[768,1]{1,0:T(8,128)}) custom-call(bf16[768,2048]{1,0:T(8,128)(2,1)} %get-tuple-element.132.refs_0_.refs_4_, bf16[768,2048]{1,0:T(8,128)(2,1)} %get-tuple-element.133.refs_1_.refs_4_, ...), custom_call_target="tpu_custom_call" | custom-call | flops 26575110144 | bytes 29884416 | tf_op jit(solution)/shard_map/run_expert/pallas_call | solution.py:701
  518.7 7.5 combine.8
  554.8 11.4 %combine.10 = bf16[2048,2048]{1,0:T(8,128)(2,1)} custom-call(f32[2,128,2048]{2,1,0:T(8,128)} %get-tuple-element.136.refs_0_.refs_1_, bf16[2048,256]{1,0:T(8,128)(2,1)} %get-tuple-element.137.refs_1_, bf16[256,2048]{1,0:T(8,128)(2,1)} %pad.17.refs_8_.refs_7_.refs_2_.refs_6_, s32[8,1,256]{2,1,0:T(1,128)} %bitcast.445, ...), custom_call_target="tpu_custom_call" | custom-call | flops 8858370048 | bytes 11534336 | tf_op jit(solution)/shard_map/combine/pallas_call | solution.py:831
  570.9 11.2 %combine.11 = bf16[2048,2048]{1,0:T(8,128)(2,1)} custom-call(bf16[4,512,2048]{2,1,0:T(8,128)(2,1)} %bitcast.459, bf16[2048,256]{1,0:T(8,128)(2,1)} %get-tuple-element.137.refs_1_, bf16[256,2048]{1,0:T(8,128)(2,1)} %pad.17.refs_8_.refs_7_.refs_2_.refs_6_, s32[8,1,256]{2,1,0:T(1,128)} %bitcast.446, bf16[768,2048]{1,0:T(8,128)(2,1)} %get-tuple-element.138.refs_4_, ...), custom_call_target="tpu_custom_call" | custom-call | flops 8858370048 | bytes 11534336 | tf_op jit(solution)/shard_map/combine/pallas_call | solution.py:831
  582.1 13.4 %collective-permute-done.53.refs_2_ = bf16[2,128,2048]{2,1,0:T(8,128)(2,1)S(1)} collective-permute-done((bf16[2,128,2048]{2,1,0:T(8,128)(2,1)}, bf16[2,128,2048]{2,1,0:T(8,128)(2,1)S(1)}, u32[]{:S(2)}, u32[]{:S(2)}) %collective-permute-start.53) | collective-permute-done | bytes 1048608 | tf_op jit(solution)/shard_map/ppermute | solution.py:30
  606.2 10.2 %core_sum.8 = (f32[4,128,2048]{2,1,0:T(8,128)}, bf16[4,128,2048]{2,1,0:T(8,128)(2,1)}, f32[4,128,2048]{2,1,0:T(8,128)}, bf16[4,128,2048]{2,1,0:T(8,128)(2,1)}) custom-call(f32[2,64,2048]{2,1,0:T(8,128)} %get-tuple-element.144.refs_0_.refs_1_, bf16[4,512,2048]{2,1,0:T(8,128)(2,1)} %bitcast.365, bf16[4,512,2048]{2,1,0:T(8,128)(2,1)} %collective-permute-done.55.refs_2_), custom_call_target="tpu_custom_call" | custom-call | bytes 33554432 | tf_op jit(solution)/shard_map/core_sum/pallas_call | solution.py:62
  639.4 10.3 %weight_sum.5 = bf16[1,256,2048]{2,1,0:T(8,128)(2,1)} custom-call(f32[2,128,2048]{2,1,0:T(8,128)} %last_sum.7.refs_0_.marker_ref, bf16[1,2048,256]{2,1,0:T(8,128)(2,1)} %bitcast.477, bf16[1,2048,256]{2,1,0:T(8,128)(2,1)} %bitcast.478, bf16[1,2048,256]{2,1,0:T(8,128)(2,1)} %bitcast.479, bf16[1,2048,256]{2,1,0:T(8,128)(2,1)} %bitcast.480, ...), custom_call_target="tpu_custom_call" | custom-call | flops 8589934592 | bytes 20971520 | tf_op jit(solution)/shard_map/weight_sum/pallas_call | solution.py:773
  651.2 14.1 %weight_sum.4 = bf16[1,512,2048]{2,1,0:T(8,128)(2,1)} custom-call(f32[2,128,2048]{2,1,0:T(8,128)} %last_sum.7.refs_0_.marker_ref, bf16[1,2048,512]{2,1,0:T(8,128)(2,1)} %bitcast.401, bf16[1,2048,512]{2,1,0:T(8,128)(2,1)} %bitcast.402, bf16[1,2048,512]{2,1,0:T(8,128)(2,1)} %bitcast.473, bf16[1,2048,512]{2,1,0:T(8,128)(2,1)} %bitcast.474, ...), custom_call_target="tpu_custom_call" | custom-call | flops 17179869184 | bytes 25165824 | tf_op jit(solution)/shard_map/weight_sum/pallas_call | solution.py:773
  678.3 7.9 collective-permute-done.58.marker_ref.refs_2_
  692.4 7.8 collective-permute-start.62
  776.5 18.2 %attend_back.1.refs_0_.refs_3_.refs_4_ = bf16[2048,768]{1,0:T(8,128)(2,1)} custom-call(bf16[2048,256]{1,0:T(8,128)(2,1)} %copy-done.39, bf16[16,528,128]{2,1,0:T(8,128)(2,1)} %all-to-all-done.3.refs_1_, f32[4,128,2048]{2,1,0:T(8,128)} %last_sum.8.refs_2_, bf16[2048,768]{1,0:T(8,128)(2,1)} %get-tuple-element.101.marker_ref.refs_1_.refs_2_.refs_3_.refs_4_.refs_5_, ...), custom_call_target="tpu_custom_call" | custom-call | flops 20132659200 | bytes 6291456 | tf_op jit(solution)/shard_map/attend_back/pallas_call | solution.py:533
  794.7 10.4 %convolution_convert_fusion = bf16[2048,768]{1,0:T(8,128)(2,1)S(1)} fusion(bf16[2048,2048]{1,0:T(8,128)(2,1)} %get-tuple-element.165, bf16[2048,768]{1,0:T(8,128)(2,1)} %attend_back.1.refs_0_.refs_3_.refs_4_), kind=kOutput, calls=%fused_computation.4 | convolution fusion | flops 6444023808 | bytes 14680064 | tf_op jit(solution)/shard_map/dot_general | solution.py:1194
  810.3 8.9 collective-permute-done.75.refs_2_
  819.9 8.9 spread.6
  828.9 16.9 %weight_sum.6.refs_0_.refs_2_ = f32[2,704,2048]{2,1,0:T(8,128)} custom-call(bf16[2048,768]{1,0:T(8,128)(2,1)} %attend_back.1.refs_0_.refs_3_.refs_4_, bf16[2,768,704]{2,1,0:T(8,128)(2,1)} %get-tuple-element.166.refs_1_, bf16[2,768,704]{2,1,0:T(8,128)(2,1)} %get-tuple-element.167.refs_2_, bf16[768,2048]{1,0:T(8,128)(2,1)} %get-tuple-element.118.refs_0_.refs_3_, ...), custom_call_target="tpu_custom_call" | custom-call | flops 17716740096 | bytes 22151168 | tf_op jit(solution)/shard_map/weight_sum/pallas_call | solution.py:773
  845.8 9.4 weight_sum.7.refs_2_.marker_ref
  872.0 9.1 spread.7
  913.3 13.5 %collective-permute-done.86 = f32[23,2048]{1,0:T(8,128)} collective-permute-done((f32[23,2048]{1,0:T(8,128)}, f32[23,2048]{1,0:T(8,128)}, u32[]{:S(2)}, u32[]{:S(2)}) %collective-permute-start.86) | collective-permute-done | bytes 188448 | tf_op jit(solution)/shard_map/ppermute | solution.py:34
  948.3 11.3 %collective-permute-done.80.refs_1_ = bf16[2,64,2048]{2,1,0:T(8,128)(2,1)S(1)} collective-permute-done((bf16[2,64,2048]{2,1,0:T(8,128)(2,1)}, bf16[2,64,2048]{2,1,0:T(8,128)(2,1)S(1)}, u32[]{:S(2)}, u32[]{:S(2)}) %collective-permute-start.80) | collective-permute-done | bytes 524320 | tf_op jit(solution)/shard_map/ppermute | solution.py:30
  (609 shorter events, 524.7 us)
Async XLA Ops:
  47.5 39.2 %collective-permute-start.7 = (bf16[2,128,2048]{2,1,0:T(8,128)(2,1)}, bf16[2,128,2048]{2,1,0:T(8,128)(2,1)}, u32[]{:S(2)}, u32[]{:S(2)}) collective-permute-start(bf16[2,128,2048]{2,1,0:T(8,128)(2,1)} %get-tuple-element.99.refs_1_), channel_id=1, source_target_pairs={{0,4},{4,0},{1,5},{5,1},{2,6},{6,2},{3,7},{7,3},{8,12},{12,8},{9,1... | collective-permute-start | bytes 3145736 | tf_op jit(solution)/shard_map/ppermute | solution.py:30
  48.2 38.6 %collective-permute-start.8 = (bf16[2,128,2048]{2,1,0:T(8,128)(2,1)}, bf16[2,128,2048]{2,1,0:T(8,128)(2,1)}, u32[]{:S(2)}, u32[]{:S(2)}) collective-permute-start(bf16[2,128,2048]{2,1,0:T(8,128)(2,1)} %get-tuple-element.100.refs_3_), channel_id=1, source_target_pairs={{0,1},{1,0},{2,3},{3,2},{4,5},{5,4},{6,7},{7,6},{8,9},{9,8},{10,11... | collective-permute-start | bytes 3145736 | tf_op jit(solution)/shard_map/ppermute | solution.py:30
  91.5 70.7 %collective-permute-start.10 = (bf16[2,512,2048]{2,1,0:T(8,128)(2,1)}, bf16[2,512,2048]{2,1,0:T(8,128)(2,1)}, u32[]{:S(2)}, u32[]{:S(2)}) collective-permute-start(bf16[2,512,2048]{2,1,0:T(8,128)(2,1)} %plane.6.marker_ref), channel_id=1, source_target_pairs={{0,2},{2,0},{1,3},{3,1},{4,6},{6,4},{5,7},{7,5},{8,10},{10,8},{9,1... | collective-permute-start | bytes 12582920 | tf_op jit(solution)/shard_map/ppermute | solution.py:30
  97.7 48.7 %collective-permute-start.11 = (bf16[2,512,768]{1,2,0:T(8,128)(2,1)}, bf16[2,512,768]{1,2,0:T(8,128)(2,1)}, u32[]{:S(2)}, u32[]{:S(2)}) collective-permute-start(bf16[2,512,768]{1,2,0:T(8,128)(2,1)} %pad_maximum_fusion.1), channel_id=1, source_target_pairs={{0,8},{8,0},{16,24},{24,16},{1,9},{9,1},{17,25},{25,17},{2,10},{10... | collective-permute-start | bytes 4718600 | tf_op jit(solution)/shard_map/ppermute | solution.py:34
  109.5 85.2 %collective-permute-start.15 = (bf16[128,2048]{1,0:T(8,128)(2,1)}, bf16[128,2048]{1,0:T(8,128)(2,1)}, u32[]{:S(2)}, u32[]{:S(2)}) collective-permute-start(bf16[128,2048]{1,0:T(8,128)(2,1)} %broadcast_select_fusion.10), channel_id=1, source_target_pairs={{0,8},{8,0},{16,24},{24,16},{1,9},{9,1},{17,25},{25,17},{2,10},{10... | collective-permute-start | bytes 1572872 | tf_op jit(solution)/shard_map/ppermute | solution.py:34
  110.8 70.3 %collective-permute-start.16 = (bf16[128,2048]{1,0:T(8,128)(2,1)}, bf16[128,2048]{1,0:T(8,128)(2,1)S(1)}, u32[]{:S(2)}, u32[]{:S(2)}) collective-permute-start(bf16[128,2048]{1,0:T(8,128)(2,1)} %broadcast_select_fusion.10), channel_id=1, source_target_pairs={{0,16},{8,24},{16,0},{24,8},{1,17},{9,25},{17,1},{25,9},{2,18},{10... | collective-permute-start | bytes 1572872 | tf_op jit(solution)/shard_map/ppermute | solution.py:34
  317.6 73.4 %all-to-all-start.1 = ((bf16[16,528,128]{2,1,0:T(8,128)(2,1)}), bf16[16,528,128]{2,1,0:T(8,128)(2,1)S(1)}, u32[]{:S(2)}, u32[]{:S(2)}) async-start(bf16[16,528,128]{2,1,0:T(8,128)(2,1)} %maximum_select_fusion), calls=%async_computation.1 | async-start | bytes 4325376 | tf_op jit(solution)/shard_map/all_to_all | solution.py:256
  326.3 68.2 %collective-permute-start.40 = (bf16[2,512,2048]{2,1,0:T(8,128)(2,1)}, bf16[2,512,2048]{2,1,0:T(8,128)(2,1)}, u32[]{:S(2)}, u32[]{:S(2)}) collective-permute-start(bf16[2,512,2048]{2,1,0:T(8,128)(2,1)} %plane.8), channel_id=1, source_target_pairs={{0,2},{2,0},{1,3},{3,1},{4,6},{6,4},{5,7},{7,5},{8,10},{10,8},{9,1... | collective-permute-start | bytes 12582920 | tf_op jit(solution)/shard_map/ppermute | solution.py:30
  352.3 43.4 %collective-permute-start.39 = (bf16[2,512,2048]{2,1,0:T(8,128)(2,1)}, bf16[2,512,2048]{2,1,0:T(8,128)(2,1)}, u32[]{:S(2)}, u32[]{:S(2)}) collective-permute-start(bf16[2,512,2048]{2,1,0:T(8,128)(2,1)} %plane.7.marker_ref), channel_id=1, source_target_pairs={{0,2},{2,0},{1,3},{3,1},{4,6},{6,4},{5,7},{7,5},{8,10},{10,8},{9,1... | collective-permute-start | bytes 12582920 | tf_op jit(solution)/shard_map/ppermute | solution.py:30
  379.7 56.0 %collective-permute-start.41 = (bf16[2,128,2048]{2,1,0:T(8,128)(2,1)}, bf16[2,128,2048]{2,1,0:T(8,128)(2,1)}, u32[]{:S(2)}, u32[]{:S(2)}) collective-permute-start(bf16[2,128,2048]{2,1,0:T(8,128)(2,1)} %get-tuple-element.114.refs_0_.refs_1_), channel_id=1, source_target_pairs={{0,4},{4,0},{1,5},{5,1},{2,6},{6,2},{3,7},{7,3},{8,12},{12,8},{9,1... | collective-permute-start | bytes 3145736 | tf_op jit(solution)/shard_map/ppermute | solution.py:30
  381.2 54.5 %collective-permute-start.42 = (bf16[2,128,2048]{2,1,0:T(8,128)(2,1)}, bf16[2,128,2048]{2,1,0:T(8,128)(2,1)}, u32[]{:S(2)}, u32[]{:S(2)}) collective-permute-start(bf16[2,128,2048]{2,1,0:T(8,128)(2,1)} %get-tuple-element.117.refs_3_), channel_id=1, source_target_pairs={{0,1},{1,0},{2,3},{3,2},{4,5},{5,4},{6,7},{7,6},{8,9},{9,8},{10,11... | collective-permute-start | bytes 3145736 | tf_op jit(solution)/shard_map/ppermute | solution.py:30
  390.9 57.4 %collective-permute-start.43 = (bf16[2,128,2048]{2,1,0:T(8,128)(2,1)}, bf16[2,128,2048]{2,1,0:T(8,128)(2,1)S(1)}, u32[]{:S(2)}, u32[]{:S(2)}) collective-permute-start(bf16[2,128,2048]{2,1,0:T(8,128)(2,1)} %get-tuple-element.115.refs_1_), channel_id=1, source_target_pairs={{0,4},{4,0},{1,5},{5,1},{2,6},{6,2},{3,7},{7,3},{8,12},{12,8},{9,1... | collective-permute-start | bytes 3145736 | tf_op jit(solution)/shard_map/ppermute | solution.py:30
  394.5 53.8 %collective-permute-start.44 = (bf16[2,128,2048]{2,1,0:T(8,128)(2,1)S(1)}, bf16[2,128,2048]{2,1,0:T(8,128)(2,1)S(1)}, u32[]{:S(2)}, u32[]{:S(2)}) collective-permute-start(bf16[2,128,2048]{2,1,0:T(8,128)(2,1)S(1)} %copy-done.48), channel_id=1, source_target_pairs={{0,1},{1,0},{2,3},{3,2},{4,5},{5,4},{6,7},{7,6},{8,9},{9,8},{10,11... | collective-permute-start | bytes 3145736 | tf_op jit(solution)/shard_map/ppermute | solution.py:30
  469.7 42.8 %collective-permute-start.46 = (bf16[2,128,2048]{2,1,0:T(8,128)(2,1)}, bf16[2,128,2048]{2,1,0:T(8,128)(2,1)S(1)}, u32[]{:S(2)}, u32[]{:S(2)}) collective-permute-start(bf16[2,128,2048]{2,1,0:T(8,128)(2,1)} %get-tuple-element.124), channel_id=1, source_target_pairs={{0,4},{4,0},{1,5},{5,1},{2,6},{6,2},{3,7},{7,3},{8,12},{12,8},{9,1... | collective-permute-start | bytes 3145736 | tf_op jit(solution)/shard_map/ppermute | solution.py:30
  471.8 40.7 %collective-permute-start.47 = (bf16[2,128,2048]{2,1,0:T(8,128)(2,1)}, bf16[2,128,2048]{2,1,0:T(8,128)(2,1)S(1)}, u32[]{:S(2)}, u32[]{:S(2)}) collective-permute-start(bf16[2,128,2048]{2,1,0:T(8,128)(2,1)} %get-tuple-element.126), channel_id=1, source_target_pairs={{0,1},{1,0},{2,3},{3,2},{4,5},{5,4},{6,7},{7,6},{8,9},{9,8},{10,11... | collective-permute-start | bytes 3145736 | tf_op jit(solution)/shard_map/ppermute | solution.py:30
  566.3 40.0 %collective-permute-start.55 = (bf16[4,512,2048]{2,1,0:T(8,128)(2,1)}, bf16[4,512,2048]{2,1,0:T(8,128)(2,1)}, u32[]{:S(2)}, u32[]{:S(2)}) collective-permute-start(bf16[4,512,2048]{2,1,0:T(8,128)(2,1)} %bitcast.458), channel_id=1, source_target_pairs={{0,2},{2,0},{1,3},{3,1},{4,6},{6,4},{5,7},{7,5},{8,10},{10,8},{9,1... | collective-permute-start | bytes 25165832 | tf_op jit(solution)/shard_map/ppermute | solution.py:30
  606.2 81.9 %collective-permute-start.59 = (bf16[128,2048]{1,0:T(8,128)(2,1)}, bf16[128,2048]{1,0:T(8,128)(2,1)}, u32[]{:S(2)}, u32[]{:S(2)}) collective-permute-start(bf16[128,2048]{1,0:T(8,128)(2,1)} %fusion.28), channel_id=1, source_target_pairs={{0,8},{8,0},{16,24},{24,16},{1,9},{9,1},{17,25},{25,17},{2,10},{10... | collective-permute-start | bytes 1572872 | tf_op jit(solution)/shard_map/ppermute | solution.py:34
  625.6 47.3 %all-to-all-start.2 = ((f32[32,2,128]{2,1,0:T(2,128)}), f32[32,2,128]{2,1,0:T(2,128)S(1)}, u32[]{:S(2)}, u32[]{:S(2)}) async-start(f32[32,2,128]{2,1,0:T(2,128)} %reshape.408), calls=%async_computation.2 | async-start | bytes 65536 | tf_op jit(solution)/shard_map/all_to_all | solution.py:256
  632.8 55.4 %collective-permute-start.61 = (bf16[128,2048]{1,0:T(8,128)(2,1)}, bf16[128,2048]{1,0:T(8,128)(2,1)}, u32[]{:S(2)}, u32[]{:S(2)}) collective-permute-start(bf16[128,2048]{1,0:T(8,128)(2,1)} %get-tuple-element.252), channel_id=1, source_target_pairs={{0,24},{8,16},{16,8},{24,0},{1,25},{9,17},{17,9},{25,1},{2,26},{10... | collective-permute-start | bytes 1572872 | tf_op jit(solution)/shard_map/ppermute | solution.py:34
  636.4 51.8 %collective-permute-start.60 = (bf16[128,2048]{1,0:T(8,128)(2,1)}, bf16[128,2048]{1,0:T(8,128)(2,1)}, u32[]{:S(2)}, u32[]{:S(2)}) collective-permute-start(bf16[128,2048]{1,0:T(8,128)(2,1)} %get-tuple-element.251), channel_id=1, source_target_pairs={{0,16},{8,24},{16,0},{24,8},{1,17},{9,25},{17,1},{25,9},{2,18},{10... | collective-permute-start | bytes 1572872 | tf_op jit(solution)/shard_map/ppermute | solution.py:34
  636.4 49.8 %collective-permute-start.58 = (bf16[4,128,2048]{2,1,0:T(8,128)(2,1)}, bf16[4,128,2048]{2,1,0:T(8,128)(2,1)}, u32[]{:S(2)}, u32[]{:S(2)}) collective-permute-start(bf16[4,128,2048]{2,1,0:T(8,128)(2,1)} %get-tuple-element.149), channel_id=1, source_target_pairs={{0,4},{4,0},{1,5},{5,1},{2,6},{6,2},{3,7},{7,3},{8,12},{12,8},{9,1... | collective-permute-start | bytes 6291464 | tf_op jit(solution)/shard_map/ppermute | solution.py:30
  637.9 75.8 %collective-permute-start.64 = (bf16[4,128,2048]{2,1,0:T(8,128)(2,1)}, bf16[4,128,2048]{2,1,0:T(8,128)(2,1)}, u32[]{:S(2)}, u32[]{:S(2)}) collective-permute-start(bf16[4,128,2048]{2,1,0:T(8,128)(2,1)} %get-tuple-element.156), channel_id=1, source_target_pairs={{0,1},{1,0},{2,3},{3,2},{4,5},{5,4},{6,7},{7,6},{8,9},{9,8},{10,11... | collective-permute-start | bytes 6291464 | tf_op jit(solution)/shard_map/ppermute | solution.py:30
  673.0 62.3 %all-to-all-start.3 = ((bf16[16,528,128]{2,1,0:T(8,128)(2,1)}), bf16[16,528,128]{2,1,0:T(8,128)(2,1)}, u32[]{:S(2)}, u32[]{:S(2)}) async-start(bf16[16,528,128]{2,1,0:T(8,128)(2,1)} %maximum_bitcast_fusion), calls=%async_computation.3 | async-start | bytes 4325376 | tf_op jit(solution)/shard_map/all_to_all | solution.py:256
  769.1 91.2 %collective-permute-start.70 = (bf16[128,2048]{1,0:T(8,128)(2,1)}, bf16[128,2048]{1,0:T(8,128)(2,1)}, u32[]{:S(2)}, u32[]{:S(2)}) collective-permute-start(bf16[128,2048]{1,0:T(8,128)(2,1)} %get-tuple-element.244), channel_id=1, source_target_pairs={{0,8},{8,0},{16,24},{24,16},{1,9},{9,1},{17,25},{25,17},{2,10},{10... | collective-permute-start | bytes 1572872 | tf_op jit(solution)/shard_map/ppermute | solution.py:34
  772.4 91.4 %collective-permute-start.71 = (bf16[128,2048]{1,0:T(8,128)(2,1)}, bf16[128,2048]{1,0:T(8,128)(2,1)}, u32[]{:S(2)}, u32[]{:S(2)}) collective-permute-start(bf16[128,2048]{1,0:T(8,128)(2,1)} %get-tuple-element.243), channel_id=1, source_target_pairs={{0,16},{8,24},{16,0},{24,8},{1,17},{9,25},{17,1},{25,9},{2,18},{10... | collective-permute-start | bytes 1572872 | tf_op jit(solution)/shard_map/ppermute | solution.py:34
  775.9 88.0 %collective-permute-start.72 = (bf16[128,2048]{1,0:T(8,128)(2,1)}, bf16[128,2048]{1,0:T(8,128)(2,1)}, u32[]{:S(2)}, u32[]{:S(2)}) collective-permute-start(bf16[128,2048]{1,0:T(8,128)(2,1)} %get-tuple-element.242), channel_id=1, source_target_pairs={{0,24},{8,16},{16,8},{24,0},{1,25},{9,17},{17,9},{25,1},{2,26},{10... | collective-permute-start | bytes 1572872 | tf_op jit(solution)/shard_map/ppermute | solution.py:34
  775.9 43.2 %collective-permute-start.75 = (bf16[2,512,256]{2,1,0:T(8,128)(2,1)S(1)}, bf16[2,512,256]{2,1,0:T(8,128)(2,1)S(1)}, u32[]{:S(2)}, u32[]{:S(2)}) collective-permute-start(bf16[2,512,256]{2,1,0:T(8,128)(2,1)S(1)} %dynamic-slice_bitcast_fusion.1), channel_id=1, source_target_pairs={{0,8},{8,0},{16,24},{24,16},{1,9},{9,1},{17,25},{25,17},{2,10},{10... | collective-permute-start | bytes 1572872 | tf_op jit(solution)/shard_map/ppermute | solution.py:34
  806.5 62.7 %collective-permute-start.73 = (bf16[2,512,768]{2,1,0:T(8,128)(2,1)}, bf16[2,512,768]{2,1,0:T(8,128)(2,1)}, u32[]{:S(2)}, u32[]{:S(2)}) collective-permute-start(bf16[2,512,768]{2,1,0:T(8,128)(2,1)} %dynamic-slice_bitcast_fusion.refs_1_), channel_id=1, source_target_pairs={{0,8},{8,0},{16,24},{24,16},{1,9},{9,1},{17,25},{25,17},{2,10},{10... | collective-permute-start | bytes 4718600 | tf_op jit(solution)/shard_map/ppermute | solution.py:34
  828.9 69.4 %collective-permute-start.77 = (bf16[2,512,2048]{2,1,0:T(8,128)(2,1)}, bf16[2,512,2048]{2,1,0:T(8,128)(2,1)}, u32[]{:S(2)}, u32[]{:S(2)}) collective-permute-start(bf16[2,512,2048]{2,1,0:T(8,128)(2,1)} %bitcast.462), channel_id=1, source_target_pairs={{0,2},{2,0},{1,3},{3,1},{4,6},{6,4},{5,7},{7,5},{8,10},{10,8},{9,1... | collective-permute-start | bytes 12582920 | tf_op jit(solution)/shard_map/ppermute | solution.py:30
  884.7 43.2 %collective-permute-start.74 = (bf16[512,768]{1,0:T(8,128)(2,1)}, bf16[512,768]{1,0:T(8,128)(2,1)}, u32[]{:S(2)}, u32[]{:S(2)}) collective-permute-start(bf16[512,768]{1,0:T(8,128)(2,1)} %fusion.25.refs_3_), channel_id=1, source_target_pairs={{0,16},{8,24},{16,0},{24,8},{1,17},{9,25},{17,1},{25,9},{2,18},{10... | collective-permute-start | bytes 2359304 | tf_op jit(solution)/shard_map/ppermute | solution.py:34
  904.6 36.1 %collective-permute-start.78 = (bf16[2,128,2048]{2,1,0:T(8,128)(2,1)}, bf16[2,128,2048]{2,1,0:T(8,128)(2,1)}, u32[]{:S(2)}, u32[]{:S(2)}) collective-permute-start(bf16[2,128,2048]{2,1,0:T(8,128)(2,1)} %get-tuple-element.173), channel_id=1, source_target_pairs={{0,4},{4,0},{1,5},{5,1},{2,6},{6,2},{3,7},{7,3},{8,12},{12,8},{9,1... | collective-permute-start | bytes 3145736 | tf_op jit(solution)/shard_map/ppermute | solution.py:30
  932.4 37.5 %all-to-all-start.4 = ((bf16[4,128,768]{1,2,0:T(8,128)(2,1)}), bf16[4,128,768]{1,2,0:T(8,128)(2,1)S(1)}, u32[]{:S(2)}, u32[]{:S(2)}) async-start(bf16[4,128,768]{1,2,0:T(8,128)(2,1)} %copy.187), calls=%async_computation.4 | async-start | bytes 1572864 | tf_op jit(solution)/shard_map/all_to_all | solution.py:256
  (167 other events, 2047.8 us)
